TPU v7x, 256 devices: a whole 4x4x8 slice. The times are simulated.
256 devices in a mesh: dp: 32 (over y, x, core), cent: 8 (over z).
Axes of the slice: x: 4, y: 4, z: 8, core: 2. Of those that a mesh axis runs over, the one named last changes fastest.
Arguments:
- emb: bfloat16 [524288, 768], P(('dp', 'cent')), may hold values from -37 to 37
- centroids: bfloat16 [8192, 768], P('cent'), may hold values from -4.1 to 4.1
- block_parent: int32 [4096], P(('dp', 'cent')), may hold values from 0 to 127, as said below
- block_live: int32 [4096], P(('dp', 'cent')), may hold values from 32 to 128
Outputs:
- new_centroids: float32 [8192, 768], P('cent')
Inputs may be any that keep to these rules, and one draw needn't show every extreme that they name: Among the 16 blocks of one device (one index of dp+cent), at most 4 have parents owned by one index of cent (block_parent // 16), and exactly 4 for some index on every device.
All inputs are finite; a program needn't handle non-finite values.
Results may differ from a plain program's by a relative error of at most 0.0029.
Values may be sent and summed in bfloat16 or wider, within the bound.
No kernel may reach another device: no remote copies, remote signals or barrier semaphores. Data moves between devices by JAX's collectives and lax.ppermute only.
A program may use at most 128 MiB of HBM per device.

v0:
```python
import math

import jax
import jax.numpy as jnp
from jax import lax
from jax.sharding import PartitionSpec as P

D = 768
KIDS = 64
ROWBLK = 128
ITERS = 2
PRIOR = 64


softness = 0.8


def block_terms(members, children, live_rows):
    products = jnp.einsum("grd,gkd->grk", members, children, preferred_element_type=jnp.float32)
    children32 = children.astype(jnp.float32)
    squares = jnp.sum(children32 * children32, axis=-1)
    logits = (2.0 * products - squares[:, None, :]) / (softness * math.sqrt(D))
    row_top = jnp.max(logits, axis=-1, keepdims=True)
    scaled = jnp.exp(logits - row_top)
    weights = scaled / jnp.sum(scaled, axis=-1, keepdims=True)
    inside = jnp.arange(members.shape[1], dtype=jnp.int32)[None, :] < live_rows[:, None]
    weights = jnp.where(inside[:, :, None], weights, 0.0).astype(jnp.bfloat16)
    child_sum = jnp.einsum("grk,grd->gkd", weights, members, preferred_element_type=jnp.float32)
    child_mass = jnp.sum(weights.astype(jnp.float32), axis=1)
    return (child_sum, child_mass)


def gather_sums(members, parents, live_rows, kid_table):
    group_size = 4
    group_count = members.shape[0] // group_size
    start_sums = (
        jnp.zeros((kid_table.shape[0], kid_table.shape[1], members.shape[2]), jnp.float32),
        jnp.zeros((kid_table.shape[0], kid_table.shape[1]), jnp.float32),
    )

    def accumulate(group_no, carried):
        total_sum, total_mass = carried
        first_row = group_no * group_size
        block_rows = lax.dynamic_slice_in_dim(members, first_row, group_size, 0)
        block_par = lax.dynamic_slice_in_dim(parents, first_row, group_size, 0)
        block_len = lax.dynamic_slice_in_dim(live_rows, first_row, group_size, 0)
        child_sum, child_mass = block_terms(block_rows, kid_table[block_par], block_len)
        return (total_sum.at[block_par].add(child_sum), total_mass.at[block_par].add(child_mass))

    return lax.fori_loop(0, group_count, accumulate, start_sums)


def shards(emb, centroids, block_parent, block_live):
    feat_width = emb.shape[1]
    members = emb.reshape(-1, ROWBLK, feat_width)
    block_count = members.shape[0]
    owner_count = lax.axis_size("cent")
    local_rows = centroids.shape[0]
    local_parents = local_rows // KIDS
    capacity = block_count // 4
    owner_of = block_parent // local_parents
    is_target = (owner_of[:, None] == jnp.arange(owner_count, dtype=jnp.int32)[None, :]).astype(
        jnp.int32
    )
    send_rank = jnp.sum((jnp.cumsum(is_target, axis=0) - 1) * is_target, axis=1)
    send_slot = owner_of * capacity + send_rank
    outgoing = (
        jnp.zeros((owner_count * capacity, ROWBLK, feat_width), jnp.bfloat16)
        .at[send_slot]
        .set(members)
    )
    tag_values = jnp.stack([block_parent - owner_of * local_parents, block_live], axis=1).astype(
        jnp.bfloat16
    )
    send_tags = jnp.zeros((owner_count * capacity, 2), jnp.bfloat16).at[send_slot].set(tag_values)
    arrived, arrived_tags = (
        lax.all_to_all(outgoing, "cent", split_axis=0, concat_axis=0, tiled=True),
        lax.all_to_all(send_tags, "cent", split_axis=0, concat_axis=0, tiled=True),
    )
    arrived_parent = arrived_tags[:, 0].astype(jnp.int32)
    arrived_live = arrived_tags[:, 1].astype(jnp.int32)
    current = centroids
    updated = centroids.astype(jnp.float32)
    for sweep_no in range(ITERS):
        kid_table = current.reshape(local_parents, KIDS, feat_width)
        total_sum, total_mass = gather_sums(arrived, arrived_parent, arrived_live, kid_table)
        total_sum = total_sum.reshape(local_rows, feat_width)
        total_mass = total_mass.reshape(local_rows)
        previous = current.astype(jnp.float32)
        is_final = sweep_no + 1 == ITERS
        summed, massed = lax.psum((total_sum, total_mass), "dp")
        updated = (summed + PRIOR * previous) / (massed[:, None] + PRIOR)
        if not is_final:
            current = updated.astype(jnp.bfloat16)
    return updated


def solution(mesh):
    placed = (P(("dp", "cent"), None), P("cent", None), P(("dp", "cent")), P(("dp", "cent")))
    return jax.shard_map(
        shards, mesh=mesh, in_specs=placed, out_specs=P("cent", None), check_vma=False
    )
```

profile of v0, /device:TPU:1, one launch (start us, length us, event | category | flops | bytes accessed | tf_op | source)
XLA Modules:
  0.0 554.5 jit_solution(13734627131006202869)
XLA Ops:
  8.9 0.7 copy.9
  9.6 9.0 %all-to-all-start = ((bf16[8,4,2]{1,2,0:T(2,128)(2,1)}), bf16[8,4,2]{1,2,0:T(2,128)(2,1)S(1)}, u32[]{:S(2)}, u32[]{:S(2)}) async-start(bf16[8,4,2]{1,2,0:T(2,128)(2,1)} %copy.9), calls=%async_computation | async-start | bytes 8192 | tf_op jit(solution)/shard_map/all_to_all | solution.py:78
  18.7 3.4 broadcast_in_dim.118
  22.0 9.1 %scatter_fusion.4 = bf16[32,128,768]{2,1,0:T(8,128)(2,1)} fusion(bf16[32,128,768]{2,1,0:T(8,128)(2,1)} %broadcast_in_dim.118, s32[16]{0:T(128)S(1)} %compare_select_fusion.2, bf16[16,128,768]{2,1,0:T(8,128)(2,1)S(1)} %bitcast.36), kind=kCustom, calls=%fused_computation.7 | custom fusion | bytes 9437248 | tf_op jit(solution)/shard_map/scatter | solution.py:70
  31.2 6.7 %all-to-all-start.1 = ((bf16[32,128,768]{2,1,0:T(8,128)(2,1)}), bf16[32,128,768]{2,1,0:T(8,128)(2,1)}, u32[]{:S(2)}, u32[]{:S(2)}) async-start(bf16[32,128,768]{2,1,0:T(8,128)(2,1)} %scatter_fusion.4), calls=%async_computation.1 | async-start | bytes 12582912 | tf_op jit(solution)/shard_map/all_to_all | solution.py:77
  38.0 141.9 %all-to-all-done.1 = bf16[32,128,768]{2,1,0:T(8,128)(2,1)} async-done(((bf16[32,128,768]{2,1,0:T(8,128)(2,1)}), bf16[32,128,768]{2,1,0:T(8,128)(2,1)}, u32[]{:S(2)}, u32[]{:S(2)}) %all-to-all-start.1) | async-done | bytes 6291488 | tf_op jit(solution)/shard_map/all_to_all | solution.py:77
  180.0 2.0 broadcast.138.clone
  182.0 60.7 %while.30 = (s32[]{:T(128)}, f32[16,64,768]{2,1,0:T(8,128)}, f32[16,64]{1,0:T(8,128)S(1)}, s32[32]{0:T(128)S(1)}, s32[32]{0:T(128)S(1)}, /*index=5*/bf16[32,128,...) while((s32[]{:T(128)}, f32[16,64,768]{2,1,0:T(8,128)}, ...), condition=%wide.region_11.12_spmd, body=%wide.region_4.11_spmd.sunk | while | flops 101778768 | bytes 6700347 | solution.py:50
  182.8 1.6 fusion.49
  184.6 1.4 fusion.50
  186.0 2.9 scatter_fusion
  190.4 1.6 fusion.49
  192.2 1.4 fusion.50
  193.6 2.9 scatter_fusion
  198.0 1.6 fusion.49
  199.8 1.4 fusion.50
  201.2 2.9 scatter_fusion
  205.6 1.6 fusion.49
  207.4 1.4 fusion.50
  208.8 2.9 scatter_fusion
  213.2 1.6 fusion.49
  215.0 1.4 fusion.50
  216.4 2.9 scatter_fusion
  220.8 1.6 fusion.49
  222.6 1.4 fusion.50
  224.0 2.8 scatter_fusion
  228.3 1.6 fusion.49
  230.1 1.4 fusion.50
  231.5 2.9 scatter_fusion
  235.9 1.6 fusion.49
  237.7 1.4 fusion.50
  239.1 2.9 scatter_fusion
  242.8 62.8 %psum.29 = f32[1024]{0:T(1024)S(1)} all-reduce(f32[1024]{0:T(1024)S(1)} %reshape.83), channel_id=1, replica_groups=mesh['dp'=32,'cent'=8] {'dp'}, use_global_device_ids=true, to_apply=%region_13.14 | all-reduce | flops 1024 | bytes 8192 | tf_op jit(solution)/shard_map/psum | solution.py:91
  305.6 53.6 %all-reduce.3.cloned.1.call-done = f32[1024,768]{1,0:T(8,128)} async-done(((f32[1024,768]{1,0:T(8,128)}), f32[1024,768]{1,0:T(8,128)}) %all-reduce.3.cloned.1.call-update) | async-done | bytes 3145744 | tf_op jit(solution)/shard_map/psum | solution.py:91
  359.2 2.4 divide_convert_fusion
  361.6 2.0 broadcast.138
  363.6 60.7 %while.31 = (s32[]{:T(128)}, f32[16,64,768]{2,1,0:T(8,128)}, f32[16,64]{1,0:T(8,128)S(1)}, s32[32]{0:T(128)S(1)}, s32[32]{0:T(128)S(1)}, /*index=5*/bf16[32,128,...) while((s32[]{:T(128)}, f32[16,64,768]{2,1,0:T(8,128)}, ...), condition=%wide.region_21.22_spmd, body=%wide.region_14.21_spmd.sunk | while | flops 101778768 | bytes 6700347 | solution.py:50
  364.4 1.6 fusion.55
  366.3 1.4 fusion.56
  367.7 2.9 scatter_fusion.2
  372.0 1.6 fusion.55
  373.9 1.4 fusion.56
  375.3 2.9 scatter_fusion.2
  379.6 1.6 fusion.55
  381.5 1.4 fusion.56
  382.9 2.9 scatter_fusion.2
  387.2 1.6 fusion.55
  389.1 1.4 fusion.56
  390.5 2.9 scatter_fusion.2
  394.8 1.6 fusion.55
  396.7 1.4 fusion.56
  398.1 2.9 scatter_fusion.2
  402.4 1.6 fusion.55
  404.3 1.4 fusion.56
  405.7 2.8 scatter_fusion.2
  410.0 1.6 fusion.55
  411.8 1.4 fusion.56
  413.2 2.9 scatter_fusion.2
  417.6 1.6 fusion.55
  419.4 1.4 fusion.56
  420.8 2.9 scatter_fusion.2
  424.4 62.6 %psum.31 = f32[1024]{0:T(1024)S(1)} all-reduce(f32[1024]{0:T(1024)S(1)} %reshape.86), channel_id=1, replica_groups=mesh['dp'=32,'cent'=8] {'dp'}, use_global_device_ids=true, to_apply=%region_23.24 | all-reduce | flops 1024 | bytes 8192 | tf_op jit(solution)/shard_map/psum | solution.py:91
  487.1 56.6 %all-reduce.5.cloned.1.call-done = f32[1024,768]{1,0:T(8,128)} async-done(((f32[1024,768]{1,0:T(8,128)}), f32[1024,768]{1,0:T(8,128)}) %all-reduce.5.cloned.1.call-update) | async-done | bytes 3145744 | tf_op jit(solution)/shard_map/psum | solution.py:91
  543.6 4.0 add_divide_fusion
  (155 shorter events, 29.7 us)
Async XLA Ops:
  9.6 21.5 %all-to-all-start = ((bf16[8,4,2]{1,2,0:T(2,128)(2,1)}), bf16[8,4,2]{1,2,0:T(2,128)(2,1)S(1)}, u32[]{:S(2)}, u32[]{:S(2)}) async-start(bf16[8,4,2]{1,2,0:T(2,128)(2,1)} %copy.9), calls=%async_computation | async-start | bytes 8192 | tf_op jit(solution)/shard_map/all_to_all | solution.py:78
  18.7 3.4 copy-start.1
  31.2 148.8 %all-to-all-start.1 = ((bf16[32,128,768]{2,1,0:T(8,128)(2,1)}), bf16[32,128,768]{2,1,0:T(8,128)(2,1)}, u32[]{:S(2)}, u32[]{:S(2)}) async-start(bf16[32,128,768]{2,1,0:T(8,128)(2,1)} %scatter_fusion.4), calls=%async_computation.1 | async-start | bytes 12582912 | tf_op jit(solution)/shard_map/all_to_all | solution.py:77
  37.9 144.1 %copy-start = (bf16[1024,768]{1,0:T(8,128)(2,1)S(1)}, bf16[1024,768]{1,0:T(8,128)(2,1)}, u32[]{:S(2)}) copy-start(bf16[1024,768]{1,0:T(8,128)(2,1)} %param.9) | copy-start | bytes 4718596
  37.9 321.4 %all-reduce.3.cloned.1.call-start = ((), (), s32[]{:S(2)}) async-start(), calls=%async_computation.2 | async-start | bytes 6291456 | tf_op jit(solution)/shard_map/psum | solution.py:91
  242.7 300.9 %all-reduce.5.cloned.1.call-start = ((), (), s32[]{:S(2)}) async-start(), calls=%async_computation.3 | async-start | bytes 6291456 | tf_op jit(solution)/shard_map/psum | solution.py:91
Sparse Core Ops, SparseCore 0:
  242.8 116.3 all-reduce.2
  424.5 119.0 all-reduce.4
where the time goes:
time: 557 us; the launch traced here: 554 us
  waiting for transfers between devices  252 us (45%)
  blocking collectives  125 us (22%)
  other arithmetic  71 us (13%)
  matrix products  47.3 us (8%)
  local copies, waits for them, and re-layouts  28.5 us (5%)
  starting transfers between devices  15.8 us (3%)
  between operations  13.5 us (2%)
    all_to_all x1, waiting for transfers between devices, shards(): lax.all_to_all(outgoing, 'cent', split_axis=0, concat_axis=0, tiled=True)  142 us
    psum x2, blocking collectives, shards(): summed, massed = lax.psum((total_sum, total_mass), 'dp')  125 us
    psum x2, waiting for transfers between devices, shards(): summed, massed = lax.psum((total_sum, total_mass), 'dp')  110 us
    scatter-add x16, other arithmetic, accumulate(): total_sum.at[block_par].add(child_sum)  46.3 us
    sub x16, matrix products, block_terms(): scaled = jnp.exp(logits - row_top)  25 us
    dot_general x16, matrix products, block_terms(): jnp.einsum('grk,grd->gkd', weights, members, preferred_element_type=jnp.f...  22.3 us
  transfers between devices with their start and end apart: 4, of which 3 were waited for; matrix products, arithmetic and copies ran while one was open for 2% of the time, Pallas kernels for 0%

commit v1 on v0

v1 whole, which is shorter than its diff:
```python
import functools
import math

import jax
import jax.numpy as jnp
from jax import lax
from jax.experimental import pallas as pl
from jax.experimental.pallas import tpu as pltpu
from jax.sharding import Mesh, PartitionSpec as P

D = 768
KIDS = 64
ROWBLK = 128
ITERS = 2
PRIOR = 64
OWNERS = 8
CAP = 4
SLOTS = OWNERS * CAP
PAR_DEV = 16
ROWS_DEV = PAR_DEV * KIDS
WIDE = D + 128
CHIPS = 16
PIECE = ROWS_DEV // CHIPS

SOFTNESS = 0.8
LOGIT_SCALE = 1.0 / (SOFTNESS * math.sqrt(D))

GROUPS = (
    (0, 0, 0, 0, 4),
    (0, 1, 0, 0, 4),
    (1, 0, 1, 0, 4),
    (-1, 0, 3, 0, 4),
    (1, 1, 1, 0, 4),
    (-1, 1, 3, 0, 4),
    (2, 0, 2, 0, 2),
    (-2, 0, 2, 2, 2),
    (2, 1, 2, 0, 2),
    (-2, 1, 2, 2, 2),
)
SENT = GROUPS[1:]
EARLY = 6
TAG_ROWS = 16


def slot_of(kind, other, rank):
    return (kind * 2 + other) * CAP + rank


def dispatch_kernel(pos_ref, par_ref, live_ref, emb_ref, *refs):
    outs, stay_ref = refs[: len(SENT)], refs[len(SENT)]
    held, tiles, src_ref, kid_ref, len_ref, count_ref, read_sem, sems, tag_sems = refs[len(SENT) + 1 :]
    read = pltpu.make_async_copy(emb_ref, held, read_sem)
    read.start()
    z, core = pos_ref[0], pos_ref[1]
    for s in range(SLOTS):
        src_ref[s] = 0
        kid_ref[s] = 0
        len_ref[s] = 0
    for o in range(OWNERS):
        count_ref[o] = 0

    def place(b, carry):
        parent = par_ref[b]
        owner = parent // PAR_DEV
        rank = count_ref[owner]
        count_ref[owner] = rank + 1
        kind = lax.rem(owner - z + 8, 4)
        other = jnp.where(owner // 4 == core, 0, 1)
        slot = slot_of(kind, other, rank)
        src_ref[slot] = b
        kid_ref[slot] = parent - owner * PAR_DEV
        len_ref[slot] = live_ref[b]
        return carry

    lax.fori_loop(0, par_ref.shape[0], place, 0)
    for k in range(CAP):
        stay_ref[0, k] = src_ref[k]
        stay_ref[1, k] = kid_ref[k]
        stay_ref[2, k] = len_ref[k]
    row = lax.broadcasted_iota(jnp.int32, (TAG_ROWS, 128), 0)
    lane = lax.broadcasted_iota(jnp.int32, (TAG_ROWS, 128), 1)
    copies = []
    for i, (_, other, kind, first, size) in enumerate(SENT):
        tile = jnp.zeros((TAG_ROWS, 128), jnp.int32)
        for k in range(size):
            s = slot_of(kind, other, first + k)
            tile = jnp.where(row == k, jnp.where(lane == 0, kid_ref[s], len_ref[s]), tile)
        tiles[i] = tile.astype(jnp.float32).astype(jnp.bfloat16)
    for i, (_, _, _, _, size) in enumerate(SENT):
        copy = pltpu.make_async_copy(
            tiles.at[i], outs[i].at[pl.ds(size * ROWBLK, TAG_ROWS), pl.ds(0, 128)], tag_sems.at[i]
        )
        copy.start()
        copies.append(copy)
    read.wait()
    for i, (_, other, kind, first, size) in enumerate(SENT):
        for k in range(size):
            s = slot_of(kind, other, first + k)
            block = src_ref[s]
            copy = pltpu.make_async_copy(
                held.at[block], outs[i].at[pl.ds(k * ROWBLK, ROWBLK)], sems.at[s]
            )
            copy.start()
            copies.append(copy)
    for copy in copies:
        copy.wait()


def dispatch(pos, parents, lives, blocks):
    smem = pl.BlockSpec(memory_space=pltpu.SMEM)
    hbm = pl.BlockSpec(memory_space=pl.ANY)
    shapes = [jax.ShapeDtypeStruct((g[4] * ROWBLK + TAG_ROWS, D), jnp.bfloat16) for g in SENT]
    return pl.pallas_call(
        dispatch_kernel,
        out_shape=shapes + [jax.ShapeDtypeStruct((3, CAP), jnp.int32)],
        in_specs=[smem, smem, smem, hbm],
        out_specs=[hbm] * len(SENT) + [smem],
        scratch_shapes=[
            pltpu.VMEM(blocks.shape, jnp.bfloat16),
            pltpu.VMEM((len(SENT), TAG_ROWS, 128), jnp.bfloat16),
            pltpu.SMEM((SLOTS,), jnp.int32),
            pltpu.SMEM((SLOTS,), jnp.int32),
            pltpu.SMEM((SLOTS,), jnp.int32),
            pltpu.SMEM((OWNERS,), jnp.int32),
            pltpu.SemaphoreType.DMA,
            pltpu.SemaphoreType.DMA((SLOTS,)),
            pltpu.SemaphoreType.DMA((len(SENT),)),
        ],
        compiler_params=pltpu.CompilerParams(vmem_limit_bytes=16 * 1024 * 1024),
        cost_estimate=pl.CostEstimate(
            flops=0, bytes_accessed=12 * 1024 * 1024, transcendentals=0
        ),
    )(pos, parents, lives, blocks)


def sums_kernel(picked, resumed, packed, *refs):
    refs = list(refs)
    stay_ref = blocks_ref = None
    local = picked[0] == GROUPS[0]
    if local:
        stay_ref, blocks_ref = refs[0], refs[1]
        del refs[:2]
    sent = picked[1:] if local else picked
    groups, table_ref = refs[: len(sent)], refs[len(sent)]
    del refs[: len(sent) + 1]
    if resumed:
        acc_in, mass_in = refs[:2]
        del refs[:2]
    if packed:
        out_ref, acc, mass = refs[:3]
        del refs[:3]
    else:
        acc, mass = refs[:2]
        del refs[:2]
    rows, squares, tiles, kid_ref, len_ref, sems, tag_sems, sum_sems = refs
    batches = rows.shape[0]

    tag_copies = []
    for i, (ref, (_, _, _, _, size)) in enumerate(zip(groups, sent)):
        copy = pltpu.make_async_copy(
            ref.at[pl.ds(size * ROWBLK, TAG_ROWS), pl.ds(0, 128)], tiles.at[i], tag_sems.at[i]
        )
        copy.start()
        tag_copies.append(copy)
    if resumed:
        sum_copies = [
            pltpu.make_async_copy(acc_in, acc, sum_sems.at[0]),
            pltpu.make_async_copy(mass_in, mass, sum_sems.at[1]),
        ]
        for copy in sum_copies:
            copy.start()
    at = 0
    if local:
        for k in range(CAP):
            pltpu.make_async_copy(
                blocks_ref.at[stay_ref[0, k]], rows.at[0, pl.ds(k * ROWBLK, ROWBLK)], sems.at[0]
            ).start()
            kid_ref[k] = stay_ref[1, k]
            len_ref[k] = stay_ref[2, k]
        at = CAP
    for ref, (_, _, _, _, size) in zip(groups, sent):
        pltpu.make_async_copy(
            ref.at[pl.ds(0, size * ROWBLK)],
            rows.at[at // CAP, pl.ds(at % CAP * ROWBLK, size * ROWBLK)],
            sems.at[at // CAP],
        ).start()
        at += size

    if not resumed:
        acc[...] = jnp.zeros_like(acc)
        mass[...] = jnp.zeros_like(mass)

    def square(p, carry):
        at_p = pl.ds(pl.multiple_of(p * KIDS, KIDS), KIDS)
        kids = table_ref[at_p, :].astype(jnp.float32)
        total = jnp.sum(kids * kids, axis=1, keepdims=True)
        squares[at_p, :] = jnp.broadcast_to(total * LOGIT_SCALE, (KIDS, 128))
        return carry

    lax.fori_loop(0, PAR_DEV, square, 0)
    at = CAP if local else 0
    for i, (_, _, _, _, size) in enumerate(sent):
        tag_copies[i].wait()
        tile = tiles[i].astype(jnp.float32).astype(jnp.int32)
        for k in range(size):
            kid_ref[at] = tile[k, 0]
            len_ref[at] = tile[k, 1]
            at += 1
    if resumed:
        for copy in sum_copies:
            copy.wait()
    lane = lax.broadcasted_iota(jnp.int32, (KIDS, ROWBLK), 1)

    def batch_step(batch, carry):
        pltpu.make_async_copy(rows.at[batch], rows.at[batch], sems.at[batch]).wait()
        places, found = [], []
        for k in range(CAP):
            at_p = pl.ds(pl.multiple_of(kid_ref[batch * CAP + k] * KIDS, KIDS), KIDS)
            products = lax.dot_general(
                table_ref[at_p, :],
                rows[batch, k * ROWBLK : (k + 1) * ROWBLK],
                (((1,), (1,)), ((), ())),
                preferred_element_type=jnp.float32,
            )
            logits = products * (2.0 * LOGIT_SCALE) - squares[at_p, :]
            scaled = jnp.exp(logits - jnp.max(logits, axis=0, keepdims=True))
            weights = scaled / jnp.sum(scaled, axis=0, keepdims=True)
            weights = jnp.where(lane < len_ref[batch * CAP + k], weights, 0.0)
            places.append(at_p)
            found.append(weights.astype(jnp.bfloat16))
        for k in range(CAP):
            acc[places[k], :] += jnp.dot(
                found[k],
                rows[batch, k * ROWBLK : (k + 1) * ROWBLK],
                preferred_element_type=jnp.float32,
            )
            mass[places[k], :] += found[k].astype(jnp.float32)
        return carry

    lax.fori_loop(0, batches, batch_step, 0)

    def finish(p, carry):
        at_p = pl.ds(pl.multiple_of(p * KIDS, KIDS), KIDS)
        total = jnp.broadcast_to(jnp.sum(mass[at_p, :], axis=1, keepdims=True), (KIDS, 128))
        high = total.astype(jnp.bfloat16)
        low = (total - high.astype(jnp.float32)).astype(jnp.bfloat16)
        out_ref[at_p, :D] = acc[at_p, :].astype(jnp.bfloat16)
        out_ref[at_p, D:] = jnp.where(lane < 64, high, low)
        return carry

    if packed:
        lax.fori_loop(0, PAR_DEV, finish, 0)


def partial_sums(picked, stay, blocks, groups, table, before=None, packed=True):
    smem = pl.BlockSpec(memory_space=pltpu.SMEM)
    hbm = pl.BlockSpec(memory_space=pl.ANY)
    vmem = pl.BlockSpec(memory_space=pltpu.VMEM)
    slots = sum(g[4] for g in picked)
    sums = [(ROWS_DEV, D), (ROWS_DEV, 128)]
    args, specs = [], []
    if picked[0] == GROUPS[0]:
        args, specs = [stay, blocks], [smem, hbm]
    args = args + list(groups) + [table]
    specs = specs + [hbm] * len(groups) + [vmem]
    if before is not None:
        args = args + list(before)
        specs = specs + [hbm, hbm]
    if packed:
        shapes, outs = jax.ShapeDtypeStruct((ROWS_DEV, WIDE), jnp.bfloat16), vmem
    else:
        shapes, outs = [jax.ShapeDtypeStruct(s, jnp.float32) for s in sums], [vmem, vmem]
    return pl.pallas_call(
        functools.partial(sums_kernel, picked, before is not None, packed),
        out_shape=shapes,
        in_specs=specs,
        out_specs=outs,
        scratch_shapes=([pltpu.VMEM(s, jnp.float32) for s in sums] if packed else [])
        + [
            pltpu.VMEM((slots // CAP, CAP * ROWBLK, D), jnp.bfloat16),
            pltpu.VMEM((ROWS_DEV, 128), jnp.float32),
            pltpu.VMEM((len(groups), TAG_ROWS, 128), jnp.bfloat16),
            pltpu.SMEM((slots,), jnp.int32),
            pltpu.SMEM((slots,), jnp.int32),
            pltpu.SemaphoreType.DMA((slots // CAP,)),
            pltpu.SemaphoreType.DMA((len(groups),)),
            pltpu.SemaphoreType.DMA((2,)),
        ],
        compiler_params=pltpu.CompilerParams(vmem_limit_bytes=40 * 1024 * 1024),
        cost_estimate=pl.CostEstimate(
            flops=slots * 4 * KIDS * ROWBLK * D,
            bytes_accessed=slots * ROWBLK * D * 2 + ROWS_DEV * (WIDE + D) * 2,
            transcendentals=slots * KIDS * ROWBLK,
        ),
    )(*args)


def move(value, shift, other):
    pairs = []
    for c in range(2):
        for z in range(8):
            pairs.append((c * 8 + z, (c ^ other) * 8 + (z + shift) % 8))
    return lax.ppermute(value, ("c", "z"), pairs)


def swap_cores(value):
    return lax.ppermute(value, "c", [(0, 1), (1, 0)])


def split_mass(value):
    high = lax.reduce_precision(value, 8, 7)
    return high.astype(jnp.bfloat16), (value - high).astype(jnp.bfloat16)


def shards(emb, centroids, block_parent, block_live):
    plane = ("y", "x")
    z = lax.axis_index("z").astype(jnp.int32)
    core = lax.axis_index("c").astype(jnp.int32)
    chip = lax.axis_index(plane)
    home = core == z // 4

    rank = lax.axis_index(("y", "x", "c"))
    piece = move(lax.dynamic_slice_in_dim(centroids, rank * 32, 32, 0), 4, 0)

    blocks = emb.reshape(-1, ROWBLK, D)
    *outgoing, stay = dispatch(jnp.stack([z, core]), block_parent, block_live, blocks)
    arrived = [move(value, g[0], g[1]) for value, g in zip(outgoing, SENT)]
    far = lax.all_to_all(
        jnp.broadcast_to(piece[None], (32, 32, D)).reshape(ROWS_DEV, D),
        ("y", "x", "c"), split_axis=0, concat_axis=0, tiled=True,
    )
    current = jnp.where(home, centroids, far)

    early = partial_sums(
        GROUPS[:EARLY], stay, blocks, arrived[: EARLY - 1], current, packed=False
    )
    sums = partial_sums(GROUPS[EARLY:], stay, blocks, arrived[EARLY - 1 :], current, before=early)

    parts = lax.all_to_all(sums, plane, split_axis=0, concat_axis=0, tiled=True)
    mine = jnp.sum(parts.reshape(CHIPS, PIECE, WIDE).astype(jnp.float32), axis=0)
    total = lax.reduce_precision(mine[:, :D], 8, 7)
    high, low = split_mass(mine[:, D : D + 1] + mine[:, D + 64 : D + 65])
    sent = jnp.concatenate(
        [
            total.astype(jnp.bfloat16),
            jnp.broadcast_to(high, (PIECE, 64)),
            jnp.broadcast_to(low, (PIECE, 64)),
        ],
        axis=1,
    )
    got = move(sent, 4, 0).astype(jnp.float32)
    total = total + got[:, :D]
    mass = (high.astype(jnp.float32) + low.astype(jnp.float32)) + (
        got[:, D : D + 1] + got[:, D + 64 : D + 65]
    )
    prior = lax.dynamic_slice_in_dim(current, chip * PIECE, PIECE, 0).astype(jnp.float32)
    updated = ((total + PRIOR * prior) / (mass + PRIOR)).astype(jnp.bfloat16)
    current = lax.all_to_all(
        jnp.broadcast_to(updated[None], (CHIPS, PIECE, D)).reshape(ROWS_DEV, D),
        plane, split_axis=0, concat_axis=0, tiled=True,
    )
    across = swap_cores(current)

    sums = partial_sums(GROUPS, stay, blocks, arrived, current)
    parts = lax.all_to_all(sums, plane, split_axis=0, concat_axis=0, tiled=True)
    mine = jnp.sum(parts.reshape(CHIPS, PIECE, WIDE).astype(jnp.float32), axis=0)
    total = mine[:, :D]
    mass = mine[:, D : D + 1] + mine[:, D + 64 : D + 65]
    high, low = split_mass(mass)
    sent = jnp.concatenate(
        [
            total.astype(jnp.bfloat16),
            jnp.broadcast_to(high, (PIECE, 64)),
            jnp.broadcast_to(low, (PIECE, 64)),
        ],
        axis=1,
    )
    homeward = [(o // 4 * 8 + (o + 4) % 8, o // 4 * 8 + o) for o in range(8)]
    got = lax.ppermute(sent, ("c", "z"), homeward).astype(jnp.float32)
    total = total + got[:, :D]
    mass = mass + (got[:, D : D + 1] + got[:, D + 64 : D + 65])
    prior = lax.dynamic_slice_in_dim(current, chip * PIECE, PIECE, 0).astype(jnp.float32)
    step = ((total - mass * prior) / (mass + PRIOR)).astype(jnp.bfloat16)

    half = PIECE // 2
    step = jnp.where(home, step, swap_cores(step))
    step = jnp.where(core == 0, step[:half], step[half:])
    step = lax.all_to_all(
        jnp.broadcast_to(step[None], (CHIPS, half, D)).reshape(ROWS_DEV // 2, D),
        plane, split_axis=0, concat_axis=0, tiled=True,
    )
    others = swap_cores(step)
    first = jnp.where(core == 0, step, others).reshape(CHIPS, half, D)
    second = jnp.where(core == 0, others, step).reshape(CHIPS, half, D)
    step = jnp.stack([first, second], axis=1).reshape(ROWS_DEV, D)
    return jnp.where(home, current, across).astype(jnp.float32) + step.astype(jnp.float32)


def solution(mesh):
    split = Mesh(mesh.devices.reshape(4, 4, 2, 8), ("y", "x", "c", "z"))
    all_axes = ("y", "x", "c", "z")
    placed = (P(all_axes, None), P("z", None), P(all_axes), P(all_axes))
    return jax.shard_map(
        shards, mesh=split, in_specs=placed, out_specs=P("z", None), check_vma=False
    )
```

time: 557 us -> 257 us (0.46)
  waiting for transfers between devices: 252 us -> 70.3 us
  other arithmetic: 71 us -> 9.29 us
  matrix products: 47.3 us -> 0 us
  blocking collectives: 125 us -> 79.6 us
  starting transfers between devices: 15.8 us -> 54.4 us
  Pallas kernels: 0 us -> 32.3 us
  local copies, waits for them, and re-layouts: 28.5 us -> 7.79 us
  between operations: 13.5 us -> 0.28 us
    all_to_all x2, waiting for transfers between devices: 142 us -> 13.3 us  [the longest x1 13.3 us: shards(): lax.all_to_all(jnp.broadcast_to(step[None], (CHIPS, half, D)).reshape(ROW...]
    psum x2 -> x0, blocking collectives: 125 us -> none  [shards(): summed, massed = lax.psum((total_sum, total_mass), 'dp')]
    psum x2 -> x0, waiting for transfers between devices: 110 us -> none  [shards(): summed, massed = lax.psum((total_sum, total_mass), 'dp')]
    all_to_all x0 -> x3, blocking collectives: none -> 79.6 us  [the longest x2 56.1 us: shards(): parts = lax.all_to_all(sums, plane, split_axis=0, concat_axis=0, tiled=True)]
    ppermute x0 -> x15, waiting for transfers between devices: none -> 57 us  [the longest x11 52.4 us: move(): return lax.ppermute(value, ('c', 'z'), pairs)]
    scatter-add x32 -> x0, other arithmetic: 55.9 us -> none  [the longest x16 46.3 us: accumulate(): total_sum.at[block_par].add(child_sum)]
    ppermute x0 -> x15, starting transfers between devices: none -> 41.8 us  [the longest x11 26.4 us: move(): return lax.ppermute(value, ('c', 'z'), pairs)]
    pallas_call x0 -> x4, Pallas kernels: none -> 32.3 us  [the longest x3 24.5 us: partial_sums(): pl.pallas_call(functools.partial(sums_kernel, picked, before is not None,...]
  transfers between devices with their start and end apart: 4 -> 17, of which waited for: 3 -> 10; matrix products, arithmetic and copies ran while one was open for 2% -> 1% of each run, Pallas kernels for 0% -> 6%
where the time goes in v1:
time: 257 us; the launch traced here: 254 us
  blocking collectives  79.6 us (31%)
  waiting for transfers between devices  70.3 us (27%)
  starting transfers between devices  54.4 us (21%)
  Pallas kernels  32.3 us (13%)
  other arithmetic  9.29 us (4%)
  local copies, waits for them, and re-layouts  7.79 us (3%)
    all_to_all x2, blocking collectives, shards(): parts = lax.all_to_all(sums, plane, split_axis=0, concat_axis=0, tiled=True)  56.1 us
    ppermute x11, waiting for transfers between devices, move(): return lax.ppermute(value, ('c', 'z'), pairs)  52.4 us
    ppermute x11, starting transfers between devices, move(): return lax.ppermute(value, ('c', 'z'), pairs)  26.4 us
    pallas_call x3, Pallas kernels, partial_sums(): pl.pallas_call(functools.partial(sums_kernel, picked, before is not None,...  24.5 us
    all_to_all x1, blocking collectives, shards(): lax.all_to_all(jnp.broadcast_to(updated[None], (CHIPS, PIECE, D)).reshape...  23.5 us
    all_to_all x1, waiting for transfers between devices, shards(): lax.all_to_all(jnp.broadcast_to(step[None], (CHIPS, half, D)).reshape(ROW...  13.3 us
    all_to_all x1, starting transfers between devices, shards(): lax.all_to_all(jnp.broadcast_to(piece[None], (32, 32, D)).reshape(ROWS_DE...  8.94 us
    ppermute x1, starting transfers between devices, shards(): got = lax.ppermute(sent, ('c', 'z'), homeward).astype(jnp.float32)  8.75 us
  transfers between devices with their start and end apart: 17, of which 10 were waited for; matrix products, arithmetic and copies ran while one was open for 1% of the time, Pallas kernels for 6%

profile of v1, /device:TPU:1, one launch (start us, length us, event | category | flops | bytes accessed | tf_op | source)
XLA Modules:
  0.0 254.0 jit_solution(591802631748328110)
XLA Ops:
  0.0 0.8 constant_dynamic-slice_fusion
  0.8 7.7 %collective-permute-start.4 = (bf16[32,768]{1,0:T(8,128)(2,1)S(1)}, bf16[32,768]{1,0:T(8,128)(2,1)S(1)}, u32[]{:S(2)}, u32[]{:S(2)}) collective-permute-start(bf16[32,768]{1,0:T(8,128)(2,1)S(1)} %constant_dynamic-slice_fusion), channel_id=1, source_target_pairs={{0,4},{1,5},{2,6},{3,7},{4,0},{5,1},{6,2},{7,3},{8,12},{9,13},{10,... | collective-permute-start | bytes 147464 | tf_op jit(solution)/shard_map/ppermute | solution.py:303
  8.5 1.5 collective-permute-done.4
  10.0 1.3 broadcast_in_dim.22
  11.3 8.9 %all-to-all-start = ((bf16[32,32,768]{2,1,0:T(8,128)(2,1)}), bf16[32,32,768]{2,1,0:T(8,128)(2,1)}, u32[]{:S(2)}, u32[]{:S(2)}) async-start(bf16[32,32,768]{2,1,0:T(8,128)(2,1)} %broadcast_in_dim.22), calls=%async_computation | async-start | bytes 3145728 | tf_op jit(solution)/shard_map/all_to_all | solution.py:328
  20.3 0.1 pad_add_fusion.pos_ref
  20.4 7.9 %shard_map.46 = (bf16[528,768]{1,0:T(8,128)(2,1)S(1)}, bf16[528,768]{1,0:T(8,128)(2,1)S(1)}, bf16[528,768]{1,0:T(8,128)(2,1)S(1)}, bf16[528,768]{1,0:T(8,128)(2,...) custom-call(s32[2]{0:T(128)S(1)} %pad_add_fusion.pos_ref, ...), custom_call_target="tpu_custom_call" | custom-call | bytes 12582912 | tf_op jit(solution)/shard_map/pallas_call | solution.py:113
  28.2 0.4 collective-permute-start.5
  28.6 0.8 collective-permute-start.6
  29.4 3.5 %collective-permute-start.7 = (bf16[528,768]{1,0:T(8,128)(2,1)S(1)}, bf16[528,768]{1,0:T(8,128)(2,1)S(1)}, u32[]{:S(2)}, u32[]{:S(2)}) collective-permute-start(bf16[528,768]{1,0:T(8,128)(2,1)S(1)} %get-tuple-element.24), channel_id=1, source_target_pairs={{0,7},{1,0},{2,1},{3,2},{4,3},{5,4},{6,5},{7,6},{8,15},{9,8},{10,9... | collective-permute-start | bytes 2433032 | tf_op jit(solution)/shard_map/ppermute | solution.py:303
  33.0 3.0 %collective-permute-start.9 = (bf16[528,768]{1,0:T(8,128)(2,1)}, bf16[528,768]{1,0:T(8,128)(2,1)}, u32[]{:S(2)}, u32[]{:S(2)}) collective-permute-start(bf16[528,768]{1,0:T(8,128)(2,1)} %get-tuple-element.26), channel_id=1, source_target_pairs={{0,15},{1,8},{2,9},{3,10},{4,11},{5,12},{6,13},{7,14},{8,7},{9,0},... | collective-permute-start | bytes 2433032 | tf_op jit(solution)/shard_map/ppermute | solution.py:303
  35.9 0.9 copy-done.4
  36.8 14.5 %collective-permute-done.6.refs_3_ = bf16[528,768]{1,0:T(8,128)(2,1)S(1)} collective-permute-done((bf16[528,768]{1,0:T(8,128)(2,1)S(1)}, bf16[528,768]{1,0:T(8,128)(2,1)S(1)}, u32[]{:S(2)}, u32[]{:S(2)}) %collective-permute-start.6) | collective-permute-done | bytes 811040 | tf_op jit(solution)/shard_map/ppermute | solution.py:303
  51.3 0.9 copy-done.7
  52.2 1.9 collective-permute-start.1
  54.1 0.9 copy-done.10
  55.0 1.7 collective-permute-start.2
  56.6 12.3 %collective-permute-done.8.refs_5_ = bf16[528,768]{1,0:T(8,128)(2,1)S(1)} collective-permute-done((bf16[528,768]{1,0:T(8,128)(2,1)S(1)}, bf16[528,768]{1,0:T(8,128)(2,1)S(1)}, u32[]{:S(2)}, u32[]{:S(2)}) %collective-permute-start.8) | collective-permute-done | bytes 811040 | tf_op jit(solution)/shard_map/ppermute | solution.py:303
  69.0 0.9 copy-done.13
  69.9 1.8 collective-permute-start.3
  71.7 1.7 bitcast_select_fusion.refs_7_.refs_4_
  73.5 0.0 copy-start.1
  73.5 0.1 copy-done.8
  73.6 0.2 copy-done.11
  73.8 0.2 copy-done.14
  74.1 8.1 %shard_map.47 = (f32[1024,768]{1,0:T(8,128)S(1)}, f32[1024,128]{1,0:T(8,128)S(1)}) custom-call(s32[3,4]{1,0:T(4,128)S(1)} %get-tuple-element.21.refs_0_, bf16[16,128,768]{2,1,0:T(8,128)(2,1)S(1)} %bitcast.18, bf16[528,768]{1,0:T(8,128)(2,1)S(1)} %copy-done.5, bf16[528,768]{1,0:T(8,128)(2,1)S(1)} %copy-done.8, bf16[528,768]{1,0:T(8,128)(2,1)S(1)} %copy-done.11, ...), custom_call_target="tpu_custom_call" | custom-call | flops 603979776 | bytes 8126464 | tf_op jit(solution)/shard_map/pallas_call | solution.py:273
  82.2 12.4 %collective-permute-done.1.refs_1_.refs_8_ = bf16[272,768]{1,0:T(8,128)(2,1)} collective-permute-done((bf16[272,768]{1,0:T(8,128)(2,1)}, bf16[272,768]{1,0:T(8,128)(2,1)}, u32[]{:S(2)}, u32[]{:S(2)}) %collective-permute-start.1) | collective-permute-done | bytes 417824 | tf_op jit(solution)/shard_map/ppermute | solution.py:303
  94.6 9.4 %collective-permute-done.3.refs_3_.refs_10_ = bf16[272,768]{1,0:T(8,128)(2,1)} collective-permute-done((bf16[272,768]{1,0:T(8,128)(2,1)}, bf16[272,768]{1,0:T(8,128)(2,1)}, u32[]{:S(2)}, u32[]{:S(2)}) %collective-permute-start.3) | collective-permute-done | bytes 417824 | tf_op jit(solution)/shard_map/ppermute | solution.py:303
  104.0 5.0 %shard_map.48 = bf16[1024,896]{1,0:T(8,128)(2,1)S(1)} custom-call(bf16[272,768]{1,0:T(8,128)(2,1)} %collective-permute-done.refs_0_.refs_7_, bf16[272,768]{1,0:T(8,128)(2,1)} %collective-permute-done.1.refs_1_.refs_8_, bf16[272,768]{1,0:T(8,128)(2,1)} %collective-permute-done.2.refs_2_.refs_9_, bf16[272,768]{1,0:T(8,128)(2,1)} %collective-permute-done.3.refs_3_.refs_10_, ...), custom_call_target="tpu_custom_call" | custom-call | flops 201326592 | bytes 4980736 | tf_op jit(solution)/shard_map/pallas_call | solution.py:273
  109.0 31.4 %all_to_all.44 = bf16[16,64,896]{2,1,0:T(8,128)(2,1)S(1)} all-to-all(bf16[16,64,896]{2,1,0:T(8,128)(2,1)S(1)} %bitcast.23), channel_id=1, replica_groups=mesh['y'=4,'x'=4,'c'=2,'z'=8] {'y','x'}, dimensions={0} | all-to-all | bytes 3670016 | tf_op jit(solution)/shard_map/all_to_all | solution.py:339
  140.5 0.2 convert_reduce_fusion.1
  140.7 0.2 fusion.16
  140.9 0.1 broadcast_in_dim.48
  141.0 0.1 broadcast_in_dim.50
  141.1 0.1 pad_maximum_fusion.1
  141.2 5.6 %collective-permute-start.10 = (bf16[64,896]{1,0:T(8,128)(2,1)S(1)}, bf16[64,896]{1,0:T(8,128)(2,1)}, u32[]{:S(2)}, u32[]{:S(2)}) collective-permute-start(bf16[64,896]{1,0:T(8,128)(2,1)S(1)} %pad_maximum_fusion.1), channel_id=1, source_target_pairs={{0,4},{1,5},{2,6},{3,7},{4,0},{5,1},{6,2},{7,3},{8,12},{9,13},{10,... | collective-permute-start | bytes 344072 | tf_op jit(solution)/shard_map/ppermute | solution.py:303
  146.8 2.3 collective-permute-done.10
  149.0 0.9 convert_element_type.61
  150.0 0.2 fusion.12
  150.1 1.0 fusion.4
  151.1 0.1 broadcast_in_dim.51
  151.3 23.5 %all_to_all.45 = bf16[16,64,768]{2,1,0:T(8,128)(2,1)S(1)} all-to-all(bf16[16,64,768]{2,1,0:T(8,128)(2,1)S(1)} %broadcast_in_dim.51), channel_id=1, replica_groups=mesh['y'=4,'x'=4,'c'=2,'z'=8] {'y','x'}, dimensions={0} | all-to-all | bytes 3145728 | tf_op jit(solution)/shard_map/all_to_all | solution.py:358
  174.9 11.3 %shard_map.49 = bf16[1024,896]{1,0:T(8,128)(2,1)S(1)} custom-call(s32[3,4]{1,0:T(4,128)S(1)} %get-tuple-element.21.refs_0_, bf16[16,128,768]{2,1,0:T(8,128)(2,1)S(1)} %bitcast.19, bf16[528,768]{1,0:T(8,128)(2,1)S(1)} %copy-done.6, bf16[528,768]{1,0:T(8,128)(2,1)S(1)} %copy-done.9, bf16[528,768]{1,0:T(8,128)(2,1)S(1)} %copy-done.12, ...), custom_call_target="tpu_custom_call" | custom-call | flops 805306368 | bytes 9699328 | tf_op jit(solution)/shard_map/pallas_call | solution.py:273
  186.2 24.7 %all_to_all.46 = bf16[16,64,896]{2,1,0:T(8,128)(2,1)S(1)} all-to-all(bf16[16,64,896]{2,1,0:T(8,128)(2,1)S(1)} %bitcast.24), channel_id=1, replica_groups=mesh['y'=4,'x'=4,'c'=2,'z'=8] {'y','x'}, dimensions={0} | all-to-all | bytes 3670016 | tf_op jit(solution)/shard_map/all_to_all | solution.py:365
  210.9 0.2 convert_reduce_fusion
  211.1 0.2 fusion.14
  211.3 0.1 broadcast_in_dim.53
  211.4 0.1 broadcast_in_dim.55
  211.5 0.1 pad_maximum_fusion.2
  211.6 8.7 %collective-permute-start.12 = (bf16[64,896]{1,0:T(8,128)(2,1)S(1)}, bf16[64,896]{1,0:T(8,128)(2,1)S(1)}, u32[]{:S(2)}, u32[]{:S(2)}) collective-permute-start(bf16[64,896]{1,0:T(8,128)(2,1)S(1)} %pad_maximum_fusion.2), channel_id=1, source_target_pairs={{4,0},{5,1},{6,2},{7,3},{8,12},{9,13},{10,14},{11,15},{20,16},{21,... | collective-permute-start | bytes 344072 | tf_op jit(solution)/shard_map/ppermute | solution.py:379
  220.3 1.8 collective-permute-done.12
  222.1 0.2 fusion.15
  222.3 0.1 fusion.5
  222.4 4.8 %collective-permute-start.13 = (bf16[64,768]{1,0:T(8,128)(2,1)S(1)}, bf16[64,768]{1,0:T(8,128)(2,1)S(1)}, u32[]{:S(2)}, u32[]{:S(2)}) collective-permute-start(bf16[64,768]{1,0:T(8,128)(2,1)S(1)} %fusion.5), channel_id=1, source_target_pairs={{0,8},{8,0},{1,9},{9,1},{2,10},{10,2},{3,11},{11,3},{4,12},{12,4},... | collective-permute-start | bytes 294920 | tf_op jit(solution)/shard_map/ppermute | solution.py:307
  227.2 0.9 collective-permute-done.13
  228.2 1.0 broadcast_in_dim.56
  229.2 3.6 %all-to-all-start.4 = ((bf16[16,32,768]{2,1,0:T(8,128)(2,1)}), bf16[16,32,768]{2,1,0:T(8,128)(2,1)S(1)}, u32[]{:S(2)}, u32[]{:S(2)}) async-start(bf16[16,32,768]{2,1,0:T(8,128)(2,1)} %broadcast_in_dim.56), calls=%async_computation.4 | async-start | bytes 1572864 | tf_op jit(solution)/shard_map/all_to_all | solution.py:388
  232.8 0.4 collective-permute-start.11
  233.3 13.3 %all-to-all-done.4 = bf16[16,32,768]{2,1,0:T(8,128)(2,1)S(1)} async-done(((bf16[16,32,768]{2,1,0:T(8,128)(2,1)}), bf16[16,32,768]{2,1,0:T(8,128)(2,1)S(1)}, u32[]{:S(2)}, u32[]{:S(2)}) %all-to-all-start.4) | async-done | bytes 786464 | tf_op jit(solution)/shard_map/all_to_all | solution.py:388
  246.6 1.5 collective-permute-start.14
  248.1 1.9 collective-permute-done.14
  250.0 0.2 broadcast_select_fusion.1
  250.2 0.2 pad_maximum_fusion
  250.3 3.7 %convert_add_fusion = f32[1024,768]{1,0:T(8,128)} fusion(bf16[16,2,32,768]{3,2,1,0:T(8,128)(2,1)S(1)} %pad_maximum_fusion, bf16[1024,768]{1,0:T(8,128)(2,1)} %collective-permute-done.11, pred[]{:T(512)S(6)} %eq.8, bf16[16,64,768]{2,1,0:T(8,128)(2,1)S(1)} %copy-done.3), kind=kLoop, calls=%fused_computation.2 | loop fusion | flops 3145728 | bytes 7864321 | tf_op jit(solution)/shard_map/add | solution.py:396
  (42 shorter events, 0.1 us)
Async XLA Ops:
  0.8 9.2 %collective-permute-start.4 = (bf16[32,768]{1,0:T(8,128)(2,1)S(1)}, bf16[32,768]{1,0:T(8,128)(2,1)S(1)}, u32[]{:S(2)}, u32[]{:S(2)}) collective-permute-start(bf16[32,768]{1,0:T(8,128)(2,1)S(1)} %constant_dynamic-slice_fusion), channel_id=1, source_target_pairs={{0,4},{1,5},{2,6},{3,7},{4,0},{5,1},{6,2},{7,3},{8,12},{9,13},{10,... | collective-permute-start | bytes 147464 | tf_op jit(solution)/shard_map/ppermute | solution.py:303
  11.3 9.0 %copy-start = (bf16[2048,768]{1,0:T(8,128)(2,1)S(1)}, bf16[2048,768]{1,0:T(8,128)(2,1)}, u32[]{:S(2)}) copy-start(bf16[2048,768]{1,0:T(8,128)(2,1)} %param.4) | copy-start | bytes 9437188
  11.3 9.0 %copy-start.16 = (s32[16]{0:T(128)S(1)}, s32[16]{0:T(128)}, u32[]{:S(2)}) copy-start(s32[16]{0:T(128)} %par_ref.1) | copy-start | bytes 196
  11.3 9.0 %copy-start.17 = (s32[16]{0:T(128)S(1)}, s32[16]{0:T(128)}, u32[]{:S(2)}) copy-start(s32[16]{0:T(128)} %live_ref.1) | copy-start | bytes 196
  11.3 60.4 %all-to-all-start = ((bf16[32,32,768]{2,1,0:T(8,128)(2,1)}), bf16[32,32,768]{2,1,0:T(8,128)(2,1)}, u32[]{:S(2)}, u32[]{:S(2)}) async-start(bf16[32,32,768]{2,1,0:T(8,128)(2,1)} %broadcast_in_dim.22), calls=%async_computation | async-start | bytes 3145728 | tf_op jit(solution)/shard_map/all_to_all | solution.py:328
  28.2 7.7 %collective-permute-start.5 = (bf16[528,768]{1,0:T(8,128)(2,1)S(1)}, bf16[528,768]{1,0:T(8,128)(2,1)S(1)}, u32[]{:S(2)}, u32[]{:S(2)}) collective-permute-start(bf16[528,768]{1,0:T(8,128)(2,1)S(1)} %get-tuple-element.22), channel_id=1, source_target_pairs={{0,8},{1,9},{2,10},{3,11},{4,12},{5,13},{6,14},{7,15},{8,0},{9,1},... | collective-permute-start | bytes 2433032 | tf_op jit(solution)/shard_map/ppermute | solution.py:303
  28.6 22.6 %collective-permute-start.6 = (bf16[528,768]{1,0:T(8,128)(2,1)S(1)}, bf16[528,768]{1,0:T(8,128)(2,1)S(1)}, u32[]{:S(2)}, u32[]{:S(2)}) collective-permute-start(bf16[528,768]{1,0:T(8,128)(2,1)S(1)} %get-tuple-element.23), channel_id=1, source_target_pairs={{0,1},{1,2},{2,3},{3,4},{4,5},{5,6},{6,7},{7,0},{8,9},{9,10},{10,1... | collective-permute-start | bytes 2433032 | tf_op jit(solution)/shard_map/ppermute | solution.py:303
  29.4 24.6 %collective-permute-start.7 = (bf16[528,768]{1,0:T(8,128)(2,1)S(1)}, bf16[528,768]{1,0:T(8,128)(2,1)S(1)}, u32[]{:S(2)}, u32[]{:S(2)}) collective-permute-start(bf16[528,768]{1,0:T(8,128)(2,1)S(1)} %get-tuple-element.24), channel_id=1, source_target_pairs={{0,7},{1,0},{2,1},{3,2},{4,3},{5,4},{6,5},{7,6},{8,15},{9,8},{10,9... | collective-permute-start | bytes 2433032 | tf_op jit(solution)/shard_map/ppermute | solution.py:303
  33.0 36.0 %collective-permute-start.8 = (bf16[528,768]{1,0:T(8,128)(2,1)S(1)}, bf16[528,768]{1,0:T(8,128)(2,1)S(1)}, u32[]{:S(2)}, u32[]{:S(2)}) collective-permute-start(bf16[528,768]{1,0:T(8,128)(2,1)S(1)} %get-tuple-element.25), channel_id=1, source_target_pairs={{0,9},{1,10},{2,11},{3,12},{4,13},{5,14},{6,15},{7,8},{8,1},{9,2},... | collective-permute-start | bytes 2433032 | tf_op jit(solution)/shard_map/ppermute | solution.py:303
  33.0 40.5 %collective-permute-start.9 = (bf16[528,768]{1,0:T(8,128)(2,1)}, bf16[528,768]{1,0:T(8,128)(2,1)}, u32[]{:S(2)}, u32[]{:S(2)}) collective-permute-start(bf16[528,768]{1,0:T(8,128)(2,1)} %get-tuple-element.26), channel_id=1, source_target_pairs={{0,15},{1,8},{2,9},{3,10},{4,11},{5,12},{6,13},{7,14},{8,7},{9,0},... | collective-permute-start | bytes 2433032 | tf_op jit(solution)/shard_map/ppermute | solution.py:303
  35.9 0.9 copy-start.4
  36.8 45.4 %collective-permute-start = (bf16[272,768]{1,0:T(8,128)(2,1)}, bf16[272,768]{1,0:T(8,128)(2,1)}, u32[]{:S(2)}, u32[]{:S(2)}) collective-permute-start(bf16[272,768]{1,0:T(8,128)(2,1)} %get-tuple-element.17), channel_id=1, source_target_pairs={{0,2},{1,3},{2,4},{3,5},{4,6},{5,7},{6,0},{7,1},{8,10},{9,11},{10,... | collective-permute-start | bytes 1253384 | tf_op jit(solution)/shard_map/ppermute | solution.py:303
  51.3 0.9 copy-start.7
  52.2 42.4 %collective-permute-start.1 = (bf16[272,768]{1,0:T(8,128)(2,1)}, bf16[272,768]{1,0:T(8,128)(2,1)}, u32[]{:S(2)}, u32[]{:S(2)}) collective-permute-start(bf16[272,768]{1,0:T(8,128)(2,1)} %get-tuple-element.18), channel_id=1, source_target_pairs={{0,6},{1,7},{2,0},{3,1},{4,2},{5,3},{6,4},{7,5},{8,14},{9,15},{10,... | collective-permute-start | bytes 1253384 | tf_op jit(solution)/shard_map/ppermute | solution.py:303
  54.1 0.9 copy-start.10
  55.0 39.6 %collective-permute-start.2 = (bf16[272,768]{1,0:T(8,128)(2,1)}, bf16[272,768]{1,0:T(8,128)(2,1)}, u32[]{:S(2)}, u32[]{:S(2)}) collective-permute-start(bf16[272,768]{1,0:T(8,128)(2,1)} %get-tuple-element.19), channel_id=1, source_target_pairs={{0,10},{1,11},{2,12},{3,13},{4,14},{5,15},{6,8},{7,9},{8,2},{9,3},... | collective-permute-start | bytes 1253384 | tf_op jit(solution)/shard_map/ppermute | solution.py:303
  69.0 0.9 copy-start.13
  69.9 34.1 %collective-permute-start.3 = (bf16[272,768]{1,0:T(8,128)(2,1)}, bf16[272,768]{1,0:T(8,128)(2,1)}, u32[]{:S(2)}, u32[]{:S(2)}) collective-permute-start(bf16[272,768]{1,0:T(8,128)(2,1)} %get-tuple-element.20), channel_id=1, source_target_pairs={{0,14},{1,15},{2,8},{3,9},{4,10},{5,11},{6,12},{7,13},{8,6},{9,7},... | collective-permute-start | bytes 1253384 | tf_op jit(solution)/shard_map/ppermute | solution.py:303
  71.7 1.8 copy-start.5
  71.7 1.9 copy-start.8
  71.7 2.1 copy-start.11
  71.7 2.3 copy-start.14
  73.5 30.5 %copy-start.1 = (bf16[1024,768]{1,0:T(8,128)(2,1)}, bf16[1024,768]{1,0:T(8,128)(2,1)S(1)}, u32[]{:S(2)}) copy-start(bf16[1024,768]{1,0:T(8,128)(2,1)S(1)} %bitcast_select_fusion.refs_7_.refs_4_) | copy-start | bytes 4718596
  141.2 7.9 %collective-permute-start.10 = (bf16[64,896]{1,0:T(8,128)(2,1)S(1)}, bf16[64,896]{1,0:T(8,128)(2,1)}, u32[]{:S(2)}, u32[]{:S(2)}) collective-permute-start(bf16[64,896]{1,0:T(8,128)(2,1)S(1)} %pad_maximum_fusion.1), channel_id=1, source_target_pairs={{0,4},{1,5},{2,6},{3,7},{4,0},{5,1},{6,2},{7,3},{8,12},{9,13},{10,... | collective-permute-start | bytes 344072 | tf_op jit(solution)/shard_map/ppermute | solution.py:303
  151.1 23.7 %copy-start.15 = (bf16[528,768]{1,0:T(8,128)(2,1)S(1)}, bf16[528,768]{1,0:T(8,128)(2,1)}, u32[]{:S(2)}) copy-start(bf16[528,768]{1,0:T(8,128)(2,1)} %copy-done.13) | copy-start | bytes 2433028
  151.3 23.5 %copy-start.6 = (bf16[528,768]{1,0:T(8,128)(2,1)S(1)}, bf16[528,768]{1,0:T(8,128)(2,1)}, u32[]{:S(2)}) copy-start(bf16[528,768]{1,0:T(8,128)(2,1)} %copy-done.4) | copy-start | bytes 2433028
  151.3 23.5 %copy-start.9 = (bf16[528,768]{1,0:T(8,128)(2,1)S(1)}, bf16[528,768]{1,0:T(8,128)(2,1)}, u32[]{:S(2)}) copy-start(bf16[528,768]{1,0:T(8,128)(2,1)} %copy-done.7) | copy-start | bytes 2433028
  151.3 23.5 %copy-start.12 = (bf16[528,768]{1,0:T(8,128)(2,1)S(1)}, bf16[528,768]{1,0:T(8,128)(2,1)}, u32[]{:S(2)}) copy-start(bf16[528,768]{1,0:T(8,128)(2,1)} %copy-done.10) | copy-start | bytes 2433028
  174.8 47.5 %copy-start.2 = (bf16[16,64,768]{2,1,0:T(8,128)(2,1)}, bf16[16,64,768]{2,1,0:T(8,128)(2,1)S(1)}, u32[]{:S(2)}) copy-start(bf16[16,64,768]{2,1,0:T(8,128)(2,1)S(1)} %all_to_all.45) | copy-start | bytes 4718596
  211.6 10.5 %collective-permute-start.12 = (bf16[64,896]{1,0:T(8,128)(2,1)S(1)}, bf16[64,896]{1,0:T(8,128)(2,1)S(1)}, u32[]{:S(2)}, u32[]{:S(2)}) collective-permute-start(bf16[64,896]{1,0:T(8,128)(2,1)S(1)} %pad_maximum_fusion.2), channel_id=1, source_target_pairs={{4,0},{5,1},{6,2},{7,3},{8,12},{9,13},{10,14},{11,15},{20,16},{21,... | collective-permute-start | bytes 344072 | tf_op jit(solution)/shard_map/ppermute | solution.py:379
  222.4 10.4 %copy-start.3 = (bf16[16,64,768]{2,1,0:T(8,128)(2,1)S(1)}, bf16[16,64,768]{2,1,0:T(8,128)(2,1)}, u32[]{:S(2)}) copy-start(bf16[16,64,768]{2,1,0:T(8,128)(2,1)} %copy-done.2) | copy-start | bytes 4718596
  222.4 5.8 %collective-permute-start.13 = (bf16[64,768]{1,0:T(8,128)(2,1)S(1)}, bf16[64,768]{1,0:T(8,128)(2,1)S(1)}, u32[]{:S(2)}, u32[]{:S(2)}) collective-permute-start(bf16[64,768]{1,0:T(8,128)(2,1)S(1)} %fusion.5), channel_id=1, source_target_pairs={{0,8},{8,0},{1,9},{9,1},{2,10},{10,2},{3,11},{11,3},{4,12},{12,4},... | collective-permute-start | bytes 294920 | tf_op jit(solution)/shard_map/ppermute | solution.py:307
  229.2 17.4 %all-to-all-start.4 = ((bf16[16,32,768]{2,1,0:T(8,128)(2,1)}), bf16[16,32,768]{2,1,0:T(8,128)(2,1)S(1)}, u32[]{:S(2)}, u32[]{:S(2)}) async-start(bf16[16,32,768]{2,1,0:T(8,128)(2,1)} %broadcast_in_dim.56), calls=%async_computation.4 | async-start | bytes 1572864 | tf_op jit(solution)/shard_map/all_to_all | solution.py:388
  232.8 17.5 %collective-permute-start.11 = (bf16[1024,768]{1,0:T(8,128)(2,1)S(1)}, bf16[1024,768]{1,0:T(8,128)(2,1)}, u32[]{:S(2)}, u32[]{:S(2)}) collective-permute-start(bf16[1024,768]{1,0:T(8,128)(2,1)S(1)} %bitcast.22), channel_id=1, source_target_pairs={{0,8},{8,0},{1,9},{9,1},{2,10},{10,2},{3,11},{11,3},{4,12},{12,4},... | collective-permute-start | bytes 4718600 | tf_op jit(solution)/shard_map/ppermute | solution.py:307
  246.6 3.4 %collective-permute-start.14 = (bf16[512,768]{1,0:T(8,128)(2,1)S(1)}, bf16[512,768]{1,0:T(8,128)(2,1)S(1)}, u32[]{:S(2)}, u32[]{:S(2)}) collective-permute-start(bf16[512,768]{1,0:T(8,128)(2,1)S(1)} %bitcast.25), channel_id=1, source_target_pairs={{0,8},{8,0},{1,9},{9,1},{2,10},{10,2},{3,11},{11,3},{4,12},{12,4},... | collective-permute-start | bytes 2359304 | tf_op jit(solution)/shard_map/ppermute | solution.py:307

commit v2 on v0

v2 whole, which is shorter than its diff:
```python
import functools
import math

import jax
import jax.numpy as jnp
from jax import lax
from jax.experimental import pallas as pl
from jax.experimental.pallas import tpu as pltpu
from jax.sharding import Mesh, PartitionSpec as P

D = 768
KIDS = 64
ROWBLK = 128
ITERS = 2
PRIOR = 64
OWNERS = 8
CAP = 4
SLOTS = OWNERS * CAP
PAR_DEV = 16
ROWS_DEV = PAR_DEV * KIDS
HALF = ROWS_DEV // 2
CHIPS = 8
PIECE = HALF // CHIPS
WIDE = D + 128

SOFTNESS = 0.8
LOGIT_SCALE = 1.0 / (SOFTNESS * math.sqrt(D))

FAR = 3

GROUPS = (
    (0, 0, 5),
    (1, 0, 5),
    (0, 6, 1),
    (0, 4, 7),
    (1, 6, 1),
    (1, 4, 7),
    (0, 2, 3),
    (1, 2, 3),
)
MOVES = {0: 0, 5: 0, 1: 1, 6: 1, 4: -1, 7: -1, 2: 2, 3: -2}
EARLY = 6
TAG_ROWS = 16
CHUNK = 8
GROUP_ROWS = CAP * ROWBLK
VMEM_ASKED = 56 * 1024 * 1024


def is_home(z, x):
    return z % 2 == x % 2


def offset_of(group, home):
    other, at_home, elsewhere = group
    return at_home if home != bool(other) else elsewhere


def dispatch_kernel(par_hbm, live_hbm, emb_hbm, *refs):
    outs = refs[: len(GROUPS)]
    par_ref, live_ref, held, built, src_ref, kid_ref, len_ref, count_ref, sems, out_sems = refs[
        len(GROUPS) :
    ]
    reads = [
        pltpu.make_async_copy(par_hbm, par_ref, sems.at[0]),
        pltpu.make_async_copy(live_hbm, live_ref, sems.at[1]),
        pltpu.make_async_copy(emb_hbm, held, sems.at[2]),
    ]
    for read in reads:
        read.start()
    z = lax.axis_index("z")
    home = is_home(z, lax.axis_index("xl"))
    for s in range(SLOTS):
        src_ref[s] = 0
        kid_ref[s] = 0
        len_ref[s] = 0
    for o in range(OWNERS):
        count_ref[o] = 0
    reads[0].wait()
    reads[1].wait()
    for b in range(held.shape[0]):
        parent = par_ref[b]
        owner = lax.shift_right_logical(parent, 4)
        rank = count_ref[owner]
        count_ref[owner] = rank + 1
        slot = lax.bitwise_and(owner - z, OWNERS - 1) * CAP + rank
        src_ref[slot] = b
        kid_ref[slot] = lax.bitwise_and(parent, PAR_DEV - 1)
        len_ref[slot] = live_ref[b]
    row = lax.broadcasted_iota(jnp.int32, (TAG_ROWS, 128), 0)
    lane = lax.broadcasted_iota(jnp.int32, (TAG_ROWS, 128), 1)
    firsts = []
    for other, at_home, elsewhere in GROUPS:
        here, there = (elsewhere, at_home) if other else (at_home, elsewhere)
        firsts.append(jnp.where(home, here, there) * CAP)
    for i, first in enumerate(firsts):
        tile = jnp.zeros((TAG_ROWS, 128), jnp.int32)
        for k in range(CAP):
            s = first + k
            tile = jnp.where(row == k, jnp.where(lane == 0, kid_ref[s], len_ref[s]), tile)
        built[i, GROUP_ROWS:, :128] = tile.astype(jnp.float32).astype(jnp.bfloat16)
    reads[2].wait()
    writes = []
    for i, first in enumerate(firsts):
        for k in range(CAP):
            built[i, k * ROWBLK : (k + 1) * ROWBLK, :] = held[src_ref[first + k]]
        write = pltpu.make_async_copy(built.at[i], outs[i], out_sems.at[i])
        write.start()
        writes.append(write)
    for write in writes:
        write.wait()


def dispatch(parents, lives, blocks):
    hbm = pl.BlockSpec(memory_space=pl.ANY)
    shape = jax.ShapeDtypeStruct((GROUP_ROWS + TAG_ROWS, D), jnp.bfloat16)
    return pl.pallas_call(
        dispatch_kernel,
        out_shape=[shape] * len(GROUPS),
        in_specs=[hbm] * 3,
        out_specs=[hbm] * len(GROUPS),
        scratch_shapes=[
            pltpu.SMEM(parents.shape, jnp.int32),
            pltpu.SMEM(lives.shape, jnp.int32),
            pltpu.VMEM(blocks.shape, jnp.bfloat16),
            pltpu.VMEM((len(GROUPS), *shape.shape), jnp.bfloat16),
            pltpu.SMEM((SLOTS,), jnp.int32),
            pltpu.SMEM((SLOTS,), jnp.int32),
            pltpu.SMEM((SLOTS,), jnp.int32),
            pltpu.SMEM((OWNERS,), jnp.int32),
            pltpu.SemaphoreType.DMA((3,)),
            pltpu.SemaphoreType.DMA((len(GROUPS),)),
        ],
        compiler_params=pltpu.CompilerParams(vmem_limit_bytes=VMEM_ASKED),
        cost_estimate=pl.CostEstimate(
            flops=0, bytes_accessed=12 * 1024 * 1024, transcendentals=0
        ),
    )(parents, lives, blocks)


def sums_kernel(count, listed, resumed, packed, *refs):
    refs = list(refs)
    groups = refs[:count]
    tables, tags_in = refs[count : count + 1 + listed], refs[count + 1 + listed : count + 1 + 3 * listed]
    del refs[: count + 1 + 3 * listed]
    if resumed:
        state_in = refs.pop(0)
    if packed:
        keep_ref, send_ref = refs[:2]
        del refs[:2]
    else:
        state_out = refs.pop(0)
    if not listed:
        tags_ref = refs.pop(0)
    state, table, rows, slot_ref, kid_ref, len_ref, sems, state_sem = refs
    tall = GROUP_ROWS + TAG_ROWS
    reads = []
    for i, ref in enumerate(groups):
        read = pltpu.make_async_copy(ref, rows.at[pl.ds(i * tall, tall)], sems.at[i])
        read.start()
        reads.append(read)
    if resumed:
        state_read = pltpu.make_async_copy(state_in, state, state_sem)
        state_read.start()
    core = lax.axis_index("c")
    if listed:
        table[:HALF, :] = tables[0][...]
        table[HALF:, :] = tables[1][...]
    else:
        own = pl.multiple_of(core * HALF, HALF)
        table[:HALF, :] = tables[0][pl.ds(own, HALF), :]
        table[HALF:, :] = tables[0][pl.ds(pl.multiple_of(HALF - own, HALF), HALF), :]

    def square(p, carry):
        at_p = pl.ds(pl.multiple_of(p * KIDS, KIDS), KIDS)
        kids = table[at_p, :].astype(jnp.float32)
        total = jnp.sum(kids * kids, axis=1, keepdims=True)
        state[at_p, WIDE:] = jnp.broadcast_to(total * LOGIT_SCALE, (KIDS, 128))
        return carry

    if not resumed:
        state[:, :WIDE] = jnp.zeros((ROWS_DEV, WIDE), jnp.float32)
        lax.fori_loop(0, PAR_DEV, square, 0)

    used = jnp.int32(0)
    for i in range(count):
        if not listed:
            reads[i].wait()
            tile = rows[i * tall + GROUP_ROWS : (i + 1) * tall, :128].astype(jnp.float32)
            tile = tile.astype(jnp.int32)
        for k in range(CAP):
            at = i * CAP + k
            if listed:
                source, at = (tags_in[0], at) if at < EARLY * CAP else (tags_in[1], at - EARLY * CAP)
                kid, length = source[0, at], source[1, at]
            else:
                kid, length = tile[k, 0], tile[k, 1]
                tags_ref[0, at] = kid
                tags_ref[1, at] = length
            slot_ref[used] = i * tall + k * ROWBLK
            kid_ref[used] = lax.bitwise_xor(kid * KIDS, core * HALF)
            len_ref[used] = length
            used = used + jnp.where(length > 0, 1, 0)
    for k in range(CHUNK):
        slot_ref[used + k] = 0
        kid_ref[used + k] = 0
        len_ref[used + k] = 0
    if listed:
        for read in reads:
            read.wait()
    if resumed:
        state_read.wait()
    lane = lax.broadcasted_iota(jnp.int32, (KIDS, ROWBLK), 1)

    def chunk(j, carry):
        places, blocks, found = [], [], []
        for k in range(CHUNK):
            at = j * CHUNK + k
            at_p = pl.ds(pl.multiple_of(kid_ref[at], KIDS), KIDS)
            at_b = pl.ds(pl.multiple_of(slot_ref[at], 16), ROWBLK)
            products = lax.dot_general(
                table[at_p, :],
                rows[at_b, :],
                (((1,), (1,)), ((), ())),
                preferred_element_type=jnp.float32,
            )
            logits = products * (2.0 * LOGIT_SCALE) - state[at_p, WIDE:]
            scaled = jnp.exp(logits - jnp.max(logits, axis=0, keepdims=True))
            weights = scaled / jnp.sum(scaled, axis=0, keepdims=True)
            weights = jnp.where(lane < len_ref[at], weights, 0.0)
            places.append(at_p)
            blocks.append(at_b)
            found.append(weights.astype(jnp.bfloat16))
        for k in range(CHUNK):
            state[places[k], :D] += jnp.dot(
                found[k], rows[blocks[k], :], preferred_element_type=jnp.float32
            )
            state[places[k], D:WIDE] += found[k].astype(jnp.float32)
        return carry

    lax.fori_loop(0, (used + CHUNK - 1) // CHUNK, chunk, 0)

    part = lax.broadcasted_iota(jnp.int32, (KIDS, 128), 1) // 32 - 2 * core

    def finish(p, carry):
        at_p = pl.ds(pl.multiple_of(p * KIDS, KIDS), KIDS)
        for first, out in ((0, keep_ref), (HALF, send_ref)):
            at_s = pl.ds(pl.multiple_of(first + p * KIDS, KIDS), KIDS)
            total = jnp.sum(state[at_s, D:WIDE], axis=1, keepdims=True)
            total = jnp.broadcast_to(total, (KIDS, 128))
            high = total.astype(jnp.bfloat16).astype(jnp.float32)
            out[at_p, :D] = state[at_s, :D].astype(jnp.bfloat16)
            out[at_p, D:] = jnp.where(
                part == 0, high, jnp.where(part == 1, total - high, 0.0)
            ).astype(jnp.bfloat16)
        return carry

    if packed:
        lax.fori_loop(0, PAR_DEV // 2, finish, 0)
    else:
        state_write = pltpu.make_async_copy(state, state_out, state_sem)
        state_write.start()
        state_write.wait()


def partial_sums(groups, tables, tags=(), state=None, packed=True):
    hbm = pl.BlockSpec(memory_space=pl.ANY)
    vmem = pl.BlockSpec(memory_space=pltpu.VMEM)
    smem = pl.BlockSpec(memory_space=pltpu.SMEM)
    slots = len(groups) * CAP
    shapes = [jax.ShapeDtypeStruct((HALF, WIDE), jnp.bfloat16)] * 2
    specs = [vmem, vmem]
    if not packed:
        shapes, specs = [jax.ShapeDtypeStruct((ROWS_DEV, WIDE + 128), jnp.float32)], [hbm]
    if not tags:
        shapes, specs = shapes + [jax.ShapeDtypeStruct((2, slots), jnp.int32)], specs + [smem]
    states = [] if state is None else [state]
    return pl.pallas_call(
        functools.partial(sums_kernel, len(groups), bool(tags), state is not None, packed),
        out_shape=shapes,
        in_specs=[hbm] * len(groups) + [vmem] * len(tables) + [smem] * len(tags) + [hbm] * len(states),
        out_specs=specs,
        scratch_shapes=[
            pltpu.VMEM((ROWS_DEV, WIDE + 128), jnp.float32),
            pltpu.VMEM((ROWS_DEV, D), jnp.bfloat16),
            pltpu.VMEM((len(groups) * (GROUP_ROWS + TAG_ROWS), D), jnp.bfloat16),
            pltpu.SMEM((slots + CHUNK,), jnp.int32),
            pltpu.SMEM((slots + CHUNK,), jnp.int32),
            pltpu.SMEM((slots + CHUNK,), jnp.int32),
            pltpu.SemaphoreType.DMA((len(groups),)),
            pltpu.SemaphoreType.DMA,
        ],
        compiler_params=pltpu.CompilerParams(vmem_limit_bytes=VMEM_ASKED),
        cost_estimate=pl.CostEstimate(
            flops=slots * 4 * KIDS * ROWBLK * D,
            bytes_accessed=slots * ROWBLK * D * 2 + ROWS_DEV * (WIDE + D) * 2,
            transcendentals=slots * KIDS * ROWBLK,
        ),
    )(*groups, *tables, *tags, *states)


AROUND = ("xh", "xl", "c", "z")


def permute(value, target):
    pairs = []
    for x in range(4):
        for core in range(2):
            for z in range(8):
                goal = target(x, core, z)
                if goal:
                    to_x, to_core, to_z = goal
                    goal = (to_x % 4 * 2 + to_core) * 8 + to_z % 8
                    pairs.append(((x * 2 + core) * 8 + z, goal))
    return lax.ppermute(value, AROUND, pairs)


def move_group(value, group):
    def target(x, core, z):
        step = MOVES[offset_of(group, is_home(z, x))]
        return (x + group[0] * (1 - 2 * core), core, z + step)

    return permute(value, target)


def swap_planes(value):
    return permute(value, lambda x, core, z: (x, core, z + (FAR if is_home(z, x) else -FAR)))


def to_home(value):
    return permute(value, lambda x, core, z: None if is_home(z, x) else (x, core, z - FAR))


def swap_cores(value):
    return lax.ppermute(value, "c", [(0, 1), (1, 0)])


def exchange(value, axes):
    return lax.all_to_all(value, axes, split_axis=0, concat_axis=0, tiled=True)


def spread(value, count, axes):
    wide = jnp.broadcast_to(value[None], (count, *value.shape))
    return exchange(wide.reshape(count * value.shape[0], value.shape[1]), axes)


def mass_of(value):
    return sum(value[:, D + 32 * part : D + 32 * part + 1] for part in range(4))


def reduced(keep, send):
    both = keep.astype(jnp.float32) + swap_cores(send).astype(jnp.float32)
    parts = exchange(both.astype(jnp.bfloat16), ("y", "xh")).reshape(CHIPS, PIECE, WIDE)
    mine = jnp.sum(parts.astype(jnp.float32), axis=0)
    total = lax.reduce_precision(mine[:, :D], 8, 7)
    mass = mass_of(mine)
    high = lax.reduce_precision(mass, 8, 7)
    low = lax.reduce_precision(mass - high, 8, 7)
    lane = lax.broadcasted_iota(jnp.int32, (PIECE, 128), 1) // 32
    split = jnp.where(lane == 0, high, jnp.where(lane == 1, low, 0.0))
    sent = jnp.concatenate([total, split], axis=1).astype(jnp.bfloat16)
    return mine[:, :D], total, mass, high + low, sent


def shards(emb, centroids, block_parent, block_live):
    z = lax.axis_index("z").astype(jnp.int32)
    core = lax.axis_index("c").astype(jnp.int32)
    odd = lax.axis_index("xl").astype(jnp.int32)
    home = is_home(z, odd)
    first_row = core * HALF + lax.axis_index(("y", "xh")) * PIECE

    rank = lax.axis_index(("y", "xh", "xl", "c"))
    piece = lax.ppermute(
        lax.dynamic_slice_in_dim(centroids, rank * 32, 32, 0),
        "z",
        [(p, (p + FAR) % 8) for p in range(8)],
    )
    outgoing = list(dispatch(block_parent, block_live, emb.reshape(-1, ROWBLK, D)))
    piece, outgoing[2] = lax.optimization_barrier((piece, outgoing[2]))
    far = lax.all_gather(piece, ("y", "xh", "xl", "c"), axis=0, tiled=True)
    arrived = [outgoing[0]] + [move_group(v, g) for v, g in zip(outgoing[1:], GROUPS[1:])]
    table = jnp.where(home, centroids, far)

    state, early_tags = partial_sums(arrived[:EARLY], [table], packed=False)
    keep, send, late_tags = partial_sums(arrived[EARLY:], [table], state=state)

    _, total, _, mass, sent = reduced(keep, send)
    got = swap_planes(sent).astype(jnp.float32)
    total, mass = total + got[:, :D], mass + mass_of(got)
    prior = lax.dynamic_slice_in_dim(table, first_row, PIECE, 0).astype(jnp.float32)
    updated = ((total + PRIOR * prior) / (mass + PRIOR)).astype(jnp.bfloat16)
    own = spread(updated, CHIPS, ("y", "xh"))
    tables = [own, swap_cores(own)]

    keep, send = partial_sums(arrived, tables, tags=(early_tags, late_tags))
    total, _, mass, _, sent = reduced(keep, send)
    got = to_home(sent).astype(jnp.float32)
    total, mass = total + got[:, :D], mass + mass_of(got)
    updated = (total + PRIOR * updated.astype(jnp.float32)) / (mass + PRIOR)

    way = (updated - prior).astype(jnp.bfloat16)
    way = jnp.where(home, way, lax.ppermute(way, "xl", [(0, 1), (1, 0)]))
    way = spread(
        jnp.where(odd == 0, way[: PIECE // 2], way[PIECE // 2 :]), 2 * CHIPS, ("y", "xh", "xl")
    )
    others = swap_cores(way)
    way = jnp.concatenate([jnp.where(core == 0, way, others), jnp.where(core == 0, others, way)])
    return centroids.astype(jnp.float32) + way.astype(jnp.float32)


def solution(mesh):
    split = Mesh(mesh.devices.reshape(4, 2, 2, 2, 8), ("y", *AROUND))
    everywhere = ("y", *AROUND)
    placed = (P(everywhere, None), P("z", None), P(everywhere), P(everywhere))
    return jax.shard_map(
        shards, mesh=split, in_specs=placed, out_specs=P("z", None), check_vma=False
    )
```

time: 557 us -> 237 us (0.43)
  waiting for transfers between devices: 252 us -> 81.1 us
  blocking collectives: 125 us -> 50.8 us
  other arithmetic: 71 us -> 10.6 us
  matrix products: 47.3 us -> 0 us
  starting transfers between devices: 15.8 us -> 47.2 us
  Pallas kernels: 0 us -> 30.3 us
  local copies, waits for them, and re-layouts: 28.5 us -> 2.57 us
    all_to_all x2 -> x1, waiting for transfers between devices: 142 us -> 15.2 us  [exchange(): return lax.all_to_all(value, axes, split_axis=0, concat_axis=0, tiled=True)]
    psum x2 -> x0, blocking collectives: 125 us -> none  [shards(): summed, massed = lax.psum((total_sum, total_mass), 'dp')]
    psum x2 -> x0, waiting for transfers between devices: 110 us -> none  [shards(): summed, massed = lax.psum((total_sum, total_mass), 'dp')]
    scatter-add x32 -> x0, other arithmetic: 55.9 us -> none  [the longest x16 46.3 us: accumulate(): total_sum.at[block_par].add(child_sum)]
    all_to_all x0 -> x3, blocking collectives: none -> 50.8 us  [exchange(): return lax.all_to_all(value, axes, split_axis=0, concat_axis=0, tiled=True)]
    ppermute x0 -> x15, starting transfers between devices: none -> 42.8 us  [the longest x9 21.6 us: permute(): return lax.ppermute(value, AROUND, pairs)]
    ppermute x0 -> x15, waiting for transfers between devices: none -> 38.4 us  [the longest x9 28 us: permute(): return lax.ppermute(value, AROUND, pairs)]
    pallas_call x0 -> x4, Pallas kernels: none -> 30.3 us  [the longest x3 25.5 us: partial_sums(): pl.pallas_call(functools.partial(sums_kernel, len(groups), bool(tags), st...]
  transfers between devices with their start and end apart: 4 -> 17, of which waited for: 3 -> 12; matrix products, arithmetic and copies ran while one was open for 2% -> 1% of each run, Pallas kernels for 0% -> 6%
where the time goes in v2:
time: 237 us; the launch traced here: 236 us
  waiting for transfers between devices  81.1 us (34%)
  blocking collectives  50.8 us (21%)
  starting transfers between devices  47.2 us (20%)
  Pallas kernels  30.3 us (13%)
  between operations  13.6 us (6%)
  other arithmetic  10.6 us (4%)
  local copies, waits for them, and re-layouts  2.57 us (1%)
    all_to_all x3, blocking collectives, exchange(): return lax.all_to_all(value, axes, split_axis=0, concat_axis=0, tiled=True)  50.8 us
    ppermute x9, waiting for transfers between devices, permute(): return lax.ppermute(value, AROUND, pairs)  28 us
    all_gather x1, waiting for transfers between devices, shards(): far = lax.all_gather(piece, ('y', 'xh', 'xl', 'c'), axis=0, tiled=True)  27.5 us
    pallas_call x3, Pallas kernels, partial_sums(): pl.pallas_call(functools.partial(sums_kernel, len(groups), bool(tags), st...  25.5 us
    ppermute x9, starting transfers between devices, permute(): return lax.ppermute(value, AROUND, pairs)  21.6 us
    all_to_all x1, waiting for transfers between devices, exchange(): return lax.all_to_all(value, axes, split_axis=0, concat_axis=0, tiled=True)  15.2 us
    ppermute x4, starting transfers between devices, swap_cores(): return lax.ppermute(value, 'c', [(0, 1), (1, 0)])  9.26 us
    ppermute x4, waiting for transfers between devices, swap_cores(): return lax.ppermute(value, 'c', [(0, 1), (1, 0)])  8.45 us
  transfers between devices with their start and end apart: 17, of which 12 were waited for; matrix products, arithmetic and copies ran while one was open for 1% of the time, Pallas kernels for 6%

profile of v2, /device:TPU:1, one launch (start us, length us, event | category | flops | bytes accessed | tf_op | source)
XLA Modules:
  0.0 236.2 jit_solution(7459917397102476748)
XLA Ops:
  6.5 0.0 all-gather.2.cloned.1.call-start
  6.5 0.9 constant_dynamic-slice_fusion
  7.5 5.2 %collective-permute-start.1 = (bf16[32,768]{1,0:T(8,128)(2,1)S(1)}, bf16[32,768]{1,0:T(8,128)(2,1)S(1)}, u32[]{:S(2)}, u32[]{:S(2)}) collective-permute-start(bf16[32,768]{1,0:T(8,128)(2,1)S(1)} %constant_dynamic-slice_fusion), channel_id=1, source_target_pairs={{0,3},{1,4},{2,5},{3,6},{4,7},{5,0},{6,1},{7,2},{8,11},{9,12},{10,... | collective-permute-start | bytes 147464 | tf_op jit(solution)/shard_map/ppermute | solution.py:372
  12.6 4.8 %shard_map.46 = (bf16[528,768]{1,0:T(8,128)(2,1)}, bf16[528,768]{1,0:T(8,128)(2,1)}, bf16[528,768]{1,0:T(8,128)(2,1)}, bf16[528,768]{1,0:T(8,128)(2,1)}, bf16[52...) custom-call(s32[16]{0:T(128)} %par_hbm.1, s32[16]{0:T(128)} %live_hbm.1, ...), custom_call_target="tpu_custom_call" | custom-call | bytes 12582912 | tf_op jit(solution)/shard_map/pallas_call | solution.py:116
  17.4 0.0 collective-permute-done.1
  17.5 0.0 copy-start.5
  17.5 0.6 copy-done.5
  18.1 0.0 all-gather.2.cloned.1.call-update
  18.1 2.6 %collective-permute-start = (bf16[528,768]{1,0:T(8,128)(2,1)}, bf16[528,768]{1,0:T(8,128)(2,1)S(1)}, u32[]{:S(2)}, u32[]{:S(2)}) collective-permute-start(bf16[528,768]{1,0:T(8,128)(2,1)} %get-tuple-element.23), channel_id=1, source_target_pairs={{0,16},{1,17},{2,18},{3,19},{4,20},{5,21},{6,22},{7,23},{8,56},{9,... | collective-permute-start | bytes 2433032 | tf_op jit(solution)/shard_map/ppermute | solution.py:314
  20.7 1.2 collective-permute-start.3
  21.9 1.9 collective-permute-start.4
  23.8 1.0 collective-permute-start.5
  24.8 0.4 collective-permute-start.2
  25.3 12.3 %collective-permute-done.refs_1_ = bf16[528,768]{1,0:T(8,128)(2,1)S(1)} collective-permute-done((bf16[528,768]{1,0:T(8,128)(2,1)}, bf16[528,768]{1,0:T(8,128)(2,1)S(1)}, u32[]{:S(2)}, u32[]{:S(2)}) %collective-permute-start) | collective-permute-done | bytes 811040 | tf_op jit(solution)/shard_map/ppermute | solution.py:314
  37.5 4.7 %collective-permute-start.6 = (bf16[528,768]{1,0:T(8,128)(2,1)}, bf16[528,768]{1,0:T(8,128)(2,1)}, u32[]{:S(2)}, u32[]{:S(2)}) collective-permute-start(bf16[528,768]{1,0:T(8,128)(2,1)} %get-tuple-element.29), channel_id=1, source_target_pairs={{0,2},{1,7},{2,4},{3,1},{4,6},{5,3},{6,0},{7,5},{8,10},{9,15},{10,... | collective-permute-start | bytes 2433032 | tf_op jit(solution)/shard_map/ppermute | solution.py:314
  42.2 0.1 collective-permute-done.3.refs_3_
  42.3 3.2 %collective-permute-start.7 = (bf16[528,768]{1,0:T(8,128)(2,1)}, bf16[528,768]{1,0:T(8,128)(2,1)}, u32[]{:S(2)}, u32[]{:S(2)}) collective-permute-start(bf16[528,768]{1,0:T(8,128)(2,1)} %get-tuple-element.30), channel_id=1, source_target_pairs={{0,22},{1,19},{2,16},{3,21},{4,18},{5,23},{6,20},{7,17},{8,62},{9,... | collective-permute-start | bytes 2433032 | tf_op jit(solution)/shard_map/ppermute | solution.py:314
  45.5 27.5 %all-gather.2.cloned.1.call-done = bf16[1024,768]{1,0:T(8,128)(2,1)} async-done(((bf16[32,768]{1,0:T(8,128)(2,1)}), bf16[1024,768]{1,0:T(8,128)(2,1)}) %all-gather.2.cloned.1.call-update) | async-done | bytes 1572880 | tf_op jit(solution)/shard_map/all_gather | solution.py:379
  73.0 0.0 copy-done
  73.0 1.3 broadcast_select_fusion.refs_6_.refs_2_
  74.3 0.0 collective-permute-done.4.refs_4_
  74.3 0.0 collective-permute-done.5.refs_5_
  74.3 0.0 collective-permute-done.2.refs_2_
  74.3 9.4 %shard_map.47 = (f32[1024,1024]{1,0:T(8,128)}, s32[2,24]{1,0:T(2,128)}) custom-call(bf16[528,768]{1,0:T(8,128)(2,1)} %get-tuple-element.22.refs_0_, bf16[528,768]{1,0:T(8,128)(2,1)} %copy-done.1, bf16[528,768]{1,0:T(8,128)(2,1)} %collective-permute-done.2.refs_2_, bf16[528,768]{1,0:T(8,128)(2,1)} %copy-done.2, ...), custom_call_target="tpu_custom_call" | custom-call | flops 603979776 | bytes 8126464 | tf_op jit(solution)/shard_map/pallas_call | solution.py:277
  83.7 0.0 collective-permute-done.6.refs_0_.refs_6_
  83.7 7.3 %collective-permute-done.7.refs_1_.refs_7_ = bf16[528,768]{1,0:T(8,128)(2,1)} collective-permute-done((bf16[528,768]{1,0:T(8,128)(2,1)}, bf16[528,768]{1,0:T(8,128)(2,1)}, u32[]{:S(2)}, u32[]{:S(2)}) %collective-permute-start.7) | collective-permute-done | bytes 811040 | tf_op jit(solution)/shard_map/ppermute | solution.py:314
  91.0 7.1 %shard_map.48 = (bf16[512,896]{1,0:T(8,128)(2,1)}, bf16[512,896]{1,0:T(8,128)(2,1)}, s32[2,8]{1,0:T(2,128)}) custom-call(bf16[528,768]{1,0:T(8,128)(2,1)} %collective-permute-done.6.refs_0_.refs_6_, bf16[528,768]{1,0:T(8,128)(2,1)} %collective-permute-done.7.refs_1_.refs_7_, bf16[1024,768]{1,0:T(8,128)(2,1)} %broadcast_select_fusion.refs_6_.refs_2_, ...), custom_call_target="tpu_custom_call" | custom-call | flops 201326592 | bytes 4980736 | tf_op jit(solution)/shard_map/pallas_call | solution.py:277
  98.1 1.7 collective-permute-start.8
  99.8 2.3 collective-permute-done.8
  102.1 2.4 add_convert_fusion.1
  104.5 4.4 %all-to-all-start = ((bf16[8,64,896]{2,1,0:T(8,128)(2,1)}), bf16[8,64,896]{2,1,0:T(8,128)(2,1)S(1)}, u32[]{:S(2)}, u32[]{:S(2)}) async-start(bf16[8,64,896]{2,1,0:T(8,128)(2,1)} %bitcast.1), calls=%async_computation | async-start | bytes 1835008 | tf_op jit(solution)/shard_map/all_to_all | solution.py:338
  108.9 15.2 %all-to-all-done = bf16[8,64,896]{2,1,0:T(8,128)(2,1)S(1)} async-done(((bf16[8,64,896]{2,1,0:T(8,128)(2,1)}), bf16[8,64,896]{2,1,0:T(8,128)(2,1)S(1)}, u32[]{:S(2)}, u32[]{:S(2)}) %all-to-all-start) | async-done | bytes 917536 | tf_op jit(solution)/shard_map/all_to_all | solution.py:338
  124.2 0.1 convert_reduce_fusion.1
  124.3 0.2 reduce-precision_reduce_fusion.1
  124.5 0.1 fusion.11
  124.6 5.3 %collective-permute-start.9 = (bf16[64,896]{1,0:T(8,128)(2,1)S(1)}, bf16[64,896]{1,0:T(8,128)(2,1)S(1)}, u32[]{:S(2)}, u32[]{:S(2)}) collective-permute-start(bf16[64,896]{1,0:T(8,128)(2,1)S(1)} %pad_maximum_fusion), channel_id=1, source_target_pairs={{0,3},{1,6},{2,5},{3,0},{4,7},{5,2},{6,1},{7,4},{8,11},{9,14},{10,... | collective-permute-start | bytes 344072 | tf_op jit(solution)/shard_map/ppermute | solution.py:314
  129.9 2.3 collective-permute-done.9
  132.2 0.2 fusion.17
  132.4 1.0 fusion.2
  133.4 0.1 broadcast_in_dim.56
  133.5 16.1 %all_to_all.35 = bf16[8,64,768]{2,1,0:T(8,128)(2,1)S(1)} all-to-all(bf16[8,64,768]{2,1,0:T(8,128)(2,1)S(1)} %broadcast_in_dim.56), channel_id=1, replica_groups=mesh['y'=4,'xh'=2,'xl'=2,'c'=2,'z'=8] {'y','xh'}, dimensions={0} | all-to-all | bytes 1572864 | tf_op jit(solution)/shard_map/all_to_all | solution.py:338
  149.6 3.3 %collective-permute-start.10 = (bf16[512,768]{1,0:T(8,128)(2,1)S(1)}, bf16[512,768]{1,0:T(8,128)(2,1)S(1)}, u32[]{:S(2)}, u32[]{:S(2)}) collective-permute-start(bf16[512,768]{1,0:T(8,128)(2,1)S(1)} %bitcast.8), channel_id=1, source_target_pairs={{0,8},{8,0},{1,9},{9,1},{2,10},{10,2},{3,11},{11,3},{4,12},{12,4},... | collective-permute-start | bytes 2359304 | tf_op jit(solution)/shard_map/ppermute | solution.py:334
  152.9 1.9 collective-permute-done.10.refs_9_
  154.8 0.9 copy-done.4
  155.7 9.1 %shard_map.49 = (bf16[512,896]{1,0:T(8,128)(2,1)}, bf16[512,896]{1,0:T(8,128)(2,1)}) custom-call(bf16[528,768]{1,0:T(8,128)(2,1)} %get-tuple-element.22.refs_0_, bf16[528,768]{1,0:T(8,128)(2,1)} %copy-done.1, bf16[528,768]{1,0:T(8,128)(2,1)} %collective-permute-done.2.refs_2_, bf16[528,768]{1,0:T(8,128)(2,1)} %copy-done.2, ...), custom_call_target="tpu_custom_call" | custom-call | flops 805306368 | bytes 9699328 | tf_op jit(solution)/shard_map/pallas_call | solution.py:277
  164.8 0.5 collective-permute-start.11
  165.3 2.3 collective-permute-done.11
  167.6 1.4 add_convert_fusion
  169.0 17.8 %all_to_all.36 = bf16[8,64,896]{2,1,0:T(8,128)(2,1)S(1)} all-to-all(bf16[8,64,896]{2,1,0:T(8,128)(2,1)S(1)} %bitcast.7), channel_id=1, replica_groups=mesh['y'=4,'xh'=2,'xl'=2,'c'=2,'z'=8] {'y','xh'}, dimensions={0} | all-to-all | bytes 1835008 | tf_op jit(solution)/shard_map/all_to_all | solution.py:338
  186.8 0.1 convert_reduce_fusion
  186.9 0.2 reduce-precision_reduce_fusion
  187.1 0.1 fusion.12
  187.2 1.3 collective-permute-start.12
  188.5 6.0 %collective-permute-done.12 = bf16[64,896]{1,0:T(8,128)(2,1)S(1)} collective-permute-done((bf16[64,896]{1,0:T(8,128)(2,1)S(1)}, bf16[64,896]{1,0:T(8,128)(2,1)S(1)}, u32[]{:S(2)}, u32[]{:S(2)}) %collective-permute-start.12) | collective-permute-done | bytes 114720 | tf_op jit(solution)/shard_map/ppermute | solution.py:314
  194.6 0.2 fusion.22
  194.8 1.0 fusion.3
  195.8 6.7 %collective-permute-start.13 = (bf16[64,768]{1,0:T(8,128)(2,1)S(1)}, bf16[64,768]{1,0:T(8,128)(2,1)S(1)}, u32[]{:S(2)}, u32[]{:S(2)}) collective-permute-start(bf16[64,768]{1,0:T(8,128)(2,1)S(1)} %fusion.3), channel_id=1, source_target_pairs={{0,16},{16,0},{1,17},{17,1},{2,18},{18,2},{3,19},{19,3},{4,20},{20... | collective-permute-start | bytes 294920 | tf_op jit(solution)/shard_map/ppermute | solution.py:401
  202.5 2.0 collective-permute-done.13
  204.5 0.1 broadcast_in_dim.61
  204.6 16.9 %all_to_all.37 = bf16[16,32,768]{2,1,0:T(8,128)(2,1)S(1)} all-to-all(bf16[16,32,768]{2,1,0:T(8,128)(2,1)S(1)} %broadcast_in_dim.61), channel_id=1, replica_groups=mesh['y'=4,'xh'=2,'xl'=2,'c'=2,'z'=8] {'y','xh','xl'}, dimensions={0} | all-to-all | bytes 1572864 | tf_op jit(solution)/shard_map/all_to_all | solution.py:338
  221.5 3.7 %collective-permute-start.14 = (bf16[512,768]{1,0:T(8,128)(2,1)S(1)}, bf16[512,768]{1,0:T(8,128)(2,1)S(1)}, u32[]{:S(2)}, u32[]{:S(2)}) collective-permute-start(bf16[512,768]{1,0:T(8,128)(2,1)S(1)} %bitcast.11), channel_id=1, source_target_pairs={{0,8},{8,0},{1,9},{9,1},{2,10},{10,2},{3,11},{11,3},{4,12},{12,4},... | collective-permute-start | bytes 2359304 | tf_op jit(solution)/shard_map/ppermute | solution.py:334
  225.2 1.9 collective-permute-done.14
  227.1 0.2 broadcast_select_fusion.2
  227.3 2.1 convert_add_fusion
  (18 shorter events, 0.1 us)
Async XLA Ops:
  6.5 66.5 %copy-start = (bf16[1024,768]{1,0:T(8,128)(2,1)S(1)}, bf16[1024,768]{1,0:T(8,128)(2,1)}, u32[]{:S(2)}) copy-start(bf16[1024,768]{1,0:T(8,128)(2,1)} %param.5) | copy-start | bytes 4718596
  6.5 66.5 %all-gather.2.cloned.1.call-start = ((), (), s32[]{:S(2)}) async-start(), calls=%async_computation.4 | async-start | bytes 1622016 | tf_op jit(solution)/shard_map/all_gather | solution.py:379
  7.5 10.0 %collective-permute-start.1 = (bf16[32,768]{1,0:T(8,128)(2,1)S(1)}, bf16[32,768]{1,0:T(8,128)(2,1)S(1)}, u32[]{:S(2)}, u32[]{:S(2)}) collective-permute-start(bf16[32,768]{1,0:T(8,128)(2,1)S(1)} %constant_dynamic-slice_fusion), channel_id=1, source_target_pairs={{0,3},{1,4},{2,5},{3,6},{4,7},{5,0},{6,1},{7,2},{8,11},{9,12},{10,... | collective-permute-start | bytes 147464 | tf_op jit(solution)/shard_map/ppermute | solution.py:372
  17.5 0.6 copy-start.5
  18.1 19.4 %collective-permute-start = (bf16[528,768]{1,0:T(8,128)(2,1)}, bf16[528,768]{1,0:T(8,128)(2,1)S(1)}, u32[]{:S(2)}, u32[]{:S(2)}) collective-permute-start(bf16[528,768]{1,0:T(8,128)(2,1)} %get-tuple-element.23), channel_id=1, source_target_pairs={{0,16},{1,17},{2,18},{3,19},{4,20},{5,21},{6,22},{7,23},{8,56},{9,... | collective-permute-start | bytes 2433032 | tf_op jit(solution)/shard_map/ppermute | solution.py:314
  20.7 21.6 %collective-permute-start.3 = (bf16[528,768]{1,0:T(8,128)(2,1)}, bf16[528,768]{1,0:T(8,128)(2,1)S(1)}, u32[]{:S(2)}, u32[]{:S(2)}) collective-permute-start(bf16[528,768]{1,0:T(8,128)(2,1)} %get-tuple-element.26), channel_id=1, source_target_pairs={{0,7},{1,0},{2,1},{3,2},{4,3},{5,4},{6,5},{7,6},{8,15},{9,8},{10,9... | collective-permute-start | bytes 2433032 | tf_op jit(solution)/shard_map/ppermute | solution.py:314
  21.9 52.4 %collective-permute-start.4 = (bf16[528,768]{1,0:T(8,128)(2,1)}, bf16[528,768]{1,0:T(8,128)(2,1)}, u32[]{:S(2)}, u32[]{:S(2)}) collective-permute-start(bf16[528,768]{1,0:T(8,128)(2,1)} %get-tuple-element.27), channel_id=1, source_target_pairs={{0,17},{1,18},{2,19},{3,20},{4,21},{5,22},{6,23},{7,16},{8,57},{9,... | collective-permute-start | bytes 2433032 | tf_op jit(solution)/shard_map/ppermute | solution.py:314
  23.8 50.5 %collective-permute-start.5 = (bf16[528,768]{1,0:T(8,128)(2,1)}, bf16[528,768]{1,0:T(8,128)(2,1)}, u32[]{:S(2)}, u32[]{:S(2)}) collective-permute-start(bf16[528,768]{1,0:T(8,128)(2,1)} %get-tuple-element.28), channel_id=1, source_target_pairs={{0,23},{1,16},{2,17},{3,18},{4,19},{5,20},{6,21},{7,22},{8,63},{9,... | collective-permute-start | bytes 2433032 | tf_op jit(solution)/shard_map/ppermute | solution.py:314
  24.8 49.5 %collective-permute-start.2 = (bf16[528,768]{1,0:T(8,128)(2,1)}, bf16[528,768]{1,0:T(8,128)(2,1)}, u32[]{:S(2)}, u32[]{:S(2)}) collective-permute-start(bf16[528,768]{1,0:T(8,128)(2,1)} %get-tuple-element.25), channel_id=1, source_target_pairs={{0,1},{1,2},{2,3},{3,4},{4,5},{5,6},{6,7},{7,0},{8,9},{9,10},{10,1... | collective-permute-start | bytes 2433032 | tf_op jit(solution)/shard_map/ppermute | solution.py:314
  37.5 36.8 %copy-start.1 = (bf16[528,768]{1,0:T(8,128)(2,1)}, bf16[528,768]{1,0:T(8,128)(2,1)S(1)}, u32[]{:S(2)}) copy-start(bf16[528,768]{1,0:T(8,128)(2,1)S(1)} %collective-permute-done.refs_1_) | copy-start | bytes 2433028
  37.5 46.2 %collective-permute-start.6 = (bf16[528,768]{1,0:T(8,128)(2,1)}, bf16[528,768]{1,0:T(8,128)(2,1)}, u32[]{:S(2)}, u32[]{:S(2)}) collective-permute-start(bf16[528,768]{1,0:T(8,128)(2,1)} %get-tuple-element.29), channel_id=1, source_target_pairs={{0,2},{1,7},{2,4},{3,1},{4,6},{5,3},{6,0},{7,5},{8,10},{9,15},{10,... | collective-permute-start | bytes 2433032 | tf_op jit(solution)/shard_map/ppermute | solution.py:314
  42.3 32.0 %copy-start.2 = (bf16[528,768]{1,0:T(8,128)(2,1)}, bf16[528,768]{1,0:T(8,128)(2,1)S(1)}, u32[]{:S(2)}) copy-start(bf16[528,768]{1,0:T(8,128)(2,1)S(1)} %collective-permute-done.3.refs_3_) | copy-start | bytes 2433028
  42.3 48.7 %collective-permute-start.7 = (bf16[528,768]{1,0:T(8,128)(2,1)}, bf16[528,768]{1,0:T(8,128)(2,1)}, u32[]{:S(2)}, u32[]{:S(2)}) collective-permute-start(bf16[528,768]{1,0:T(8,128)(2,1)} %get-tuple-element.30), channel_id=1, source_target_pairs={{0,22},{1,19},{2,16},{3,21},{4,18},{5,23},{6,20},{7,17},{8,62},{9,... | collective-permute-start | bytes 2433032 | tf_op jit(solution)/shard_map/ppermute | solution.py:314
  98.1 4.0 %collective-permute-start.8 = (bf16[512,896]{1,0:T(8,128)(2,1)}, bf16[512,896]{1,0:T(8,128)(2,1)S(1)}, u32[]{:S(2)}, u32[]{:S(2)}) collective-permute-start(bf16[512,896]{1,0:T(8,128)(2,1)} %get-tuple-element.34), channel_id=1, source_target_pairs={{0,8},{8,0},{1,9},{9,1},{2,10},{10,2},{3,11},{11,3},{4,12},{12,4},... | collective-permute-start | bytes 2752520 | tf_op jit(solution)/shard_map/ppermute | solution.py:334
  104.5 19.7 %all-to-all-start = ((bf16[8,64,896]{2,1,0:T(8,128)(2,1)}), bf16[8,64,896]{2,1,0:T(8,128)(2,1)S(1)}, u32[]{:S(2)}, u32[]{:S(2)}) async-start(bf16[8,64,896]{2,1,0:T(8,128)(2,1)} %bitcast.1), calls=%async_computation | async-start | bytes 1835008 | tf_op jit(solution)/shard_map/all_to_all | solution.py:338
  124.6 7.6 %collective-permute-start.9 = (bf16[64,896]{1,0:T(8,128)(2,1)S(1)}, bf16[64,896]{1,0:T(8,128)(2,1)S(1)}, u32[]{:S(2)}, u32[]{:S(2)}) collective-permute-start(bf16[64,896]{1,0:T(8,128)(2,1)S(1)} %pad_maximum_fusion), channel_id=1, source_target_pairs={{0,3},{1,6},{2,5},{3,0},{4,7},{5,2},{6,1},{7,4},{8,11},{9,14},{10,... | collective-permute-start | bytes 344072 | tf_op jit(solution)/shard_map/ppermute | solution.py:314
  149.6 5.2 %copy-start.3 = (bf16[8,64,768]{2,1,0:T(8,128)(2,1)}, bf16[8,64,768]{2,1,0:T(8,128)(2,1)S(1)}, u32[]{:S(2)}) copy-start(bf16[8,64,768]{2,1,0:T(8,128)(2,1)S(1)} %all_to_all.35) | copy-start | bytes 2359300
  149.6 5.2 %collective-permute-start.10 = (bf16[512,768]{1,0:T(8,128)(2,1)S(1)}, bf16[512,768]{1,0:T(8,128)(2,1)S(1)}, u32[]{:S(2)}, u32[]{:S(2)}) collective-permute-start(bf16[512,768]{1,0:T(8,128)(2,1)S(1)} %bitcast.8), channel_id=1, source_target_pairs={{0,8},{8,0},{1,9},{9,1},{2,10},{10,2},{3,11},{11,3},{4,12},{12,4},... | collective-permute-start | bytes 2359304 | tf_op jit(solution)/shard_map/ppermute | solution.py:334
  154.8 0.9 copy-start.4
  164.8 2.8 %collective-permute-start.11 = (bf16[512,896]{1,0:T(8,128)(2,1)}, bf16[512,896]{1,0:T(8,128)(2,1)S(1)}, u32[]{:S(2)}, u32[]{:S(2)}) collective-permute-start(bf16[512,896]{1,0:T(8,128)(2,1)} %get-tuple-element.38), channel_id=1, source_target_pairs={{0,8},{8,0},{1,9},{9,1},{2,10},{10,2},{3,11},{11,3},{4,12},{12,4},... | collective-permute-start | bytes 2752520 | tf_op jit(solution)/shard_map/ppermute | solution.py:334
  187.2 7.3 %collective-permute-start.12 = (bf16[64,896]{1,0:T(8,128)(2,1)S(1)}, bf16[64,896]{1,0:T(8,128)(2,1)S(1)}, u32[]{:S(2)}, u32[]{:S(2)}) collective-permute-start(bf16[64,896]{1,0:T(8,128)(2,1)S(1)} %pad_maximum_fusion.1), channel_id=1, source_target_pairs={{1,6},{3,0},{5,2},{7,4},{9,14},{11,8},{13,10},{15,12},{16,21},{18,... | collective-permute-start | bytes 344072 | tf_op jit(solution)/shard_map/ppermute | solution.py:314
  195.8 8.7 %collective-permute-start.13 = (bf16[64,768]{1,0:T(8,128)(2,1)S(1)}, bf16[64,768]{1,0:T(8,128)(2,1)S(1)}, u32[]{:S(2)}, u32[]{:S(2)}) collective-permute-start(bf16[64,768]{1,0:T(8,128)(2,1)S(1)} %fusion.3), channel_id=1, source_target_pairs={{0,16},{16,0},{1,17},{17,1},{2,18},{18,2},{3,19},{19,3},{4,20},{20... | collective-permute-start | bytes 294920 | tf_op jit(solution)/shard_map/ppermute | solution.py:401
  221.5 5.7 %collective-permute-start.14 = (bf16[512,768]{1,0:T(8,128)(2,1)S(1)}, bf16[512,768]{1,0:T(8,128)(2,1)S(1)}, u32[]{:S(2)}, u32[]{:S(2)}) collective-permute-start(bf16[512,768]{1,0:T(8,128)(2,1)S(1)} %bitcast.11), channel_id=1, source_target_pairs={{0,8},{8,0},{1,9},{9,1},{2,10},{10,2},{3,11},{11,3},{4,12},{12,4},... | collective-permute-start | bytes 2359304 | tf_op jit(solution)/shard_map/ppermute | solution.py:334
Sparse Core Ops, SparseCore 0:
  18.2 54.7 all-gather.1

commit v3 on v2

--- a/solution.py
+++ b/solution.py
@@ -43,7 +43,7 @@
 TAG_ROWS = 16
 CHUNK = 8
 GROUP_ROWS = CAP * ROWBLK
-VMEM_ASKED = 56 * 1024 * 1024
+VMEM_ASKED = 24 * 1024 * 1024
 
 
 def is_home(z, x):
@@ -130,7 +130,7 @@
             pltpu.SemaphoreType.DMA((3,)),
             pltpu.SemaphoreType.DMA((len(GROUPS),)),
         ],
-        compiler_params=pltpu.CompilerParams(vmem_limit_bytes=VMEM_ASKED),
+        compiler_params=pltpu.CompilerParams(vmem_limit_bytes=56 * 1024 * 1024),
         cost_estimate=pl.CostEstimate(
             flops=0, bytes_accessed=12 * 1024 * 1024, transcendentals=0
         ),

time: 237 us -> 229 us (0.966)
  Pallas kernels: 30.3 us -> 18.1 us
  waiting for transfers between devices: 81.1 us -> 84.5 us
  starting transfers between devices: 47.2 us -> 50.2 us
    pallas_call x3, Pallas kernels: 25.5 us -> 13.2 us  [partial_sums(): pl.pallas_call(functools.partial(sums_kernel, len(groups), bool(tags), st...]
    ppermute x9, waiting for transfers between devices: 28 us -> 32.5 us  [permute(): return lax.ppermute(value, AROUND, pairs)]
    convert_element_type x2, other arithmetic: 3.76 us -> 1.37 us  [reduced(): both.astype(jnp.bfloat16)]
  transfers between devices with their start and end apart: 17 -> 17, of which waited for: 12 -> 12; matrix products, arithmetic and copies ran while one was open for 1% -> 1% of each run, Pallas kernels for 6% -> 4%
where the time goes in v3:
time: 229 us; the launch traced here: 228 us
  waiting for transfers between devices  84.5 us (37%)
  starting transfers between devices  50.2 us (22%)
  blocking collectives  50 us (22%)
  Pallas kernels  18.1 us (8%)
  between operations  13.6 us (6%)
  other arithmetic  9.49 us (4%)
  local copies, waits for them, and re-layouts  2.46 us (1%)
    all_to_all x3, blocking collectives, exchange(): return lax.all_to_all(value, axes, split_axis=0, concat_axis=0, tiled=True)  50 us
    ppermute x9, waiting for transfers between devices, permute(): return lax.ppermute(value, AROUND, pairs)  32.5 us
    all_gather x1, waiting for transfers between devices, shards(): far = lax.all_gather(piece, ('y', 'xh', 'xl', 'c'), axis=0, tiled=True)  26.6 us
    ppermute x9, starting transfers between devices, permute(): return lax.ppermute(value, AROUND, pairs)  21.5 us
    all_to_all x1, waiting for transfers between devices, exchange(): return lax.all_to_all(value, axes, split_axis=0, concat_axis=0, tiled=True)  15.3 us
    pallas_call x3, Pallas kernels, partial_sums(): pl.pallas_call(functools.partial(sums_kernel, len(groups), bool(tags), st...  13.2 us
    ppermute x4, starting transfers between devices, swap_cores(): return lax.ppermute(value, 'c', [(0, 1), (1, 0)])  10.8 us
    ppermute x1, starting transfers between devices, shards(): way = jnp.where(home, way, lax.ppermute(way, 'xl', [(0, 1), (1, 0)]))  8.31 us
  transfers between devices with their start and end apart: 17, of which 12 were waited for; matrix products, arithmetic and copies ran while one was open for 1% of the time, Pallas kernels for 4%

profile of v3, /device:TPU:1, one launch (start us, length us, event | category | flops | bytes accessed | tf_op | source)
XLA Modules:
  0.0 228.3 jit_solution(3659308861597343525)
XLA Ops:
  6.5 0.0 all-gather.2.cloned.1.call-start
  6.5 0.8 constant_dynamic-slice_fusion
  7.3 5.2 %collective-permute-start.1 = (bf16[32,768]{1,0:T(8,128)(2,1)S(1)}, bf16[32,768]{1,0:T(8,128)(2,1)S(1)}, u32[]{:S(2)}, u32[]{:S(2)}) collective-permute-start(bf16[32,768]{1,0:T(8,128)(2,1)S(1)} %constant_dynamic-slice_fusion), channel_id=1, source_target_pairs={{0,3},{1,4},{2,5},{3,6},{4,7},{5,0},{6,1},{7,2},{8,11},{9,12},{10,... | collective-permute-start | bytes 147464 | tf_op jit(solution)/shard_map/ppermute | solution.py:372
  12.5 4.8 %shard_map.46 = (bf16[528,768]{1,0:T(8,128)(2,1)}, bf16[528,768]{1,0:T(8,128)(2,1)}, bf16[528,768]{1,0:T(8,128)(2,1)}, bf16[528,768]{1,0:T(8,128)(2,1)}, bf16[52...) custom-call(s32[16]{0:T(128)} %par_hbm.1, s32[16]{0:T(128)} %live_hbm.1, ...), custom_call_target="tpu_custom_call" | custom-call | bytes 12582912 | tf_op jit(solution)/shard_map/pallas_call | solution.py:116
  17.4 0.0 collective-permute-done.1
  17.4 0.6 copy-done.5
  18.0 0.0 all-gather.2.cloned.1.call-update
  18.0 2.6 %collective-permute-start = (bf16[528,768]{1,0:T(8,128)(2,1)}, bf16[528,768]{1,0:T(8,128)(2,1)S(1)}, u32[]{:S(2)}, u32[]{:S(2)}) collective-permute-start(bf16[528,768]{1,0:T(8,128)(2,1)} %get-tuple-element.23), channel_id=1, source_target_pairs={{0,16},{1,17},{2,18},{3,19},{4,20},{5,21},{6,22},{7,23},{8,56},{9,... | collective-permute-start | bytes 2433032 | tf_op jit(solution)/shard_map/ppermute | solution.py:314
  20.6 1.2 collective-permute-start.3
  21.8 1.9 collective-permute-start.4
  23.7 1.0 collective-permute-start.5
  24.7 0.4 collective-permute-start.2
  25.1 12.3 %collective-permute-done.refs_1_ = bf16[528,768]{1,0:T(8,128)(2,1)S(1)} collective-permute-done((bf16[528,768]{1,0:T(8,128)(2,1)}, bf16[528,768]{1,0:T(8,128)(2,1)S(1)}, u32[]{:S(2)}, u32[]{:S(2)}) %collective-permute-start) | collective-permute-done | bytes 811040 | tf_op jit(solution)/shard_map/ppermute | solution.py:314
  37.4 4.7 %collective-permute-start.6 = (bf16[528,768]{1,0:T(8,128)(2,1)}, bf16[528,768]{1,0:T(8,128)(2,1)}, u32[]{:S(2)}, u32[]{:S(2)}) collective-permute-start(bf16[528,768]{1,0:T(8,128)(2,1)} %get-tuple-element.29), channel_id=1, source_target_pairs={{0,2},{1,7},{2,4},{3,1},{4,6},{5,3},{6,0},{7,5},{8,10},{9,15},{10,... | collective-permute-start | bytes 2433032 | tf_op jit(solution)/shard_map/ppermute | solution.py:314
  42.1 0.1 collective-permute-done.3.refs_3_
  42.2 0.9 copy-done.1
  43.1 3.1 %collective-permute-start.7 = (bf16[528,768]{1,0:T(8,128)(2,1)}, bf16[528,768]{1,0:T(8,128)(2,1)}, u32[]{:S(2)}, u32[]{:S(2)}) collective-permute-start(bf16[528,768]{1,0:T(8,128)(2,1)} %get-tuple-element.30), channel_id=1, source_target_pairs={{0,22},{1,19},{2,16},{3,21},{4,18},{5,23},{6,20},{7,17},{8,62},{9,... | collective-permute-start | bytes 2433032 | tf_op jit(solution)/shard_map/ppermute | solution.py:314
  46.2 26.6 %all-gather.2.cloned.1.call-done = bf16[1024,768]{1,0:T(8,128)(2,1)} async-done(((bf16[32,768]{1,0:T(8,128)(2,1)}), bf16[1024,768]{1,0:T(8,128)(2,1)}) %all-gather.2.cloned.1.call-update) | async-done | bytes 1572880 | tf_op jit(solution)/shard_map/all_gather | solution.py:379
  72.8 1.6 broadcast_select_fusion.refs_6_.refs_2_
  74.5 0.0 collective-permute-done.4.refs_4_
  74.5 0.0 collective-permute-done.5.refs_5_
  74.5 0.0 collective-permute-done.2.refs_2_
  74.6 4.8 %shard_map.47 = (f32[1024,1024]{1,0:T(8,128)S(1)}, s32[2,24]{1,0:T(2,128)S(1)}) custom-call(bf16[528,768]{1,0:T(8,128)(2,1)S(1)} %copy-done, bf16[528,768]{1,0:T(8,128)(2,1)S(1)} %collective-permute-done.refs_1_, bf16[528,768]{1,0:T(8,128)(2,1)} %collective-permute-done.2.refs_2_, bf16[528,768]{1,0:T(8,128)(2,1)S(1)} %copy-done.2, ...), custom_call_target="tpu_custom_call" | custom-call | flops 603979776 | bytes 8126464 | tf_op jit(solution)/shard_map/pallas_call | solution.py:277
  79.4 0.0 collective-permute-done.6.refs_0_.refs_6_
  79.4 11.6 %collective-permute-done.7.refs_1_.refs_7_ = bf16[528,768]{1,0:T(8,128)(2,1)} collective-permute-done((bf16[528,768]{1,0:T(8,128)(2,1)}, bf16[528,768]{1,0:T(8,128)(2,1)}, u32[]{:S(2)}, u32[]{:S(2)}) %collective-permute-start.7) | collective-permute-done | bytes 811040 | tf_op jit(solution)/shard_map/ppermute | solution.py:314
  90.9 3.7 %shard_map.48 = (bf16[512,896]{1,0:T(8,128)(2,1)S(1)}, bf16[512,896]{1,0:T(8,128)(2,1)S(1)}, s32[2,8]{1,0:T(2,128)S(1)}) custom-call(bf16[528,768]{1,0:T(8,128)(2,1)} %collective-permute-done.6.refs_0_.refs_6_, bf16[528,768]{1,0:T(8,128)(2,1)} %collective-permute-done.7.refs_1_.refs_7_, bf16[1024,768]{1,0:T(8,128)(2,1)S(1)} %broadcast_select_fusion.refs_6_.refs_2_, ...), custom_call_target="tpu_custom_call" | custom-call | flops 201326592 | bytes 4980736 | tf_op jit(solution)/shard_map/pallas_call | solution.py:277
  94.7 1.7 collective-permute-start.8
  96.4 2.1 collective-permute-done.8
  98.5 1.1 add_convert_fusion.1
  99.6 4.4 %all-to-all-start = ((bf16[8,64,896]{2,1,0:T(8,128)(2,1)}), bf16[8,64,896]{2,1,0:T(8,128)(2,1)}, u32[]{:S(2)}, u32[]{:S(2)}) async-start(bf16[8,64,896]{2,1,0:T(8,128)(2,1)} %bitcast.9), calls=%async_computation | async-start | bytes 1835008 | tf_op jit(solution)/shard_map/all_to_all | solution.py:338
  104.1 15.3 %all-to-all-done = bf16[8,64,896]{2,1,0:T(8,128)(2,1)} async-done(((bf16[8,64,896]{2,1,0:T(8,128)(2,1)}), bf16[8,64,896]{2,1,0:T(8,128)(2,1)}, u32[]{:S(2)}, u32[]{:S(2)}) %all-to-all-start) | async-done | bytes 917536 | tf_op jit(solution)/shard_map/all_to_all | solution.py:338
  119.4 1.3 convert_reduce_fusion.1
  120.7 0.2 reduce-precision_reduce_fusion.1
  120.9 0.1 fusion.11
  121.0 0.7 pad_maximum_fusion
  121.7 5.2 %collective-permute-start.9 = (bf16[64,896]{1,0:T(8,128)(2,1)}, bf16[64,896]{1,0:T(8,128)(2,1)}, u32[]{:S(2)}, u32[]{:S(2)}) collective-permute-start(bf16[64,896]{1,0:T(8,128)(2,1)} %pad_maximum_fusion), channel_id=1, source_target_pairs={{0,3},{1,6},{2,5},{3,0},{4,7},{5,2},{6,1},{7,4},{8,11},{9,14},{10,... | collective-permute-start | bytes 344072 | tf_op jit(solution)/shard_map/ppermute | solution.py:314
  126.9 2.6 %collective-permute-done.9 = bf16[64,896]{1,0:T(8,128)(2,1)} collective-permute-done((bf16[64,896]{1,0:T(8,128)(2,1)}, bf16[64,896]{1,0:T(8,128)(2,1)}, u32[]{:S(2)}, u32[]{:S(2)}) %collective-permute-start.9) | collective-permute-done | bytes 114720 | tf_op jit(solution)/shard_map/ppermute | solution.py:314
  129.5 0.9 convert_element_type.55
  130.4 0.2 fusion.17
  130.6 0.1 fusion.2
  130.7 0.1 broadcast_in_dim.56
  130.8 16.1 %all_to_all.35 = bf16[8,64,768]{2,1,0:T(8,128)(2,1)S(1)} all-to-all(bf16[8,64,768]{2,1,0:T(8,128)(2,1)S(1)} %broadcast_in_dim.56), channel_id=1, replica_groups=mesh['y'=4,'xh'=2,'xl'=2,'c'=2,'z'=8] {'y','xh'}, dimensions={0} | all-to-all | bytes 1572864 | tf_op jit(solution)/shard_map/all_to_all | solution.py:338
  146.9 3.3 %collective-permute-start.10 = (bf16[512,768]{1,0:T(8,128)(2,1)S(1)}, bf16[512,768]{1,0:T(8,128)(2,1)S(1)}, u32[]{:S(2)}, u32[]{:S(2)}) collective-permute-start(bf16[512,768]{1,0:T(8,128)(2,1)S(1)} %bitcast.7), channel_id=1, source_target_pairs={{0,8},{8,0},{1,9},{9,1},{2,10},{10,2},{3,11},{11,3},{4,12},{12,4},... | collective-permute-start | bytes 2359304 | tf_op jit(solution)/shard_map/ppermute | solution.py:334
  150.2 1.9 collective-permute-done.10.refs_9_
  152.1 4.7 %shard_map.49 = (bf16[512,896]{1,0:T(8,128)(2,1)S(1)}, bf16[512,896]{1,0:T(8,128)(2,1)S(1)}) custom-call(bf16[528,768]{1,0:T(8,128)(2,1)S(1)} %copy-done, bf16[528,768]{1,0:T(8,128)(2,1)S(1)} %collective-permute-done.refs_1_, bf16[528,768]{1,0:T(8,128)(2,1)} %collective-permute-done.2.refs_2_, bf16[528,768]{1,0:T(8,128)(2,1)S(1)} %copy-done.3, ...), custom_call_target="tpu_custom_call" | custom-call | flops 805306368 | bytes 9699328 | tf_op jit(solution)/shard_map/pallas_call | solution.py:277
  156.8 2.3 collective-permute-start.11
  159.1 2.1 collective-permute-done.11
  161.2 0.2 add_convert_fusion
  161.4 18.1 %all_to_all.36 = bf16[8,64,896]{2,1,0:T(8,128)(2,1)S(1)} all-to-all(bf16[8,64,896]{2,1,0:T(8,128)(2,1)S(1)} %bitcast.10), channel_id=1, replica_groups=mesh['y'=4,'xh'=2,'xl'=2,'c'=2,'z'=8] {'y','xh'}, dimensions={0} | all-to-all | bytes 1835008 | tf_op jit(solution)/shard_map/all_to_all | solution.py:338
  179.5 0.1 convert_reduce_fusion
  179.7 0.2 reduce-precision_reduce_fusion
  179.9 0.1 fusion.12
  180.0 1.3 collective-permute-start.12
  181.3 6.0 %collective-permute-done.12 = bf16[64,896]{1,0:T(8,128)(2,1)S(1)} collective-permute-done((bf16[64,896]{1,0:T(8,128)(2,1)S(1)}, bf16[64,896]{1,0:T(8,128)(2,1)S(1)}, u32[]{:S(2)}, u32[]{:S(2)}) %collective-permute-start.12) | collective-permute-done | bytes 114720 | tf_op jit(solution)/shard_map/ppermute | solution.py:314
  187.3 0.2 fusion.22
  187.5 0.1 fusion.3
  187.6 8.3 %collective-permute-start.13 = (bf16[64,768]{1,0:T(8,128)(2,1)S(1)}, bf16[64,768]{1,0:T(8,128)(2,1)S(1)}, u32[]{:S(2)}, u32[]{:S(2)}) collective-permute-start(bf16[64,768]{1,0:T(8,128)(2,1)S(1)} %fusion.3), channel_id=1, source_target_pairs={{0,16},{16,0},{1,17},{17,1},{2,18},{18,2},{3,19},{19,3},{4,20},{20... | collective-permute-start | bytes 294920 | tf_op jit(solution)/shard_map/ppermute | solution.py:401
  195.9 2.0 collective-permute-done.13
  198.0 0.1 broadcast_in_dim.61
  198.1 15.8 %all_to_all.37 = bf16[16,32,768]{2,1,0:T(8,128)(2,1)S(1)} all-to-all(bf16[16,32,768]{2,1,0:T(8,128)(2,1)S(1)} %broadcast_in_dim.61), channel_id=1, replica_groups=mesh['y'=4,'xh'=2,'xl'=2,'c'=2,'z'=8] {'y','xh','xl'}, dimensions={0} | all-to-all | bytes 1572864 | tf_op jit(solution)/shard_map/all_to_all | solution.py:338
  213.8 3.5 %collective-permute-start.14 = (bf16[512,768]{1,0:T(8,128)(2,1)S(1)}, bf16[512,768]{1,0:T(8,128)(2,1)S(1)}, u32[]{:S(2)}, u32[]{:S(2)}) collective-permute-start(bf16[512,768]{1,0:T(8,128)(2,1)S(1)} %bitcast.12), channel_id=1, source_target_pairs={{0,8},{8,0},{1,9},{9,1},{2,10},{10,2},{3,11},{11,3},{4,12},{12,4},... | collective-permute-start | bytes 2359304 | tf_op jit(solution)/shard_map/ppermute | solution.py:334
  217.3 1.9 collective-permute-done.14
  219.2 0.2 broadcast_select_fusion.2
  219.4 2.1 convert_add_fusion
  (18 shorter events, 0.1 us)
Async XLA Ops:
  6.5 66.3 %all-gather.2.cloned.1.call-start = ((), (), s32[]{:S(2)}) async-start(), calls=%async_computation.4 | async-start | bytes 1622016 | tf_op jit(solution)/shard_map/all_gather | solution.py:379
  7.3 10.0 %collective-permute-start.1 = (bf16[32,768]{1,0:T(8,128)(2,1)S(1)}, bf16[32,768]{1,0:T(8,128)(2,1)S(1)}, u32[]{:S(2)}, u32[]{:S(2)}) collective-permute-start(bf16[32,768]{1,0:T(8,128)(2,1)S(1)} %constant_dynamic-slice_fusion), channel_id=1, source_target_pairs={{0,3},{1,4},{2,5},{3,6},{4,7},{5,0},{6,1},{7,2},{8,11},{9,12},{10,... | collective-permute-start | bytes 147464 | tf_op jit(solution)/shard_map/ppermute | solution.py:372
  17.4 0.6 copy-start.5
  18.0 19.4 %collective-permute-start = (bf16[528,768]{1,0:T(8,128)(2,1)}, bf16[528,768]{1,0:T(8,128)(2,1)S(1)}, u32[]{:S(2)}, u32[]{:S(2)}) collective-permute-start(bf16[528,768]{1,0:T(8,128)(2,1)} %get-tuple-element.23), channel_id=1, source_target_pairs={{0,16},{1,17},{2,18},{3,19},{4,20},{5,21},{6,22},{7,23},{8,56},{9,... | collective-permute-start | bytes 2433032 | tf_op jit(solution)/shard_map/ppermute | solution.py:314
  20.6 21.6 %collective-permute-start.3 = (bf16[528,768]{1,0:T(8,128)(2,1)}, bf16[528,768]{1,0:T(8,128)(2,1)S(1)}, u32[]{:S(2)}, u32[]{:S(2)}) collective-permute-start(bf16[528,768]{1,0:T(8,128)(2,1)} %get-tuple-element.26), channel_id=1, source_target_pairs={{0,7},{1,0},{2,1},{3,2},{4,3},{5,4},{6,5},{7,6},{8,15},{9,8},{10,9... | collective-permute-start | bytes 2433032 | tf_op jit(solution)/shard_map/ppermute | solution.py:314
  21.8 52.7 %collective-permute-start.4 = (bf16[528,768]{1,0:T(8,128)(2,1)}, bf16[528,768]{1,0:T(8,128)(2,1)}, u32[]{:S(2)}, u32[]{:S(2)}) collective-permute-start(bf16[528,768]{1,0:T(8,128)(2,1)} %get-tuple-element.27), channel_id=1, source_target_pairs={{0,17},{1,18},{2,19},{3,20},{4,21},{5,22},{6,23},{7,16},{8,57},{9,... | collective-permute-start | bytes 2433032 | tf_op jit(solution)/shard_map/ppermute | solution.py:314
  23.7 50.8 %collective-permute-start.5 = (bf16[528,768]{1,0:T(8,128)(2,1)}, bf16[528,768]{1,0:T(8,128)(2,1)}, u32[]{:S(2)}, u32[]{:S(2)}) collective-permute-start(bf16[528,768]{1,0:T(8,128)(2,1)} %get-tuple-element.28), channel_id=1, source_target_pairs={{0,23},{1,16},{2,17},{3,18},{4,19},{5,20},{6,21},{7,22},{8,63},{9,... | collective-permute-start | bytes 2433032 | tf_op jit(solution)/shard_map/ppermute | solution.py:314
  24.7 49.8 %collective-permute-start.2 = (bf16[528,768]{1,0:T(8,128)(2,1)}, bf16[528,768]{1,0:T(8,128)(2,1)}, u32[]{:S(2)}, u32[]{:S(2)}) collective-permute-start(bf16[528,768]{1,0:T(8,128)(2,1)} %get-tuple-element.25), channel_id=1, source_target_pairs={{0,1},{1,2},{2,3},{3,4},{4,5},{5,6},{6,7},{7,0},{8,9},{9,10},{10,1... | collective-permute-start | bytes 2433032 | tf_op jit(solution)/shard_map/ppermute | solution.py:314
  37.4 42.0 %collective-permute-start.6 = (bf16[528,768]{1,0:T(8,128)(2,1)}, bf16[528,768]{1,0:T(8,128)(2,1)}, u32[]{:S(2)}, u32[]{:S(2)}) collective-permute-start(bf16[528,768]{1,0:T(8,128)(2,1)} %get-tuple-element.29), channel_id=1, source_target_pairs={{0,2},{1,7},{2,4},{3,1},{4,6},{5,3},{6,0},{7,5},{8,10},{9,15},{10,... | collective-permute-start | bytes 2433032 | tf_op jit(solution)/shard_map/ppermute | solution.py:314
  42.2 0.9 copy-start.1
  43.1 47.8 %collective-permute-start.7 = (bf16[528,768]{1,0:T(8,128)(2,1)}, bf16[528,768]{1,0:T(8,128)(2,1)}, u32[]{:S(2)}, u32[]{:S(2)}) collective-permute-start(bf16[528,768]{1,0:T(8,128)(2,1)} %get-tuple-element.30), channel_id=1, source_target_pairs={{0,22},{1,19},{2,16},{3,21},{4,18},{5,23},{6,20},{7,17},{8,62},{9,... | collective-permute-start | bytes 2433032 | tf_op jit(solution)/shard_map/ppermute | solution.py:314
  46.2 28.3 %copy-start = (bf16[528,768]{1,0:T(8,128)(2,1)S(1)}, bf16[528,768]{1,0:T(8,128)(2,1)}, u32[]{:S(2)}) copy-start(bf16[528,768]{1,0:T(8,128)(2,1)} %get-tuple-element.22.refs_0_) | copy-start | bytes 2433028
  72.8 1.7 copy-start.2
  94.7 3.8 %collective-permute-start.8 = (bf16[512,896]{1,0:T(8,128)(2,1)S(1)}, bf16[512,896]{1,0:T(8,128)(2,1)S(1)}, u32[]{:S(2)}, u32[]{:S(2)}) collective-permute-start(bf16[512,896]{1,0:T(8,128)(2,1)S(1)} %get-tuple-element.34), channel_id=1, source_target_pairs={{0,8},{8,0},{1,9},{9,1},{2,10},{10,2},{3,11},{11,3},{4,12},{12,4},... | collective-permute-start | bytes 2752520 | tf_op jit(solution)/shard_map/ppermute | solution.py:334
  99.6 19.8 %all-to-all-start = ((bf16[8,64,896]{2,1,0:T(8,128)(2,1)}), bf16[8,64,896]{2,1,0:T(8,128)(2,1)}, u32[]{:S(2)}, u32[]{:S(2)}) async-start(bf16[8,64,896]{2,1,0:T(8,128)(2,1)} %bitcast.9), calls=%async_computation | async-start | bytes 1835008 | tf_op jit(solution)/shard_map/all_to_all | solution.py:338
  121.7 7.8 %collective-permute-start.9 = (bf16[64,896]{1,0:T(8,128)(2,1)}, bf16[64,896]{1,0:T(8,128)(2,1)}, u32[]{:S(2)}, u32[]{:S(2)}) collective-permute-start(bf16[64,896]{1,0:T(8,128)(2,1)} %pad_maximum_fusion), channel_id=1, source_target_pairs={{0,3},{1,6},{2,5},{3,0},{4,7},{5,2},{6,1},{7,4},{8,11},{9,14},{10,... | collective-permute-start | bytes 344072 | tf_op jit(solution)/shard_map/ppermute | solution.py:314
  126.9 25.2 %copy-start.3 = (bf16[528,768]{1,0:T(8,128)(2,1)S(1)}, bf16[528,768]{1,0:T(8,128)(2,1)}, u32[]{:S(2)}) copy-start(bf16[528,768]{1,0:T(8,128)(2,1)} %copy-done.1) | copy-start | bytes 2433028
  146.9 5.2 %collective-permute-start.10 = (bf16[512,768]{1,0:T(8,128)(2,1)S(1)}, bf16[512,768]{1,0:T(8,128)(2,1)S(1)}, u32[]{:S(2)}, u32[]{:S(2)}) collective-permute-start(bf16[512,768]{1,0:T(8,128)(2,1)S(1)} %bitcast.7), channel_id=1, source_target_pairs={{0,8},{8,0},{1,9},{9,1},{2,10},{10,2},{3,11},{11,3},{4,12},{12,4},... | collective-permute-start | bytes 2359304 | tf_op jit(solution)/shard_map/ppermute | solution.py:334
  156.8 4.4 %collective-permute-start.11 = (bf16[512,896]{1,0:T(8,128)(2,1)S(1)}, bf16[512,896]{1,0:T(8,128)(2,1)S(1)}, u32[]{:S(2)}, u32[]{:S(2)}) collective-permute-start(bf16[512,896]{1,0:T(8,128)(2,1)S(1)} %get-tuple-element.38), channel_id=1, source_target_pairs={{0,8},{8,0},{1,9},{9,1},{2,10},{10,2},{3,11},{11,3},{4,12},{12,4},... | collective-permute-start | bytes 2752520 | tf_op jit(solution)/shard_map/ppermute | solution.py:334
  180.0 7.3 %collective-permute-start.12 = (bf16[64,896]{1,0:T(8,128)(2,1)S(1)}, bf16[64,896]{1,0:T(8,128)(2,1)S(1)}, u32[]{:S(2)}, u32[]{:S(2)}) collective-permute-start(bf16[64,896]{1,0:T(8,128)(2,1)S(1)} %pad_maximum_fusion.1), channel_id=1, source_target_pairs={{1,6},{3,0},{5,2},{7,4},{9,14},{11,8},{13,10},{15,12},{16,21},{18,... | collective-permute-start | bytes 344072 | tf_op jit(solution)/shard_map/ppermute | solution.py:314
  187.6 10.3 %collective-permute-start.13 = (bf16[64,768]{1,0:T(8,128)(2,1)S(1)}, bf16[64,768]{1,0:T(8,128)(2,1)S(1)}, u32[]{:S(2)}, u32[]{:S(2)}) collective-permute-start(bf16[64,768]{1,0:T(8,128)(2,1)S(1)} %fusion.3), channel_id=1, source_target_pairs={{0,16},{16,0},{1,17},{17,1},{2,18},{18,2},{3,19},{19,3},{4,20},{20... | collective-permute-start | bytes 294920 | tf_op jit(solution)/shard_map/ppermute | solution.py:401
  213.8 5.6 %copy-start.4 = (bf16[1024,768]{1,0:T(8,128)(2,1)S(1)}, bf16[1024,768]{1,0:T(8,128)(2,1)}, u32[]{:S(2)}) copy-start(bf16[1024,768]{1,0:T(8,128)(2,1)} %param.5) | copy-start | bytes 4718596
  213.8 5.4 %collective-permute-start.14 = (bf16[512,768]{1,0:T(8,128)(2,1)S(1)}, bf16[512,768]{1,0:T(8,128)(2,1)S(1)}, u32[]{:S(2)}, u32[]{:S(2)}) collective-permute-start(bf16[512,768]{1,0:T(8,128)(2,1)S(1)} %bitcast.12), channel_id=1, source_target_pairs={{0,8},{8,0},{1,9},{9,1},{2,10},{10,2},{3,11},{11,3},{4,12},{12,4},... | collective-permute-start | bytes 2359304 | tf_op jit(solution)/shard_map/ppermute | solution.py:334
Sparse Core Ops, SparseCore 0:
  18.1 54.6 all-gather.1

commit v4 on v3

--- a/solution.py
+++ b/solution.py
@@ -179,7 +179,7 @@
 
     if not resumed:
         state[:, :WIDE] = jnp.zeros((ROWS_DEV, WIDE), jnp.float32)
-        lax.fori_loop(0, PAR_DEV, square, 0)
+        lax.fori_loop(0, PAR_DEV, square, 0, unroll=4)
 
     used = jnp.int32(0)
     for i in range(count):
@@ -255,7 +255,7 @@
         return carry
 
     if packed:
-        lax.fori_loop(0, PAR_DEV // 2, finish, 0)
+        lax.fori_loop(0, PAR_DEV // 2, finish, 0, unroll=2)
     else:
         state_write = pltpu.make_async_copy(state, state_out, state_sem)
         state_write.start()
@@ -344,7 +344,8 @@
 
 
 def mass_of(value):
-    return sum(value[:, D + 32 * part : D + 32 * part + 1] for part in range(4))
+    parts = [value[:, D + 32 * part : D + 32 * part + 1] for part in range(4)]
+    return sum(part.astype(jnp.float32) for part in parts)
 
 
 def reduced(keep, send):
@@ -355,9 +356,9 @@
     mass = mass_of(mine)
     high = lax.reduce_precision(mass, 8, 7)
     low = lax.reduce_precision(mass - high, 8, 7)
-    lane = lax.broadcasted_iota(jnp.int32, (PIECE, 128), 1) // 32
-    split = jnp.where(lane == 0, high, jnp.where(lane == 1, low, 0.0))
-    sent = jnp.concatenate([total, split], axis=1).astype(jnp.bfloat16)
+    column = lax.broadcasted_iota(jnp.int32, (PIECE, WIDE), 1)
+    split = jnp.where(column < D + 32, high, jnp.where(column < D + 64, low, 0.0))
+    sent = jnp.where(column < D, mine, split).astype(jnp.bfloat16)
     return mine[:, :D], total, mass, high + low, sent
 
 
@@ -384,8 +385,8 @@
     keep, send, late_tags = partial_sums(arrived[EARLY:], [table], state=state)
 
     _, total, _, mass, sent = reduced(keep, send)
-    got = swap_planes(sent).astype(jnp.float32)
-    total, mass = total + got[:, :D], mass + mass_of(got)
+    got = swap_planes(sent)
+    total, mass = total + got[:, :D].astype(jnp.float32), mass + mass_of(got)
     prior = lax.dynamic_slice_in_dim(table, first_row, PIECE, 0).astype(jnp.float32)
     updated = ((total + PRIOR * prior) / (mass + PRIOR)).astype(jnp.bfloat16)
     own = spread(updated, CHIPS, ("y", "xh"))
@@ -393,8 +394,8 @@
 
     keep, send = partial_sums(arrived, tables, tags=(early_tags, late_tags))
     total, _, mass, _, sent = reduced(keep, send)
-    got = to_home(sent).astype(jnp.float32)
-    total, mass = total + got[:, :D], mass + mass_of(got)
+    got = to_home(sent)
+    total, mass = total + got[:, :D].astype(jnp.float32), mass + mass_of(got)
     updated = (total + PRIOR * updated.astype(jnp.float32)) / (mass + PRIOR)
 
     way = (updated - prior).astype(jnp.bfloat16)

time: 229 us -> 229 us (level)
  starting transfers between devices: 50.2 us -> 47.6 us
  blocking collectives: 50 us -> 52.3 us
    all_to_all x3, blocking collectives: 50 us -> 52.3 us  [exchange(): return lax.all_to_all(value, axes, split_axis=0, concat_axis=0, tiled=True)]
where the time goes in v4:
time: 229 us; the launch traced here: 228 us
  waiting for transfers between devices  84.4 us (37%)
  blocking collectives  52.3 us (23%)
  starting transfers between devices  47.6 us (21%)
  Pallas kernels  18.2 us (8%)
  between operations  13.6 us (6%)
  other arithmetic  9.9 us (4%)
  local copies, waits for them, and re-layouts  2.45 us (1%)
    all_to_all x3, blocking collectives, exchange(): return lax.all_to_all(value, axes, split_axis=0, concat_axis=0, tiled=True)  52.3 us
    ppermute x9, waiting for transfers between devices, permute(): return lax.ppermute(value, AROUND, pairs)  32.4 us
    all_gather x1, waiting for transfers between devices, shards(): far = lax.all_gather(piece, ('y', 'xh', 'xl', 'c'), axis=0, tiled=True)  26.6 us
    ppermute x9, starting transfers between devices, permute(): return lax.ppermute(value, AROUND, pairs)  21.5 us
    all_to_all x1, waiting for transfers between devices, exchange(): return lax.all_to_all(value, axes, split_axis=0, concat_axis=0, tiled=True)  15.3 us
    pallas_call x3, Pallas kernels, partial_sums(): pl.pallas_call(functools.partial(sums_kernel, len(groups), bool(tags), st...  13.5 us
    ppermute x4, starting transfers between devices, swap_cores(): return lax.ppermute(value, 'c', [(0, 1), (1, 0)])  9.56 us
    ppermute x4, waiting for transfers between devices, swap_cores(): return lax.ppermute(value, 'c', [(0, 1), (1, 0)])  8.02 us
  transfers between devices with their start and end apart: 17, of which 12 were waited for; matrix products, arithmetic and copies ran while one was open for 1% of the time, Pallas kernels for 4%

profile of v4, /device:TPU:1, one launch (start us, length us, event | category | flops | bytes accessed | tf_op | source)
XLA Modules:
  0.0 228.5 jit_solution(6864180336260537720)
XLA Ops:
  6.5 0.8 constant_dynamic-slice_fusion
  7.3 5.2 %collective-permute-start.1 = (bf16[32,768]{1,0:T(8,128)(2,1)S(1)}, bf16[32,768]{1,0:T(8,128)(2,1)S(1)}, u32[]{:S(2)}, u32[]{:S(2)}) collective-permute-start(bf16[32,768]{1,0:T(8,128)(2,1)S(1)} %constant_dynamic-slice_fusion), channel_id=1, source_target_pairs={{0,3},{1,4},{2,5},{3,6},{4,7},{5,0},{6,1},{7,2},{8,11},{9,12},{10,... | collective-permute-start | bytes 147464 | tf_op jit(solution)/shard_map/ppermute | solution.py:373
  12.5 4.8 %shard_map.46 = (bf16[528,768]{1,0:T(8,128)(2,1)}, bf16[528,768]{1,0:T(8,128)(2,1)}, bf16[528,768]{1,0:T(8,128)(2,1)}, bf16[528,768]{1,0:T(8,128)(2,1)}, bf16[52...) custom-call(s32[16]{0:T(128)} %par_hbm.1, s32[16]{0:T(128)} %live_hbm.1, ...), custom_call_target="tpu_custom_call" | custom-call | bytes 12582912 | tf_op jit(solution)/shard_map/pallas_call | solution.py:116
  17.3 0.0 collective-permute-done.1
  17.3 0.6 copy-done.5
  17.9 0.0 all-gather.2.cloned.1.call-update
  18.0 2.6 %collective-permute-start = (bf16[528,768]{1,0:T(8,128)(2,1)}, bf16[528,768]{1,0:T(8,128)(2,1)S(1)}, u32[]{:S(2)}, u32[]{:S(2)}) collective-permute-start(bf16[528,768]{1,0:T(8,128)(2,1)} %get-tuple-element.23), channel_id=1, source_target_pairs={{0,16},{1,17},{2,18},{3,19},{4,20},{5,21},{6,22},{7,23},{8,56},{9,... | collective-permute-start | bytes 2433032 | tf_op jit(solution)/shard_map/ppermute | solution.py:314
  20.5 1.2 collective-permute-start.3
  21.7 1.9 collective-permute-start.4
  23.6 1.0 collective-permute-start.5
  24.7 0.4 collective-permute-start.2
  25.1 12.3 %collective-permute-done.refs_1_ = bf16[528,768]{1,0:T(8,128)(2,1)S(1)} collective-permute-done((bf16[528,768]{1,0:T(8,128)(2,1)}, bf16[528,768]{1,0:T(8,128)(2,1)S(1)}, u32[]{:S(2)}, u32[]{:S(2)}) %collective-permute-start) | collective-permute-done | bytes 811040 | tf_op jit(solution)/shard_map/ppermute | solution.py:314
  37.4 4.7 %collective-permute-start.6 = (bf16[528,768]{1,0:T(8,128)(2,1)}, bf16[528,768]{1,0:T(8,128)(2,1)}, u32[]{:S(2)}, u32[]{:S(2)}) collective-permute-start(bf16[528,768]{1,0:T(8,128)(2,1)} %get-tuple-element.29), channel_id=1, source_target_pairs={{0,2},{1,7},{2,4},{3,1},{4,6},{5,3},{6,0},{7,5},{8,10},{9,15},{10,... | collective-permute-start | bytes 2433032 | tf_op jit(solution)/shard_map/ppermute | solution.py:314
  42.1 0.1 collective-permute-done.3.refs_3_
  42.2 0.9 copy-done.1
  43.1 3.2 %collective-permute-start.7 = (bf16[528,768]{1,0:T(8,128)(2,1)}, bf16[528,768]{1,0:T(8,128)(2,1)}, u32[]{:S(2)}, u32[]{:S(2)}) collective-permute-start(bf16[528,768]{1,0:T(8,128)(2,1)} %get-tuple-element.30), channel_id=1, source_target_pairs={{0,22},{1,19},{2,16},{3,21},{4,18},{5,23},{6,20},{7,17},{8,62},{9,... | collective-permute-start | bytes 2433032 | tf_op jit(solution)/shard_map/ppermute | solution.py:314
  46.2 26.6 %all-gather.2.cloned.1.call-done = bf16[1024,768]{1,0:T(8,128)(2,1)} async-done(((bf16[32,768]{1,0:T(8,128)(2,1)}), bf16[1024,768]{1,0:T(8,128)(2,1)}) %all-gather.2.cloned.1.call-update) | async-done | bytes 1572880 | tf_op jit(solution)/shard_map/all_gather | solution.py:380
  72.9 1.6 broadcast_select_fusion.refs_6_.refs_2_
  74.5 0.0 collective-permute-done.4.refs_4_
  74.5 0.0 collective-permute-done.5.refs_5_
  74.5 0.0 collective-permute-done.2.refs_2_
  74.6 4.8 %shard_map.47 = (f32[1024,1024]{1,0:T(8,128)S(1)}, s32[2,24]{1,0:T(2,128)S(1)}) custom-call(bf16[528,768]{1,0:T(8,128)(2,1)S(1)} %copy-done, bf16[528,768]{1,0:T(8,128)(2,1)S(1)} %collective-permute-done.refs_1_, bf16[528,768]{1,0:T(8,128)(2,1)} %collective-permute-done.2.refs_2_, bf16[528,768]{1,0:T(8,128)(2,1)S(1)} %copy-done.2, ...), custom_call_target="tpu_custom_call" | custom-call | flops 603979776 | bytes 8126464 | tf_op jit(solution)/shard_map/pallas_call | solution.py:277
  79.3 0.0 collective-permute-done.6.refs_0_.refs_6_
  79.3 11.5 %collective-permute-done.7.refs_1_.refs_7_ = bf16[528,768]{1,0:T(8,128)(2,1)} collective-permute-done((bf16[528,768]{1,0:T(8,128)(2,1)}, bf16[528,768]{1,0:T(8,128)(2,1)}, u32[]{:S(2)}, u32[]{:S(2)}) %collective-permute-start.7) | collective-permute-done | bytes 811040 | tf_op jit(solution)/shard_map/ppermute | solution.py:314
  90.8 3.4 %shard_map.48 = (bf16[512,896]{1,0:T(8,128)(2,1)S(1)}, bf16[512,896]{1,0:T(8,128)(2,1)S(1)}, s32[2,8]{1,0:T(2,128)S(1)}) custom-call(bf16[528,768]{1,0:T(8,128)(2,1)} %collective-permute-done.6.refs_0_.refs_6_, bf16[528,768]{1,0:T(8,128)(2,1)} %collective-permute-done.7.refs_1_.refs_7_, bf16[1024,768]{1,0:T(8,128)(2,1)S(1)} %broadcast_select_fusion.refs_6_.refs_2_, ...), custom_call_target="tpu_custom_call" | custom-call | flops 201326592 | bytes 4980736 | tf_op jit(solution)/shard_map/pallas_call | solution.py:277
  94.2 1.8 collective-permute-start.8
  96.0 2.1 collective-permute-done.8
  98.1 1.1 add_convert_fusion.1
  99.2 4.4 %all-to-all-start = ((bf16[8,64,896]{2,1,0:T(8,128)(2,1)}), bf16[8,64,896]{2,1,0:T(8,128)(2,1)}, u32[]{:S(2)}, u32[]{:S(2)}) async-start(bf16[8,64,896]{2,1,0:T(8,128)(2,1)} %bitcast.9), calls=%async_computation | async-start | bytes 1835008 | tf_op jit(solution)/shard_map/all_to_all | solution.py:338
  103.7 15.3 %all-to-all-done = bf16[8,64,896]{2,1,0:T(8,128)(2,1)} async-done(((bf16[8,64,896]{2,1,0:T(8,128)(2,1)}), bf16[8,64,896]{2,1,0:T(8,128)(2,1)}, u32[]{:S(2)}, u32[]{:S(2)}) %all-to-all-start) | async-done | bytes 917536 | tf_op jit(solution)/shard_map/all_to_all | solution.py:338
  119.0 1.3 convert_reduce_fusion.1
  120.3 0.8 reduce-precision_reduce_fusion.1
  121.2 0.8 select_convert_fusion.1
  121.9 5.2 %collective-permute-start.9 = (bf16[64,896]{1,0:T(8,128)(2,1)}, bf16[64,896]{1,0:T(8,128)(2,1)S(1)}, u32[]{:S(2)}, u32[]{:S(2)}) collective-permute-start(bf16[64,896]{1,0:T(8,128)(2,1)} %select_convert_fusion.1), channel_id=1, source_target_pairs={{0,3},{1,6},{2,5},{3,0},{4,7},{5,2},{6,1},{7,4},{8,11},{9,14},{10,... | collective-permute-start | bytes 344072 | tf_op jit(solution)/shard_map/ppermute | solution.py:314
  127.1 2.5 %collective-permute-done.9 = bf16[64,896]{1,0:T(8,128)(2,1)S(1)} collective-permute-done((bf16[64,896]{1,0:T(8,128)(2,1)}, bf16[64,896]{1,0:T(8,128)(2,1)S(1)}, u32[]{:S(2)}, u32[]{:S(2)}) %collective-permute-start.9) | collective-permute-done | bytes 114720 | tf_op jit(solution)/shard_map/ppermute | solution.py:314
  129.6 0.9 fusion.11
  130.6 0.1 fusion.2
  130.7 0.1 broadcast_in_dim.56
  130.7 16.1 %all_to_all.35 = bf16[8,64,768]{2,1,0:T(8,128)(2,1)S(1)} all-to-all(bf16[8,64,768]{2,1,0:T(8,128)(2,1)S(1)} %broadcast_in_dim.56), channel_id=1, replica_groups=mesh['y'=4,'xh'=2,'xl'=2,'c'=2,'z'=8] {'y','xh'}, dimensions={0} | all-to-all | bytes 1572864 | tf_op jit(solution)/shard_map/all_to_all | solution.py:338
  146.8 3.3 %collective-permute-start.10 = (bf16[512,768]{1,0:T(8,128)(2,1)S(1)}, bf16[512,768]{1,0:T(8,128)(2,1)S(1)}, u32[]{:S(2)}, u32[]{:S(2)}) collective-permute-start(bf16[512,768]{1,0:T(8,128)(2,1)S(1)} %bitcast.7), channel_id=1, source_target_pairs={{0,8},{8,0},{1,9},{9,1},{2,10},{10,2},{3,11},{11,3},{4,12},{12,4},... | collective-permute-start | bytes 2359304 | tf_op jit(solution)/shard_map/ppermute | solution.py:334
  150.2 1.9 collective-permute-done.10.refs_9_
  152.1 0.0 copy-done.3
  152.1 5.3 %shard_map.49 = (bf16[512,896]{1,0:T(8,128)(2,1)S(1)}, bf16[512,896]{1,0:T(8,128)(2,1)S(1)}) custom-call(bf16[528,768]{1,0:T(8,128)(2,1)S(1)} %copy-done, bf16[528,768]{1,0:T(8,128)(2,1)S(1)} %collective-permute-done.refs_1_, bf16[528,768]{1,0:T(8,128)(2,1)} %collective-permute-done.2.refs_2_, bf16[528,768]{1,0:T(8,128)(2,1)S(1)} %copy-done.3, ...), custom_call_target="tpu_custom_call" | custom-call | flops 805306368 | bytes 9699328 | tf_op jit(solution)/shard_map/pallas_call | solution.py:277
  157.4 1.4 collective-permute-start.11
  158.7 2.1 collective-permute-done.11
  160.8 0.2 add_convert_fusion
  161.1 0.0 copy-start.7
  161.1 18.0 %all_to_all.36 = bf16[8,64,896]{2,1,0:T(8,128)(2,1)S(1)} all-to-all(bf16[8,64,896]{2,1,0:T(8,128)(2,1)S(1)} %bitcast.10), channel_id=1, replica_groups=mesh['y'=4,'xh'=2,'xl'=2,'c'=2,'z'=8] {'y','xh'}, dimensions={0} | all-to-all | bytes 1835008 | tf_op jit(solution)/shard_map/all_to_all | solution.py:338
  179.0 0.1 convert_reduce_fusion
  179.1 0.2 reduce-precision_reduce_fusion
  179.3 0.0 copy-done.7
  179.3 0.1 select_convert_fusion
  179.5 1.3 collective-permute-start.12
  180.8 6.0 %collective-permute-done.12 = bf16[64,896]{1,0:T(8,128)(2,1)S(1)} collective-permute-done((bf16[64,896]{1,0:T(8,128)(2,1)S(1)}, bf16[64,896]{1,0:T(8,128)(2,1)S(1)}, u32[]{:S(2)}, u32[]{:S(2)}) %collective-permute-start.12) | collective-permute-done | bytes 114720 | tf_op jit(solution)/shard_map/ppermute | solution.py:314
  186.8 0.2 add_reduce_fusion
  187.0 0.1 fusion.3
  187.1 7.0 %collective-permute-start.13 = (bf16[64,768]{1,0:T(8,128)(2,1)S(1)}, bf16[64,768]{1,0:T(8,128)(2,1)S(1)}, u32[]{:S(2)}, u32[]{:S(2)}) collective-permute-start(bf16[64,768]{1,0:T(8,128)(2,1)S(1)} %fusion.3), channel_id=1, source_target_pairs={{0,16},{16,0},{1,17},{17,1},{2,18},{18,2},{3,19},{19,3},{4,20},{20... | collective-permute-start | bytes 294920 | tf_op jit(solution)/shard_map/ppermute | solution.py:402
  194.0 2.0 collective-permute-done.13
  196.1 0.1 broadcast_in_dim.61
  196.2 18.2 %all_to_all.37 = bf16[16,32,768]{2,1,0:T(8,128)(2,1)S(1)} all-to-all(bf16[16,32,768]{2,1,0:T(8,128)(2,1)S(1)} %broadcast_in_dim.61), channel_id=1, replica_groups=mesh['y'=4,'xh'=2,'xl'=2,'c'=2,'z'=8] {'y','xh','xl'}, dimensions={0} | all-to-all | bytes 1572864 | tf_op jit(solution)/shard_map/all_to_all | solution.py:338
  214.4 3.1 %collective-permute-start.14 = (bf16[512,768]{1,0:T(8,128)(2,1)S(1)}, bf16[512,768]{1,0:T(8,128)(2,1)S(1)}, u32[]{:S(2)}, u32[]{:S(2)}) collective-permute-start(bf16[512,768]{1,0:T(8,128)(2,1)S(1)} %bitcast.12), channel_id=1, source_target_pairs={{0,8},{8,0},{1,9},{9,1},{2,10},{10,2},{3,11},{11,3},{4,12},{12,4},... | collective-permute-start | bytes 2359304 | tf_op jit(solution)/shard_map/ppermute | solution.py:334
  217.5 1.9 collective-permute-done.14
  219.4 0.2 broadcast_select_fusion.2
  219.6 2.1 convert_add_fusion
  (16 shorter events, 0.1 us)
Async XLA Ops:
  6.5 66.3 %all-gather.2.cloned.1.call-start = ((), (), s32[]{:S(2)}) async-start(), calls=%async_computation.4 | async-start | bytes 1622016 | tf_op jit(solution)/shard_map/all_gather | solution.py:380
  7.3 10.0 %collective-permute-start.1 = (bf16[32,768]{1,0:T(8,128)(2,1)S(1)}, bf16[32,768]{1,0:T(8,128)(2,1)S(1)}, u32[]{:S(2)}, u32[]{:S(2)}) collective-permute-start(bf16[32,768]{1,0:T(8,128)(2,1)S(1)} %constant_dynamic-slice_fusion), channel_id=1, source_target_pairs={{0,3},{1,4},{2,5},{3,6},{4,7},{5,0},{6,1},{7,2},{8,11},{9,12},{10,... | collective-permute-start | bytes 147464 | tf_op jit(solution)/shard_map/ppermute | solution.py:373
  17.3 0.6 copy-start.5
  18.0 19.4 %collective-permute-start = (bf16[528,768]{1,0:T(8,128)(2,1)}, bf16[528,768]{1,0:T(8,128)(2,1)S(1)}, u32[]{:S(2)}, u32[]{:S(2)}) collective-permute-start(bf16[528,768]{1,0:T(8,128)(2,1)} %get-tuple-element.23), channel_id=1, source_target_pairs={{0,16},{1,17},{2,18},{3,19},{4,20},{5,21},{6,22},{7,23},{8,56},{9,... | collective-permute-start | bytes 2433032 | tf_op jit(solution)/shard_map/ppermute | solution.py:314
  20.5 21.6 %collective-permute-start.3 = (bf16[528,768]{1,0:T(8,128)(2,1)}, bf16[528,768]{1,0:T(8,128)(2,1)S(1)}, u32[]{:S(2)}, u32[]{:S(2)}) collective-permute-start(bf16[528,768]{1,0:T(8,128)(2,1)} %get-tuple-element.26), channel_id=1, source_target_pairs={{0,7},{1,0},{2,1},{3,2},{4,3},{5,4},{6,5},{7,6},{8,15},{9,8},{10,9... | collective-permute-start | bytes 2433032 | tf_op jit(solution)/shard_map/ppermute | solution.py:314
  21.7 52.8 %collective-permute-start.4 = (bf16[528,768]{1,0:T(8,128)(2,1)}, bf16[528,768]{1,0:T(8,128)(2,1)}, u32[]{:S(2)}, u32[]{:S(2)}) collective-permute-start(bf16[528,768]{1,0:T(8,128)(2,1)} %get-tuple-element.27), channel_id=1, source_target_pairs={{0,17},{1,18},{2,19},{3,20},{4,21},{5,22},{6,23},{7,16},{8,57},{9,... | collective-permute-start | bytes 2433032 | tf_op jit(solution)/shard_map/ppermute | solution.py:314
  23.6 50.9 %collective-permute-start.5 = (bf16[528,768]{1,0:T(8,128)(2,1)}, bf16[528,768]{1,0:T(8,128)(2,1)}, u32[]{:S(2)}, u32[]{:S(2)}) collective-permute-start(bf16[528,768]{1,0:T(8,128)(2,1)} %get-tuple-element.28), channel_id=1, source_target_pairs={{0,23},{1,16},{2,17},{3,18},{4,19},{5,20},{6,21},{7,22},{8,63},{9,... | collective-permute-start | bytes 2433032 | tf_op jit(solution)/shard_map/ppermute | solution.py:314
  24.7 49.9 %collective-permute-start.2 = (bf16[528,768]{1,0:T(8,128)(2,1)}, bf16[528,768]{1,0:T(8,128)(2,1)}, u32[]{:S(2)}, u32[]{:S(2)}) collective-permute-start(bf16[528,768]{1,0:T(8,128)(2,1)} %get-tuple-element.25), channel_id=1, source_target_pairs={{0,1},{1,2},{2,3},{3,4},{4,5},{5,6},{6,7},{7,0},{8,9},{9,10},{10,1... | collective-permute-start | bytes 2433032 | tf_op jit(solution)/shard_map/ppermute | solution.py:314
  37.4 41.9 %collective-permute-start.6 = (bf16[528,768]{1,0:T(8,128)(2,1)}, bf16[528,768]{1,0:T(8,128)(2,1)}, u32[]{:S(2)}, u32[]{:S(2)}) collective-permute-start(bf16[528,768]{1,0:T(8,128)(2,1)} %get-tuple-element.29), channel_id=1, source_target_pairs={{0,2},{1,7},{2,4},{3,1},{4,6},{5,3},{6,0},{7,5},{8,10},{9,15},{10,... | collective-permute-start | bytes 2433032 | tf_op jit(solution)/shard_map/ppermute | solution.py:314
  42.1 0.9 copy-start.1
  43.1 47.8 %collective-permute-start.7 = (bf16[528,768]{1,0:T(8,128)(2,1)}, bf16[528,768]{1,0:T(8,128)(2,1)}, u32[]{:S(2)}, u32[]{:S(2)}) collective-permute-start(bf16[528,768]{1,0:T(8,128)(2,1)} %get-tuple-element.30), channel_id=1, source_target_pairs={{0,22},{1,19},{2,16},{3,21},{4,18},{5,23},{6,20},{7,17},{8,62},{9,... | collective-permute-start | bytes 2433032 | tf_op jit(solution)/shard_map/ppermute | solution.py:314
  46.2 28.3 %copy-start = (bf16[528,768]{1,0:T(8,128)(2,1)S(1)}, bf16[528,768]{1,0:T(8,128)(2,1)}, u32[]{:S(2)}) copy-start(bf16[528,768]{1,0:T(8,128)(2,1)} %get-tuple-element.22.refs_0_) | copy-start | bytes 2433028
  72.9 1.7 copy-start.2
  94.2 3.9 %collective-permute-start.8 = (bf16[512,896]{1,0:T(8,128)(2,1)S(1)}, bf16[512,896]{1,0:T(8,128)(2,1)S(1)}, u32[]{:S(2)}, u32[]{:S(2)}) collective-permute-start(bf16[512,896]{1,0:T(8,128)(2,1)S(1)} %get-tuple-element.34), channel_id=1, source_target_pairs={{0,8},{8,0},{1,9},{9,1},{2,10},{10,2},{3,11},{11,3},{4,12},{12,4},... | collective-permute-start | bytes 2752520 | tf_op jit(solution)/shard_map/ppermute | solution.py:334
  99.2 19.8 %all-to-all-start = ((bf16[8,64,896]{2,1,0:T(8,128)(2,1)}), bf16[8,64,896]{2,1,0:T(8,128)(2,1)}, u32[]{:S(2)}, u32[]{:S(2)}) async-start(bf16[8,64,896]{2,1,0:T(8,128)(2,1)} %bitcast.9), calls=%async_computation | async-start | bytes 1835008 | tf_op jit(solution)/shard_map/all_to_all | solution.py:338
  103.7 17.5 %copy-start.6 = (pred[896]{0:T(1024)(128)(4,1)}, pred[896]{0:T(1024)(128)(4,1)S(1)}, u32[]{:S(2)}) copy-start(pred[896]{0:T(1024)(128)(4,1)S(1)} %iota_compare_fusion.2) | copy-start | bytes 2692
  121.9 7.7 %collective-permute-start.9 = (bf16[64,896]{1,0:T(8,128)(2,1)}, bf16[64,896]{1,0:T(8,128)(2,1)S(1)}, u32[]{:S(2)}, u32[]{:S(2)}) collective-permute-start(bf16[64,896]{1,0:T(8,128)(2,1)} %select_convert_fusion.1), channel_id=1, source_target_pairs={{0,3},{1,6},{2,5},{3,0},{4,7},{5,2},{6,1},{7,4},{8,11},{9,14},{10,... | collective-permute-start | bytes 344072 | tf_op jit(solution)/shard_map/ppermute | solution.py:314
  127.1 25.0 %copy-start.3 = (bf16[528,768]{1,0:T(8,128)(2,1)S(1)}, bf16[528,768]{1,0:T(8,128)(2,1)}, u32[]{:S(2)}) copy-start(bf16[528,768]{1,0:T(8,128)(2,1)} %copy-done.1) | copy-start | bytes 2433028
  146.8 5.2 %collective-permute-start.10 = (bf16[512,768]{1,0:T(8,128)(2,1)S(1)}, bf16[512,768]{1,0:T(8,128)(2,1)S(1)}, u32[]{:S(2)}, u32[]{:S(2)}) collective-permute-start(bf16[512,768]{1,0:T(8,128)(2,1)S(1)} %bitcast.7), channel_id=1, source_target_pairs={{0,8},{8,0},{1,9},{9,1},{2,10},{10,2},{3,11},{11,3},{4,12},{12,4},... | collective-permute-start | bytes 2359304 | tf_op jit(solution)/shard_map/ppermute | solution.py:334
  157.4 3.5 %collective-permute-start.11 = (bf16[512,896]{1,0:T(8,128)(2,1)S(1)}, bf16[512,896]{1,0:T(8,128)(2,1)S(1)}, u32[]{:S(2)}, u32[]{:S(2)}) collective-permute-start(bf16[512,896]{1,0:T(8,128)(2,1)S(1)} %get-tuple-element.38), channel_id=1, source_target_pairs={{0,8},{8,0},{1,9},{9,1},{2,10},{10,2},{3,11},{11,3},{4,12},{12,4},... | collective-permute-start | bytes 2752520 | tf_op jit(solution)/shard_map/ppermute | solution.py:334
  161.1 18.3 %copy-start.7 = (pred[896]{0:T(1024)(128)(4,1)S(1)}, pred[896]{0:T(1024)(128)(4,1)}, u32[]{:S(2)}) copy-start(pred[896]{0:T(1024)(128)(4,1)} %copy-done.6) | copy-start | bytes 2692
  179.5 7.3 %collective-permute-start.12 = (bf16[64,896]{1,0:T(8,128)(2,1)S(1)}, bf16[64,896]{1,0:T(8,128)(2,1)S(1)}, u32[]{:S(2)}, u32[]{:S(2)}) collective-permute-start(bf16[64,896]{1,0:T(8,128)(2,1)S(1)} %select_convert_fusion), channel_id=1, source_target_pairs={{1,6},{3,0},{5,2},{7,4},{9,14},{11,8},{13,10},{15,12},{16,21},{18,... | collective-permute-start | bytes 344072 | tf_op jit(solution)/shard_map/ppermute | solution.py:314
  187.1 9.0 %collective-permute-start.13 = (bf16[64,768]{1,0:T(8,128)(2,1)S(1)}, bf16[64,768]{1,0:T(8,128)(2,1)S(1)}, u32[]{:S(2)}, u32[]{:S(2)}) collective-permute-start(bf16[64,768]{1,0:T(8,128)(2,1)S(1)} %fusion.3), channel_id=1, source_target_pairs={{0,16},{16,0},{1,17},{17,1},{2,18},{18,2},{3,19},{19,3},{4,20},{20... | collective-permute-start | bytes 294920 | tf_op jit(solution)/shard_map/ppermute | solution.py:402
  214.4 5.2 %copy-start.4 = (bf16[1024,768]{1,0:T(8,128)(2,1)S(1)}, bf16[1024,768]{1,0:T(8,128)(2,1)}, u32[]{:S(2)}) copy-start(bf16[1024,768]{1,0:T(8,128)(2,1)} %param.5) | copy-start | bytes 4718596
  214.4 5.0 %collective-permute-start.14 = (bf16[512,768]{1,0:T(8,128)(2,1)S(1)}, bf16[512,768]{1,0:T(8,128)(2,1)S(1)}, u32[]{:S(2)}, u32[]{:S(2)}) collective-permute-start(bf16[512,768]{1,0:T(8,128)(2,1)S(1)} %bitcast.12), channel_id=1, source_target_pairs={{0,8},{8,0},{1,9},{9,1},{2,10},{10,2},{3,11},{11,3},{4,12},{12,4},... | collective-permute-start | bytes 2359304 | tf_op jit(solution)/shard_map/ppermute | solution.py:334
Sparse Core Ops, SparseCore 0:
  18.1 54.7 all-gather.1

commit v5 on v3

--- a/solution.py
+++ b/solution.py
@@ -33,10 +33,10 @@
     (1, 0, 5),
     (0, 6, 1),
     (0, 4, 7),
+    (0, 2, 3),
+    (1, 2, 3),
     (1, 6, 1),
     (1, 4, 7),
-    (0, 2, 3),
-    (1, 2, 3),
 )
 MOVES = {0: 0, 5: 0, 1: 1, 6: 1, 4: -1, 7: -1, 2: 2, 3: -2}
 EARLY = 6

time: 229 us -> 228 us (level)
  starting transfers between devices: 50.2 us -> 42.9 us
  waiting for transfers between devices: 84.5 us -> 88 us
    ppermute x1, starting transfers between devices: 8.31 us -> 2.26 us  [shards(): way = jnp.where(home, way, lax.ppermute(way, 'xl', [(0, 1), (1, 0)]))]
    ppermute x9, waiting for transfers between devices: 32.5 us -> 36.9 us  [permute(): return lax.ppermute(value, AROUND, pairs)]
    ppermute x9, starting transfers between devices: 21.5 us -> 18.5 us  [permute(): return lax.ppermute(value, AROUND, pairs)]
  transfers between devices with their start and end apart: 17 -> 17, of which waited for: 12 -> 14; matrix products, arithmetic and copies ran while one was open for 1% -> 1% of each run, Pallas kernels for 4% -> 5%
where the time goes in v5:
time: 228 us; the launch traced here: 226 us
  waiting for transfers between devices  88 us (39%)
  blocking collectives  49.8 us (22%)
  starting transfers between devices  42.9 us (19%)
  Pallas kernels  19.8 us (9%)
  between operations  13.6 us (6%)
  other arithmetic  9.49 us (4%)
  local copies, waits for them, and re-layouts  2.46 us (1%)
    all_to_all x3, blocking collectives, exchange(): return lax.all_to_all(value, axes, split_axis=0, concat_axis=0, tiled=True)  49.8 us
    ppermute x9, waiting for transfers between devices, permute(): return lax.ppermute(value, AROUND, pairs)  36.9 us
    all_gather x1, waiting for transfers between devices, shards(): far = lax.all_gather(piece, ('y', 'xh', 'xl', 'c'), axis=0, tiled=True)  25.7 us
    ppermute x9, starting transfers between devices, permute(): return lax.ppermute(value, AROUND, pairs)  18.5 us
    all_to_all x1, waiting for transfers between devices, exchange(): return lax.all_to_all(value, axes, split_axis=0, concat_axis=0, tiled=True)  15.3 us
    pallas_call x3, Pallas kernels, partial_sums(): pl.pallas_call(functools.partial(sums_kernel, len(groups), bool(tags), st...  15 us
    ppermute x4, starting transfers between devices, swap_cores(): return lax.ppermute(value, 'c', [(0, 1), (1, 0)])  11.5 us
    ppermute x4, waiting for transfers between devices, swap_cores(): return lax.ppermute(value, 'c', [(0, 1), (1, 0)])  8.02 us
  transfers between devices with their start and end apart: 17, of which 14 were waited for; matrix products, arithmetic and copies ran while one was open for 1% of the time, Pallas kernels for 5%

profile of v5, /device:TPU:1, one launch (start us, length us, event | category | flops | bytes accessed | tf_op | source)
XLA Modules:
  0.0 226.1 jit_solution(8481701755192872904)
XLA Ops:
  6.5 0.8 constant_dynamic-slice_fusion
  7.3 5.2 %collective-permute-start.1 = (bf16[32,768]{1,0:T(8,128)(2,1)S(1)}, bf16[32,768]{1,0:T(8,128)(2,1)S(1)}, u32[]{:S(2)}, u32[]{:S(2)}) collective-permute-start(bf16[32,768]{1,0:T(8,128)(2,1)S(1)} %constant_dynamic-slice_fusion), channel_id=1, source_target_pairs={{0,3},{1,4},{2,5},{3,6},{4,7},{5,0},{6,1},{7,2},{8,11},{9,12},{10,... | collective-permute-start | bytes 147464 | tf_op jit(solution)/shard_map/ppermute | solution.py:372
  12.5 4.8 %shard_map.46 = (bf16[528,768]{1,0:T(8,128)(2,1)}, bf16[528,768]{1,0:T(8,128)(2,1)}, bf16[528,768]{1,0:T(8,128)(2,1)}, bf16[528,768]{1,0:T(8,128)(2,1)}, bf16[52...) custom-call(s32[16]{0:T(128)} %par_hbm.1, s32[16]{0:T(128)} %live_hbm.1, ...), custom_call_target="tpu_custom_call" | custom-call | bytes 12582912 | tf_op jit(solution)/shard_map/pallas_call | solution.py:116
  17.4 0.0 collective-permute-done.1
  17.4 0.0 copy-start.5
  17.4 0.6 copy-done.5
  18.0 0.0 all-gather.2.cloned.1.call-update
  18.0 2.6 %collective-permute-start = (bf16[528,768]{1,0:T(8,128)(2,1)}, bf16[528,768]{1,0:T(8,128)(2,1)S(1)}, u32[]{:S(2)}, u32[]{:S(2)}) collective-permute-start(bf16[528,768]{1,0:T(8,128)(2,1)} %get-tuple-element.23), channel_id=1, source_target_pairs={{0,16},{1,17},{2,18},{3,19},{4,20},{5,21},{6,22},{7,23},{8,56},{9,... | collective-permute-start | bytes 2433032 | tf_op jit(solution)/shard_map/ppermute | solution.py:314
  20.6 1.2 collective-permute-start.3
  21.8 2.8 %collective-permute-start.4 = (bf16[528,768]{1,0:T(8,128)(2,1)}, bf16[528,768]{1,0:T(8,128)(2,1)}, u32[]{:S(2)}, u32[]{:S(2)}) collective-permute-start(bf16[528,768]{1,0:T(8,128)(2,1)} %get-tuple-element.27), channel_id=1, source_target_pairs={{0,2},{1,7},{2,4},{3,1},{4,6},{5,3},{6,0},{7,5},{8,10},{9,15},{10,... | collective-permute-start | bytes 2433032 | tf_op jit(solution)/shard_map/ppermute | solution.py:314
  24.6 2.7 %collective-permute-start.5 = (bf16[528,768]{1,0:T(8,128)(2,1)}, bf16[528,768]{1,0:T(8,128)(2,1)}, u32[]{:S(2)}, u32[]{:S(2)}) collective-permute-start(bf16[528,768]{1,0:T(8,128)(2,1)} %get-tuple-element.28), channel_id=1, source_target_pairs={{0,22},{1,19},{2,16},{3,21},{4,18},{5,23},{6,20},{7,17},{8,62},{9,... | collective-permute-start | bytes 2433032 | tf_op jit(solution)/shard_map/ppermute | solution.py:314
  27.3 0.1 collective-permute-start.2
  27.4 2.7 %collective-permute-done.refs_1_ = bf16[528,768]{1,0:T(8,128)(2,1)S(1)} collective-permute-done((bf16[528,768]{1,0:T(8,128)(2,1)}, bf16[528,768]{1,0:T(8,128)(2,1)S(1)}, u32[]{:S(2)}, u32[]{:S(2)}) %collective-permute-start) | collective-permute-done | bytes 811040 | tf_op jit(solution)/shard_map/ppermute | solution.py:314
  30.1 6.5 %collective-permute-start.6 = (bf16[528,768]{1,0:T(8,128)(2,1)}, bf16[528,768]{1,0:T(8,128)(2,1)}, u32[]{:S(2)}, u32[]{:S(2)}) collective-permute-start(bf16[528,768]{1,0:T(8,128)(2,1)} %get-tuple-element.29), channel_id=1, source_target_pairs={{0,17},{1,18},{2,19},{3,20},{4,21},{5,22},{6,23},{7,16},{8,57},{9,... | collective-permute-start | bytes 2433032 | tf_op jit(solution)/shard_map/ppermute | solution.py:314
  36.6 5.6 %collective-permute-done.3.refs_3_ = bf16[528,768]{1,0:T(8,128)(2,1)S(1)} collective-permute-done((bf16[528,768]{1,0:T(8,128)(2,1)}, bf16[528,768]{1,0:T(8,128)(2,1)S(1)}, u32[]{:S(2)}, u32[]{:S(2)}) %collective-permute-start.3) | collective-permute-done | bytes 811040 | tf_op jit(solution)/shard_map/ppermute | solution.py:314
  42.2 0.9 copy-done.1
  43.1 0.0 collective-permute-start.7
  43.1 25.7 %all-gather.2.cloned.1.call-done = bf16[1024,768]{1,0:T(8,128)(2,1)} async-done(((bf16[32,768]{1,0:T(8,128)(2,1)}), bf16[1024,768]{1,0:T(8,128)(2,1)}) %all-gather.2.cloned.1.call-update) | async-done | bytes 1572880 | tf_op jit(solution)/shard_map/all_gather | solution.py:379
  68.9 1.6 broadcast_select_fusion.refs_6_.refs_2_
  70.5 0.0 collective-permute-done.4.refs_4_
  70.5 3.1 %collective-permute-done.5.refs_5_ = bf16[528,768]{1,0:T(8,128)(2,1)} collective-permute-done((bf16[528,768]{1,0:T(8,128)(2,1)}, bf16[528,768]{1,0:T(8,128)(2,1)}, u32[]{:S(2)}, u32[]{:S(2)}) %collective-permute-start.5) | collective-permute-done | bytes 811040 | tf_op jit(solution)/shard_map/ppermute | solution.py:314
  73.6 6.0 %collective-permute-done.2.refs_2_ = bf16[528,768]{1,0:T(8,128)(2,1)} collective-permute-done((bf16[528,768]{1,0:T(8,128)(2,1)}, bf16[528,768]{1,0:T(8,128)(2,1)}, u32[]{:S(2)}, u32[]{:S(2)}) %collective-permute-start.2) | collective-permute-done | bytes 811040 | tf_op jit(solution)/shard_map/ppermute | solution.py:314
  79.6 5.7 %shard_map.47 = (f32[1024,1024]{1,0:T(8,128)S(1)}, s32[2,24]{1,0:T(2,128)S(1)}) custom-call(bf16[528,768]{1,0:T(8,128)(2,1)S(1)} %copy-done, bf16[528,768]{1,0:T(8,128)(2,1)S(1)} %collective-permute-done.refs_1_, bf16[528,768]{1,0:T(8,128)(2,1)} %collective-permute-done.2.refs_2_, bf16[528,768]{1,0:T(8,128)(2,1)S(1)} %copy-done.2, ...), custom_call_target="tpu_custom_call" | custom-call | flops 603979776 | bytes 8126464 | tf_op jit(solution)/shard_map/pallas_call | solution.py:277
  85.3 9.1 %collective-permute-done.6.refs_0_.refs_6_ = bf16[528,768]{1,0:T(8,128)(2,1)} collective-permute-done((bf16[528,768]{1,0:T(8,128)(2,1)}, bf16[528,768]{1,0:T(8,128)(2,1)}, u32[]{:S(2)}, u32[]{:S(2)}) %collective-permute-start.6) | collective-permute-done | bytes 811040 | tf_op jit(solution)/shard_map/ppermute | solution.py:314
  94.4 0.0 collective-permute-done.7.refs_1_.refs_7_
  94.4 3.7 %shard_map.48 = (bf16[512,896]{1,0:T(8,128)(2,1)S(1)}, bf16[512,896]{1,0:T(8,128)(2,1)S(1)}, s32[2,8]{1,0:T(2,128)S(1)}) custom-call(bf16[528,768]{1,0:T(8,128)(2,1)} %collective-permute-done.6.refs_0_.refs_6_, bf16[528,768]{1,0:T(8,128)(2,1)} %collective-permute-done.7.refs_1_.refs_7_, bf16[1024,768]{1,0:T(8,128)(2,1)S(1)} %broadcast_select_fusion.refs_6_.refs_2_, ...), custom_call_target="tpu_custom_call" | custom-call | flops 201326592 | bytes 4980736 | tf_op jit(solution)/shard_map/pallas_call | solution.py:277
  98.1 3.4 %collective-permute-start.8 = (bf16[512,896]{1,0:T(8,128)(2,1)S(1)}, bf16[512,896]{1,0:T(8,128)(2,1)S(1)}, u32[]{:S(2)}, u32[]{:S(2)}) collective-permute-start(bf16[512,896]{1,0:T(8,128)(2,1)S(1)} %get-tuple-element.34), channel_id=1, source_target_pairs={{0,8},{8,0},{1,9},{9,1},{2,10},{10,2},{3,11},{11,3},{4,12},{12,4},... | collective-permute-start | bytes 2752520 | tf_op jit(solution)/shard_map/ppermute | solution.py:334
  101.6 2.1 collective-permute-done.8
  103.7 1.1 add_convert_fusion.1
  104.8 5.4 %all-to-all-start = ((bf16[8,64,896]{2,1,0:T(8,128)(2,1)}), bf16[8,64,896]{2,1,0:T(8,128)(2,1)}, u32[]{:S(2)}, u32[]{:S(2)}) async-start(bf16[8,64,896]{2,1,0:T(8,128)(2,1)} %bitcast.9), calls=%async_computation | async-start | bytes 1835008 | tf_op jit(solution)/shard_map/all_to_all | solution.py:338
  110.2 15.3 %all-to-all-done = bf16[8,64,896]{2,1,0:T(8,128)(2,1)} async-done(((bf16[8,64,896]{2,1,0:T(8,128)(2,1)}), bf16[8,64,896]{2,1,0:T(8,128)(2,1)}, u32[]{:S(2)}, u32[]{:S(2)}) %all-to-all-start) | async-done | bytes 917536 | tf_op jit(solution)/shard_map/all_to_all | solution.py:338
  125.6 1.3 convert_reduce_fusion.1
  126.9 0.2 reduce-precision_reduce_fusion.1
  127.1 0.1 fusion.11
  127.2 0.7 pad_maximum_fusion
  127.9 1.3 collective-permute-start.9
  129.2 4.4 %collective-permute-done.9 = bf16[64,896]{1,0:T(8,128)(2,1)} collective-permute-done((bf16[64,896]{1,0:T(8,128)(2,1)}, bf16[64,896]{1,0:T(8,128)(2,1)}, u32[]{:S(2)}, u32[]{:S(2)}) %collective-permute-start.9) | collective-permute-done | bytes 114720 | tf_op jit(solution)/shard_map/ppermute | solution.py:314
  133.6 0.9 convert_element_type.55
  134.5 0.2 fusion.17
  134.7 0.1 fusion.2
  134.8 0.1 broadcast_in_dim.56
  134.9 15.9 %all_to_all.35 = bf16[8,64,768]{2,1,0:T(8,128)(2,1)S(1)} all-to-all(bf16[8,64,768]{2,1,0:T(8,128)(2,1)S(1)} %broadcast_in_dim.56), channel_id=1, replica_groups=mesh['y'=4,'xh'=2,'xl'=2,'c'=2,'z'=8] {'y','xh'}, dimensions={0} | all-to-all | bytes 1572864 | tf_op jit(solution)/shard_map/all_to_all | solution.py:338
  150.8 3.3 %collective-permute-start.10 = (bf16[512,768]{1,0:T(8,128)(2,1)S(1)}, bf16[512,768]{1,0:T(8,128)(2,1)S(1)}, u32[]{:S(2)}, u32[]{:S(2)}) collective-permute-start(bf16[512,768]{1,0:T(8,128)(2,1)S(1)} %bitcast.7), channel_id=1, source_target_pairs={{0,8},{8,0},{1,9},{9,1},{2,10},{10,2},{3,11},{11,3},{4,12},{12,4},... | collective-permute-start | bytes 2359304 | tf_op jit(solution)/shard_map/ppermute | solution.py:334
  154.1 1.9 collective-permute-done.10.refs_9_
  156.0 5.6 %shard_map.49 = (bf16[512,896]{1,0:T(8,128)(2,1)S(1)}, bf16[512,896]{1,0:T(8,128)(2,1)S(1)}) custom-call(bf16[528,768]{1,0:T(8,128)(2,1)S(1)} %copy-done, bf16[528,768]{1,0:T(8,128)(2,1)S(1)} %collective-permute-done.refs_1_, bf16[528,768]{1,0:T(8,128)(2,1)} %collective-permute-done.2.refs_2_, bf16[528,768]{1,0:T(8,128)(2,1)S(1)} %copy-done.3, ...), custom_call_target="tpu_custom_call" | custom-call | flops 805306368 | bytes 9699328 | tf_op jit(solution)/shard_map/pallas_call | solution.py:277
  161.6 0.5 collective-permute-start.11
  162.1 2.1 collective-permute-done.11
  164.2 0.2 add_convert_fusion
  164.4 19.0 %all_to_all.36 = bf16[8,64,896]{2,1,0:T(8,128)(2,1)S(1)} all-to-all(bf16[8,64,896]{2,1,0:T(8,128)(2,1)S(1)} %bitcast.10), channel_id=1, replica_groups=mesh['y'=4,'xh'=2,'xl'=2,'c'=2,'z'=8] {'y','xh'}, dimensions={0} | all-to-all | bytes 1835008 | tf_op jit(solution)/shard_map/all_to_all | solution.py:338
  183.4 0.1 convert_reduce_fusion
  183.6 0.2 reduce-precision_reduce_fusion
  183.8 0.1 fusion.12
  183.9 1.3 collective-permute-start.12
  185.2 6.0 %collective-permute-done.12 = bf16[64,896]{1,0:T(8,128)(2,1)S(1)} collective-permute-done((bf16[64,896]{1,0:T(8,128)(2,1)S(1)}, bf16[64,896]{1,0:T(8,128)(2,1)S(1)}, u32[]{:S(2)}, u32[]{:S(2)}) %collective-permute-start.12) | collective-permute-done | bytes 114720 | tf_op jit(solution)/shard_map/ppermute | solution.py:314
  191.2 0.2 fusion.22
  191.4 0.1 fusion.3
  191.6 2.3 %collective-permute-start.13 = (bf16[64,768]{1,0:T(8,128)(2,1)S(1)}, bf16[64,768]{1,0:T(8,128)(2,1)S(1)}, u32[]{:S(2)}, u32[]{:S(2)}) collective-permute-start(bf16[64,768]{1,0:T(8,128)(2,1)S(1)} %fusion.3), channel_id=1, source_target_pairs={{0,16},{16,0},{1,17},{17,1},{2,18},{18,2},{3,19},{19,3},{4,20},{20... | collective-permute-start | bytes 294920 | tf_op jit(solution)/shard_map/ppermute | solution.py:401
  193.8 2.0 collective-permute-done.13
  195.9 0.1 broadcast_in_dim.61
  195.9 14.8 %all_to_all.37 = bf16[16,32,768]{2,1,0:T(8,128)(2,1)S(1)} all-to-all(bf16[16,32,768]{2,1,0:T(8,128)(2,1)S(1)} %broadcast_in_dim.61), channel_id=1, replica_groups=mesh['y'=4,'xh'=2,'xl'=2,'c'=2,'z'=8] {'y','xh','xl'}, dimensions={0} | all-to-all | bytes 1572864 | tf_op jit(solution)/shard_map/all_to_all | solution.py:338
  210.7 4.3 %collective-permute-start.14 = (bf16[512,768]{1,0:T(8,128)(2,1)S(1)}, bf16[512,768]{1,0:T(8,128)(2,1)S(1)}, u32[]{:S(2)}, u32[]{:S(2)}) collective-permute-start(bf16[512,768]{1,0:T(8,128)(2,1)S(1)} %bitcast.12), channel_id=1, source_target_pairs={{0,8},{8,0},{1,9},{9,1},{2,10},{10,2},{3,11},{11,3},{4,12},{12,4},... | collective-permute-start | bytes 2359304 | tf_op jit(solution)/shard_map/ppermute | solution.py:334
  215.1 1.9 collective-permute-done.14
  217.0 0.2 broadcast_select_fusion.2
  217.2 2.1 convert_add_fusion
  (18 shorter events, 0.1 us)
Async XLA Ops:
  6.5 62.3 %all-gather.2.cloned.1.call-start = ((), (), s32[]{:S(2)}) async-start(), calls=%async_computation.4 | async-start | bytes 1622016 | tf_op jit(solution)/shard_map/all_gather | solution.py:379
  7.3 10.0 %collective-permute-start.1 = (bf16[32,768]{1,0:T(8,128)(2,1)S(1)}, bf16[32,768]{1,0:T(8,128)(2,1)S(1)}, u32[]{:S(2)}, u32[]{:S(2)}) collective-permute-start(bf16[32,768]{1,0:T(8,128)(2,1)S(1)} %constant_dynamic-slice_fusion), channel_id=1, source_target_pairs={{0,3},{1,4},{2,5},{3,6},{4,7},{5,0},{6,1},{7,2},{8,11},{9,12},{10,... | collective-permute-start | bytes 147464 | tf_op jit(solution)/shard_map/ppermute | solution.py:372
  17.4 0.6 copy-start.5
  18.0 12.1 %collective-permute-start = (bf16[528,768]{1,0:T(8,128)(2,1)}, bf16[528,768]{1,0:T(8,128)(2,1)S(1)}, u32[]{:S(2)}, u32[]{:S(2)}) collective-permute-start(bf16[528,768]{1,0:T(8,128)(2,1)} %get-tuple-element.23), channel_id=1, source_target_pairs={{0,16},{1,17},{2,18},{3,19},{4,20},{5,21},{6,22},{7,23},{8,56},{9,... | collective-permute-start | bytes 2433032 | tf_op jit(solution)/shard_map/ppermute | solution.py:314
  20.6 21.6 %collective-permute-start.3 = (bf16[528,768]{1,0:T(8,128)(2,1)}, bf16[528,768]{1,0:T(8,128)(2,1)S(1)}, u32[]{:S(2)}, u32[]{:S(2)}) collective-permute-start(bf16[528,768]{1,0:T(8,128)(2,1)} %get-tuple-element.26), channel_id=1, source_target_pairs={{0,7},{1,0},{2,1},{3,2},{4,3},{5,4},{6,5},{7,6},{8,15},{9,8},{10,9... | collective-permute-start | bytes 2433032 | tf_op jit(solution)/shard_map/ppermute | solution.py:314
  21.8 48.7 %collective-permute-start.4 = (bf16[528,768]{1,0:T(8,128)(2,1)}, bf16[528,768]{1,0:T(8,128)(2,1)}, u32[]{:S(2)}, u32[]{:S(2)}) collective-permute-start(bf16[528,768]{1,0:T(8,128)(2,1)} %get-tuple-element.27), channel_id=1, source_target_pairs={{0,2},{1,7},{2,4},{3,1},{4,6},{5,3},{6,0},{7,5},{8,10},{9,15},{10,... | collective-permute-start | bytes 2433032 | tf_op jit(solution)/shard_map/ppermute | solution.py:314
  24.6 49.0 %collective-permute-start.5 = (bf16[528,768]{1,0:T(8,128)(2,1)}, bf16[528,768]{1,0:T(8,128)(2,1)}, u32[]{:S(2)}, u32[]{:S(2)}) collective-permute-start(bf16[528,768]{1,0:T(8,128)(2,1)} %get-tuple-element.28), channel_id=1, source_target_pairs={{0,22},{1,19},{2,16},{3,21},{4,18},{5,23},{6,20},{7,17},{8,62},{9,... | collective-permute-start | bytes 2433032 | tf_op jit(solution)/shard_map/ppermute | solution.py:314
  27.3 52.3 %collective-permute-start.2 = (bf16[528,768]{1,0:T(8,128)(2,1)}, bf16[528,768]{1,0:T(8,128)(2,1)}, u32[]{:S(2)}, u32[]{:S(2)}) collective-permute-start(bf16[528,768]{1,0:T(8,128)(2,1)} %get-tuple-element.25), channel_id=1, source_target_pairs={{0,1},{1,2},{2,3},{3,4},{4,5},{5,6},{6,7},{7,0},{8,9},{9,10},{10,1... | collective-permute-start | bytes 2433032 | tf_op jit(solution)/shard_map/ppermute | solution.py:314
  30.1 64.3 %collective-permute-start.6 = (bf16[528,768]{1,0:T(8,128)(2,1)}, bf16[528,768]{1,0:T(8,128)(2,1)}, u32[]{:S(2)}, u32[]{:S(2)}) collective-permute-start(bf16[528,768]{1,0:T(8,128)(2,1)} %get-tuple-element.29), channel_id=1, source_target_pairs={{0,17},{1,18},{2,19},{3,20},{4,21},{5,22},{6,23},{7,16},{8,57},{9,... | collective-permute-start | bytes 2433032 | tf_op jit(solution)/shard_map/ppermute | solution.py:314
  42.2 0.9 copy-start.1
  43.1 51.2 %collective-permute-start.7 = (bf16[528,768]{1,0:T(8,128)(2,1)}, bf16[528,768]{1,0:T(8,128)(2,1)}, u32[]{:S(2)}, u32[]{:S(2)}) collective-permute-start(bf16[528,768]{1,0:T(8,128)(2,1)} %get-tuple-element.30), channel_id=1, source_target_pairs={{0,23},{1,16},{2,17},{3,18},{4,19},{5,20},{6,21},{7,22},{8,63},{9,... | collective-permute-start | bytes 2433032 | tf_op jit(solution)/shard_map/ppermute | solution.py:314
  43.1 36.4 %copy-start = (bf16[528,768]{1,0:T(8,128)(2,1)S(1)}, bf16[528,768]{1,0:T(8,128)(2,1)}, u32[]{:S(2)}) copy-start(bf16[528,768]{1,0:T(8,128)(2,1)} %get-tuple-element.22.refs_0_) | copy-start | bytes 2433028
  68.9 10.7 %copy-start.2 = (bf16[528,768]{1,0:T(8,128)(2,1)S(1)}, bf16[528,768]{1,0:T(8,128)(2,1)}, u32[]{:S(2)}) copy-start(bf16[528,768]{1,0:T(8,128)(2,1)} %copy-done.1) | copy-start | bytes 2433028
  98.1 5.5 %collective-permute-start.8 = (bf16[512,896]{1,0:T(8,128)(2,1)S(1)}, bf16[512,896]{1,0:T(8,128)(2,1)S(1)}, u32[]{:S(2)}, u32[]{:S(2)}) collective-permute-start(bf16[512,896]{1,0:T(8,128)(2,1)S(1)} %get-tuple-element.34), channel_id=1, source_target_pairs={{0,8},{8,0},{1,9},{9,1},{2,10},{10,2},{3,11},{11,3},{4,12},{12,4},... | collective-permute-start | bytes 2752520 | tf_op jit(solution)/shard_map/ppermute | solution.py:334
  104.8 20.8 %all-to-all-start = ((bf16[8,64,896]{2,1,0:T(8,128)(2,1)}), bf16[8,64,896]{2,1,0:T(8,128)(2,1)}, u32[]{:S(2)}, u32[]{:S(2)}) async-start(bf16[8,64,896]{2,1,0:T(8,128)(2,1)} %bitcast.9), calls=%async_computation | async-start | bytes 1835008 | tf_op jit(solution)/shard_map/all_to_all | solution.py:338
  127.9 5.8 %collective-permute-start.9 = (bf16[64,896]{1,0:T(8,128)(2,1)}, bf16[64,896]{1,0:T(8,128)(2,1)}, u32[]{:S(2)}, u32[]{:S(2)}) collective-permute-start(bf16[64,896]{1,0:T(8,128)(2,1)} %pad_maximum_fusion), channel_id=1, source_target_pairs={{0,3},{1,6},{2,5},{3,0},{4,7},{5,2},{6,1},{7,4},{8,11},{9,14},{10,... | collective-permute-start | bytes 344072 | tf_op jit(solution)/shard_map/ppermute | solution.py:314
  129.2 26.8 %copy-start.3 = (bf16[528,768]{1,0:T(8,128)(2,1)S(1)}, bf16[528,768]{1,0:T(8,128)(2,1)}, u32[]{:S(2)}) copy-start(bf16[528,768]{1,0:T(8,128)(2,1)} %copy-done.1) | copy-start | bytes 2433028
  150.8 5.2 %collective-permute-start.10 = (bf16[512,768]{1,0:T(8,128)(2,1)S(1)}, bf16[512,768]{1,0:T(8,128)(2,1)S(1)}, u32[]{:S(2)}, u32[]{:S(2)}) collective-permute-start(bf16[512,768]{1,0:T(8,128)(2,1)S(1)} %bitcast.7), channel_id=1, source_target_pairs={{0,8},{8,0},{1,9},{9,1},{2,10},{10,2},{3,11},{11,3},{4,12},{12,4},... | collective-permute-start | bytes 2359304 | tf_op jit(solution)/shard_map/ppermute | solution.py:334
  161.6 2.6 %collective-permute-start.11 = (bf16[512,896]{1,0:T(8,128)(2,1)S(1)}, bf16[512,896]{1,0:T(8,128)(2,1)S(1)}, u32[]{:S(2)}, u32[]{:S(2)}) collective-permute-start(bf16[512,896]{1,0:T(8,128)(2,1)S(1)} %get-tuple-element.38), channel_id=1, source_target_pairs={{0,8},{8,0},{1,9},{9,1},{2,10},{10,2},{3,11},{11,3},{4,12},{12,4},... | collective-permute-start | bytes 2752520 | tf_op jit(solution)/shard_map/ppermute | solution.py:334
  183.9 7.3 %collective-permute-start.12 = (bf16[64,896]{1,0:T(8,128)(2,1)S(1)}, bf16[64,896]{1,0:T(8,128)(2,1)S(1)}, u32[]{:S(2)}, u32[]{:S(2)}) collective-permute-start(bf16[64,896]{1,0:T(8,128)(2,1)S(1)} %pad_maximum_fusion.1), channel_id=1, source_target_pairs={{1,6},{3,0},{5,2},{7,4},{9,14},{11,8},{13,10},{15,12},{16,21},{18,... | collective-permute-start | bytes 344072 | tf_op jit(solution)/shard_map/ppermute | solution.py:314
  191.6 4.3 %collective-permute-start.13 = (bf16[64,768]{1,0:T(8,128)(2,1)S(1)}, bf16[64,768]{1,0:T(8,128)(2,1)S(1)}, u32[]{:S(2)}, u32[]{:S(2)}) collective-permute-start(bf16[64,768]{1,0:T(8,128)(2,1)S(1)} %fusion.3), channel_id=1, source_target_pairs={{0,16},{16,0},{1,17},{17,1},{2,18},{18,2},{3,19},{19,3},{4,20},{20... | collective-permute-start | bytes 294920 | tf_op jit(solution)/shard_map/ppermute | solution.py:401
  210.7 6.4 %copy-start.4 = (bf16[1024,768]{1,0:T(8,128)(2,1)S(1)}, bf16[1024,768]{1,0:T(8,128)(2,1)}, u32[]{:S(2)}) copy-start(bf16[1024,768]{1,0:T(8,128)(2,1)} %param.5) | copy-start | bytes 4718596
  210.7 6.2 %collective-permute-start.14 = (bf16[512,768]{1,0:T(8,128)(2,1)S(1)}, bf16[512,768]{1,0:T(8,128)(2,1)S(1)}, u32[]{:S(2)}, u32[]{:S(2)}) collective-permute-start(bf16[512,768]{1,0:T(8,128)(2,1)S(1)} %bitcast.12), channel_id=1, source_target_pairs={{0,8},{8,0},{1,9},{9,1},{2,10},{10,2},{3,11},{11,3},{4,12},{12,4},... | collective-permute-start | bytes 2359304 | tf_op jit(solution)/shard_map/ppermute | solution.py:334
Sparse Core Ops, SparseCore 0:
  18.1 50.6 all-gather.1
